TPU v7x, 32 devices: a whole 2x2x4 slice. The times are simulated.
32 devices in a mesh: seq: 8 (over z, y), head: 4 (over x, core).
Axes of the slice: x: 2, y: 2, z: 4, core: 2. Of those that a mesh axis runs over, the one named last changes fastest.
Arguments:
- queries: bfloat16 [4096, 4096], P('seq', 'head'), may hold values from -6 to 6
- key_vectors: bfloat16 [4096, 4096], P('seq', 'head'), may hold values from -6 to 6
- value_vectors: bfloat16 [4096, 4096], P('seq', 'head'), may hold values from -6 to 6
- log_decay: float32 [4096, 32], P('seq', 'head'), may hold values from -0.78 to 0
- head_scale: float32 [32], P('head'), may hold values from 0.2 to 1.6
- send_rows: int32 [8, 2, 128], P('seq'), may hold values from 0 to 511, as said below
- take_rows: int32 [4096], P('seq'), may hold values from 0 to 767, as said below
- doc_lengths: int32 [8], replicated, may hold values from 1 to 1024, as said below
- cotangent: bfloat16 [4096, 4096], P('seq', 'head'), may hold values from -6 to 6
Outputs:
- normed: bfloat16 [4096, 4096], P('seq', 'head')
- grad_queries: bfloat16 [4096, 4096], P('seq', 'head')
- grad_keys: bfloat16 [4096, 4096], P('seq', 'head')
- grad_values: bfloat16 [4096, 4096], P('seq', 'head')
Inputs may be any that keep to these rules, and one draw needn't show every extreme that they name: For shard d, send_rows[d, 0] lists local rows handed to shard d - 1 and send_rows[d, 1] rows handed to shard d + 1; a slot is live only if shard d - 1 (resp. d + 1) takes it; live rows of one shard are distinct over both lists and never a row that take_rows of shard d names among its own; the first shard hands nothing left and the last nothing right. take_rows at a position of shard d indexes [128 rows from shard d - 1, the 512 own rows, 128 rows from shard d + 1]; the values of one shard are distinct and take exactly as many rows from a neighbour as that neighbour hands over; the numbers handed between two neighbours are equal both ways and in every draw some pair hands 128. `doc_lengths`: document lengths sum to 4096; some document other than the first starts at a multiple of 512.
All inputs are finite; a program needn't handle non-finite values.
Results may differ from a plain program's by a relative error of at most 0.0061.
Values may be sent and summed in bfloat16 or wider, within the bound.
No kernel may reach another device: no remote copies, remote signals or barrier semaphores. Data moves between devices by JAX's collectives and lax.ppermute only.
A program may use at most 64 MiB of HBM per device.

v0:
```python
import functools
import math

import jax
import jax.numpy as jnp
from jax import lax
from jax.experimental import pallas as pl
from jax.experimental.pallas import tpu as pltpu
from jax.sharding import PartitionSpec as P

EPSILON = 1e-05
LOG2E = math.log2(math.e)
MASKED = -1e30
MIB = 1024 * 1024
BF = jnp.bfloat16
F32 = jnp.float32
NT = (((1,), (1,)), ((), ()))
TN = (((0,), (0,)), ((), ()))
CHUNK = 256


def dot(a, b):
    return jnp.dot(a, b, preferred_element_type=F32)


def dot_nt(a, b):
    return lax.dot_general(a, b, NT, preferred_element_type=F32)


def dot_tn(a, b):
    return lax.dot_general(a, b, TN, preferred_element_type=F32)


def along_rows(row, lanes=128):
    return jnp.broadcast_to(row, (lanes, row.shape[1])).T


def iota(shape, dim):
    return lax.broadcasted_iota(jnp.int32, shape, dim)


def one_hot(hit):
    return jnp.where(hit, 1.0, 0.0).astype(BF)


def pieces(x):
    high = x.astype(BF)
    rest = x - high.astype(F32)
    middle = rest.astype(BF)
    return high, middle, (rest - middle.astype(F32)).astype(BF)


def chunks(features):
    return [slice(start, start + CHUNK) for start in range(0, features, CHUNK)]


def head_slices(features, heads):
    width = features // heads
    return [slice(h * width, (h + 1) * width) for h in range(heads)]


def local(kernel, name, us, out_shape, operands, scalars=0, scratch=(), spaces=None):
    vmem = pl.BlockSpec(memory_space=pltpu.VMEM)
    smem = pl.BlockSpec(memory_space=pltpu.SMEM)
    specs = [smem] * scalars + [vmem] * (len(operands) - scalars)
    if spaces is not None:
        specs = [pl.BlockSpec(memory_space=space) for space in spaces]
    return pl.pallas_call(
        kernel,
        in_specs=specs,
        out_specs=[vmem] * len(out_shape),
        out_shape=out_shape,
        scratch_shapes=list(scratch),
        compiler_params=pltpu.CompilerParams(vmem_limit_bytes=16 * MIB),
        cost_estimate=pl.CostEstimate(
            flops=int(us * 1.1e9), bytes_accessed=1_000_000, transcendentals=0
        ),
        name=name,
    )(*operands)


def sds(shape, dtype=BF):
    return jax.ShapeDtypeStruct(shape, dtype)


def pick_kernel(send_hbm, k_hbm, v_hbm, left_ref, right_ref, hot_ref, send_ref, k_ref, v_ref, sem):
    rows, features = k_ref.shape
    capacity = send_ref.shape[1]
    named_copy = pltpu.make_async_copy(send_hbm, send_ref, sem.at[0])
    named_copy.start()
    copies = []
    for source, target in ((k_hbm, k_ref), (v_hbm, v_ref)):
        for part in chunks(features):
            copy = pltpu.make_async_copy(
                source.at[:, part], target.at[:, part], sem.at[1 + len(copies)]
            )
            copy.start()
            copies.append(copy)
    named_copy.wait()
    lane = iota((capacity, 128), 1)
    for side in range(2):
        named = along_rows(send_ref[side : side + 1, :])
        for start in range(0, rows, 128):
            hot_ref[side * capacity : (side + 1) * capacity, start : start + 128] = one_hot(
                named == lane + start
            )
    parts = chunks(features)
    for index, target in enumerate((k_ref, v_ref)):
        for number, part in enumerate(parts):
            copies[index * len(parts) + number].wait()
            picked = dot(hot_ref[...], target[:, part]).astype(BF)
            left_ref[index, :, part] = picked[:capacity]
            right_ref[index, :, part] = picked[capacity:]


def pick(send, k, v):
    rows, features = k.shape
    capacity = send.shape[1]
    slots = sds((2, capacity, features))
    return local(
        pick_kernel,
        "pick",
        2,
        [slots, slots, sds((2 * capacity, rows))],
        [pltpu.with_memory_space_constraint(x, pltpu.HBM) for x in (send, k, v)],
        scratch=(
            pltpu.VMEM((2, capacity), jnp.int32),
            pltpu.VMEM((rows, features), BF),
            pltpu.VMEM((rows, features), BF),
            pltpu.SemaphoreType.DMA((1 + 2 * len(chunks(features)),)),
        ),
        spaces=(pl.ANY, pl.ANY, pl.ANY),
    )


def prep_kernel(
    docs_ref, first_ref, take_ref, log_ref, named_ref, q_ref, k_ref, v_ref,
    left_ref, right_ref, qo_ref, ko_ref, vo_ref, hot_ref,
    mask_ref, cols_ref, rows_ref, through_ref, state_ref, leave_ref, own_ref,
):
    rows, features = q_ref.shape
    heads = log_ref.shape[0]
    capacity = hot_ref.shape[1] // 2
    for part in chunks(features):
        picked = dot(named_ref[...], q_ref[:, part]).astype(BF)
        left_ref[0, :, part] = picked[:capacity]
        right_ref[0, :, part] = picked[capacity:]

    first = first_ref[0]
    position = first + iota((rows, 1), 0)
    position_row = first + iota((1, rows), 1)
    segment = jnp.zeros((rows, 1), jnp.int32)
    segment_row = jnp.zeros((1, rows), jnp.int32)
    segment_first = jnp.int32(0)
    segment_last = jnp.int32(0)
    opens_first = jnp.int32(0)
    opens = jnp.int32(0)
    start = jnp.int32(0)
    for n in range(docs_ref.shape[0]):
        segment += (position >= start).astype(jnp.int32)
        segment_row += (position_row >= start).astype(jnp.int32)
        segment_first += (first >= start).astype(jnp.int32)
        segment_last += (first + rows - 1 >= start).astype(jnp.int32)
        opens_first += (first == start).astype(jnp.int32)
        opens += ((start >= first) & (start < first + rows)).astype(jnp.int32)
        start += docs_ref[n]
    below = iota((rows, rows), 0) >= iota((rows, rows), 1)
    scale = -0.5 * math.log2(features // heads)
    mask_ref[...] = jnp.where((segment == segment_row) & below, scale, MASKED)
    triangle = one_hot(below)
    logs = jnp.concatenate([log_ref[...], jnp.zeros((128 - heads, rows), F32)], axis=0).T
    high, middle, low = pieces(logs)
    running = (dot(triangle, high) + (dot(triangle, middle) + dot(triangle, low))) * LOG2E
    rows_ref[...] = running.T[:heads]
    final = running[rows - 1 : rows, :]
    keep_f = segment == segment_last
    keep_e = (segment == segment_first) & (opens_first == 0)
    leaving = jnp.where(keep_f, jnp.exp2(final - running), 0.0)
    entering = jnp.where(keep_e, jnp.exp2(running + scale), 0.0)
    through = jnp.where(opens == 0, jnp.exp2(final), 0.0)
    cols_ref[0], cols_ref[1], cols_ref[2] = leaving, entering, running
    parts = [x.astype(F32) for x in pieces(through)]
    line = iota((16, 128), 0)
    for h in range(heads):
        high, middle, low = [jnp.broadcast_to(x[:, h : h + 1], (16, 128)) for x in parts]
        through_ref[h] = jnp.where(
            line == 0, high, jnp.where(line == 1, middle, jnp.where(line == 2, low, 0.0))
        ).astype(BF)

    lane = iota((rows, 128), 1)
    taken = along_rows(take_ref[...])
    for start_row in range(0, rows, 128):
        own_ref[:, start_row : start_row + 128] = one_hot(taken - capacity == lane + start_row)
    hot_ref[:, :capacity] = one_hot(taken == lane)
    hot_ref[:, capacity:] = one_hot(taken - (capacity + rows) == lane)
    leave_ref[...] = sum(dot_tn(hot_ref[...], piece) for piece in pieces(leaving))
    for part in chunks(features):
        for source, target in ((k_ref, ko_ref), (v_ref, vo_ref), (q_ref, qo_ref)):
            target[:, part] = dot(own_ref[...], source[:, part]).astype(BF)
    for h, part in enumerate(head_slices(features, heads)):
        kf = (ko_ref[:, part].astype(F32) * cols_ref[0, :, h : h + 1]).astype(BF)
        state_ref[h] = dot_tn(kf, vo_ref[:, part])


def prep(docs, first, take, log_decay, named, q, k, v):
    rows, features = q.shape
    heads = log_decay.shape[0]
    width = features // heads
    capacity = named.shape[0] // 2
    slots, own_rows = sds((1, capacity, features)), sds((rows, features))
    return local(
        prep_kernel,
        "prep",
        30,
        [
            slots, slots, own_rows, own_rows, own_rows,
            sds((rows, 2 * capacity)),
            sds((rows, rows), F32),
            sds((3, rows, 128), F32),
            sds((heads, rows), F32),
            sds((heads, 16, 128)),
            sds((heads, width, width), F32),
            sds((2 * capacity, 128), F32),
        ],
        (docs, first, take, log_decay, named, q, k, v),
        scalars=2,
        scratch=(pltpu.VMEM((rows, rows), BF),),
    )


def state_kernel(left_ref, right_ref, leave_ref, own_ref, through_ref, message_ref):
    heads, width = own_ref.shape[:2]
    for h, part in enumerate(head_slices(heads * width, heads)):
        k = jnp.concatenate([left_ref[0, :, part], right_ref[0, :, part]], axis=0)
        v = jnp.concatenate([left_ref[1, :, part], right_ref[1, :, part]], axis=0)
        kf = (k.astype(F32) * leave_ref[:, h : h + 1]).astype(BF)
        message_ref[h, :width, :] = (own_ref[h] + dot_tn(kf, v)).astype(BF)
        message_ref[h, width:, :] = through_ref[h]


def assemble(hot_ref, left_ref, right_ref, index, own_rows, target):
    for part in chunks(target.shape[1]):
        extra = jnp.concatenate([left_ref[index, :, part], right_ref[index, :, part]], axis=0)
        target[:, part] = own_rows[:, part] + dot(hot_ref[...], extra).astype(BF)


def assemble_kernel(hot_ref, left_ref, right_ref, ko_ref, vo_ref, _, k_ref, v_ref):
    assemble(hot_ref, left_ref, right_ref, 0, ko_ref, k_ref)
    assemble(hot_ref, left_ref, right_ref, 1, vo_ref, v_ref)


def decay(mask_ref, cols_ref, rows_ref, h, top, half, reach):
    column = cols_ref[2, top : top + half, h : h + 1]
    row = rows_ref[h : h + 1, :reach]
    return jnp.exp2((column - row) + mask_ref[top : top + half, :reach])


def inside_kernel(hot_ref, left_ref, right_ref, qo_ref, k_ref, v_ref, mask_ref, cols_ref, rows_ref, q_ref, p_ref, o_ref):
    rows, features = k_ref.shape
    assemble(hot_ref, left_ref, right_ref, 0, qo_ref, q_ref)
    heads, half = p_ref.shape[0], rows // 2
    for h, part in enumerate(head_slices(features, heads)):
        for i in range(2):
            top, reach = i * half, (i + 1) * half
            here = slice(top, top + half)
            scores = dot_nt(q_ref[here, part], k_ref[:reach, part])
            weight = decay(mask_ref, cols_ref, rows_ref, h, top, half, reach)
            p = (scores * weight).astype(BF)
            p_ref[h, here, :reach] = p
            o_ref[here, part] = dot(p, v_ref[:reach, part])


def joined(near_ref, far_ref, h, width):
    through = jnp.sum(near_ref[h, width:, :].astype(F32), axis=0, keepdims=True)
    near = near_ref[h, :width, :].astype(F32)
    return (near + through * far_ref[h, :width, :].astype(F32)).astype(BF)


def output_kernel(scale_ref, o_ref, q_ref, near_ref, far_ref, cols_ref, ct_ref, u_ref, h_ref, sums_ref):
    rows, features = q_ref.shape
    heads, width = h_ref.shape[:2]
    squares = jnp.zeros((rows, width), F32)
    cross = jnp.zeros((rows, width), F32)
    for h, part in enumerate(head_slices(features, heads)):
        carried_in = joined(near_ref, far_ref, h, width)
        h_ref[h] = carried_in
        outer = dot(q_ref[:, part], carried_in) * cols_ref[1, :, h : h + 1]
        u = (o_ref[:, part] + outer) * scale_ref[h]
        u_ref[:, part] = u
        squares += u * u
        cross += ct_ref[:, part].astype(F32) * u
    sums_ref[0:1, :] = jnp.sum(squares.T, axis=0, keepdims=True)
    sums_ref[1:2, :] = jnp.sum(cross.T, axis=0, keepdims=True)


def norm_kernel(total, scale_ref, u_ref, ct_ref, q_ref, cols_ref, through_ref, *refs):
    *sums, g_ref, message_ref, inverse_ref = refs
    rows, features = q_ref.shape
    heads = through_ref.shape[0]
    width = features // heads
    summed = sums[0][...]
    for more in sums[1:]:
        summed += more[...]
    inverse = lax.rsqrt(along_rows(summed[0:1, :], width) / total + EPSILON)
    mean = inverse * inverse * inverse * (along_rows(summed[1:2, :], width) / total)
    inverse_ref[...] = inverse
    for h, part in enumerate(head_slices(features, heads)):
        g = (inverse * ct_ref[:, part].astype(F32) - u_ref[:, part] * mean) * scale_ref[h]
        g = g.astype(BF)
        g_ref[:, part] = g
        qe = (q_ref[:, part].astype(F32) * cols_ref[1, :, h : h + 1]).astype(BF)
        message_ref[h, :width, :] = dot_tn(qe, g).astype(BF)
        message_ref[h, width:, :] = through_ref[h]


def normed_kernel(u_ref, inverse_ref, _, normed_ref):
    rows, features = u_ref.shape
    width = inverse_ref.shape[1]
    for part in head_slices(features, features // width):
        normed_ref[:, part] = (u_ref[:, part] * inverse_ref[...]).astype(BF)


def send_back(hot, source, left_ref, right_ref, index):
    capacity = left_ref.shape[1]
    for part in chunks(source.shape[1]):
        back = dot(hot, source[:, part]).astype(BF)
        left_ref[index, :, part] = back[:capacity]
        right_ref[index, :, part] = back[capacity:]


def slots_hot(take_ref, capacity):
    rows = take_ref.shape[1]
    taken = jnp.broadcast_to(take_ref[...], (capacity, rows))
    slot = iota((capacity, rows), 0)
    return jnp.concatenate(
        [one_hot(taken == slot), one_hot(taken - (capacity + rows) == slot)], axis=0
    )


def grad_q_kernel(take_ref, g_ref, k_ref, v_ref, h_ref, mask_ref, cols_ref, rows_ref, dq_ref, z_ref, left_ref, right_ref):
    rows, features = k_ref.shape
    heads, half = h_ref.shape[0], rows // 2
    for h, part in enumerate(head_slices(features, heads)):
        for i in range(2):
            top, reach = i * half, (i + 1) * half
            here = slice(top, top + half)
            g = g_ref[here, part]
            weight = decay(mask_ref, cols_ref, rows_ref, h, top, half, reach)
            z = (dot_nt(g, v_ref[:reach, part]) * weight).astype(BF)
            z_ref[h, here, :reach] = z
            outer = dot_nt(g, h_ref[h]) * cols_ref[1, here, h : h + 1]
            dq_ref[here, part] = (dot(z, k_ref[:reach, part]) + outer).astype(BF)
    send_back(slots_hot(take_ref, left_ref.shape[1]), dq_ref, left_ref, right_ref, 0)


def inner_kernel(z_ref, p_ref, q_ref, g_ref, dk_ref, dv_ref):
    rows, features = q_ref.shape
    heads, half = z_ref.shape[0], rows // 2
    for h, part in enumerate(head_slices(features, heads)):
        for square, source, target in ((z_ref, q_ref, dk_ref), (p_ref, g_ref, dv_ref)):
            for j in range(2):
                here = slice(j * half, (j + 1) * half)
                target[here, part] = dot_tn(square[h, j * half :, here], source[j * half :, part])


def grad_kv_kernel(take_ref, near_ref, far_ref, k_ref, v_ref, cols_ref, dki_ref, dvi_ref, dk_ref, dv_ref, left_ref, right_ref):
    rows, features = k_ref.shape
    heads = near_ref.shape[0]
    for h, part in enumerate(head_slices(features, heads)):
        state_grad = joined(near_ref, far_ref, h, features // heads)
        leaving = cols_ref[0, :, h : h + 1]
        dk_ref[:, part] = (dki_ref[:, part] + leaving * dot_nt(v_ref[:, part], state_grad)).astype(BF)
        dv_ref[:, part] = (dvi_ref[:, part] + leaving * dot(k_ref[:, part], state_grad)).astype(BF)
    hot = slots_hot(take_ref, left_ref.shape[1])
    send_back(hot, dk_ref, left_ref, right_ref, 0)
    send_back(hot, dv_ref, left_ref, right_ref, 1)


def own_kernel(capacity, count, take_ref, *refs):
    rows = refs[0].shape[0]
    taken = jnp.broadcast_to(take_ref[...], (rows, rows))
    hot = one_hot(taken - capacity == iota((rows, rows), 0))
    for source, target in zip(refs[:count], refs[-count:]):
        for part in chunks(source.shape[1]):
            target[:, part] = dot(hot, source[:, part]).astype(BF)


def finish_kernel(count, send_ref, left_ref, right_ref, *refs):
    rows = refs[0].shape[0]
    capacity = send_ref.shape[1]
    line = iota((rows, capacity), 0)
    hot = jnp.concatenate(
        [
            one_hot(jnp.broadcast_to(send_ref[side : side + 1, :], (rows, capacity)) == line)
            for side in range(2)
        ],
        axis=1,
    )
    for index, (source, target) in enumerate(zip(refs[:count], refs[count : 2 * count])):
        for part in chunks(source.shape[1]):
            back = jnp.concatenate([left_ref[index, :, part], right_ref[index, :, part]], axis=0)
            target[:, part] = source[:, part] + dot(hot, back).astype(BF)
    for order in refs[2 * count :]:
        order[...] = jnp.zeros_like(order)


def shifted(array, by):
    peers = lax.axis_size("seq")
    return lax.ppermute(array, "seq", [(i, i + by) for i in range(peers) if 0 <= i + by < peers])


def turned_by(array, by):
    peers = lax.axis_size("head")
    return lax.ppermute(array, "head", [(i, (i + by) % peers) for i in range(peers)])


def carried(message, direction):
    reach = lax.axis_size("seq") // 4
    if reach <= 2:
        return shifted(message, direction), shifted(message, 2 * direction)
    size = message.shape[2]
    own_state = message[:, :size].astype(F32)
    through = jnp.sum(message[:, size:, :1].astype(F32), axis=1, keepdims=True)

    def relay(_, state_here):
        return shifted((through * state_here + own_state).astype(BF), direction).astype(F32)

    incoming = lax.fori_loop(0, reach, relay, jnp.zeros_like(own_state)).astype(BF)
    near = jnp.concatenate([incoming, jnp.zeros_like(message[:, size:])], axis=1)
    return near, jnp.zeros_like(message)


def on_device(
    queries, key_vectors, value_vectors, log_decay, head_scale,
    send_rows, take_rows, doc_lengths, cotangent,
):
    rows, features = queries.shape
    heads = head_scale.shape[0]
    width = features // heads
    capacity = send_rows.shape[2]
    send = send_rows.reshape(2, capacity)
    take = take_rows.reshape(1, rows)
    first = (lax.axis_index("seq") * rows).astype(jnp.int32).reshape(1)
    total = features * lax.axis_size("head")
    full, full32 = sds((rows, features)), sds((rows, features), F32)
    squares = sds((heads, rows, rows))
    message_shape = sds((heads, width + 16, width))
    one_side, two_sides = sds((1, capacity, features)), sds((2, capacity, features))

    kv_left, kv_right, named = pick(send, key_vectors, value_vectors)
    kv_before, kv_after = shifted(kv_right, 1), shifted(kv_left, -1)
    (
        q_left, q_right, q_own, k_own, v_own, hot, mask, cols, turned, through, state_own, leave
    ) = prep(doc_lengths, first, take, log_decay.T, named, queries, key_vectors, value_vectors)
    q_before, q_after = shifted(q_right, 1), shifted(q_left, -1)
    (message,) = local(
        state_kernel, "state", 30, [message_shape], (kv_before, kv_after, leave, state_own, through)
    )
    near, far = carried(message, 1)
    k, v = local(
        assemble_kernel,
        "assemble",
        5,
        [full, full],
        (hot, kv_before, kv_after, k_own, v_own, message),
    )
    q, probs, o_inside = local(
        inside_kernel,
        "inside",
        30,
        [full, squares, full32],
        (hot, q_before, q_after, q_own, k, v, mask, cols, turned),
    )
    u, state_low, sums = local(
        output_kernel,
        "output",
        3,
        [full32, sds((heads, width, width)), sds((2, rows), F32)],
        (head_scale, o_inside, q, near, far, cols, cotangent),
        scalars=1,
    )
    others = [turned_by(sums, by) for by in range(1, lax.axis_size("head"))]
    g, grad_message, inverse = local(
        functools.partial(norm_kernel, total),
        "norm",
        4,
        [full, message_shape, sds((rows, width), F32)],
        (head_scale, u, cotangent, q, cols, through, sums, *others),
        scalars=1,
    )
    grad_near, grad_far = carried(grad_message, -1)
    dq, z, dq_left, dq_right = local(
        grad_q_kernel,
        "grad_q",
        30,
        [full, squares, one_side, one_side],
        (take, g, k, v, state_low, mask, cols, turned),
    )
    dq_before, dq_after = shifted(dq_right, 1), shifted(dq_left, -1)
    dk_inner, dv_inner = local(inner_kernel, "inner", 5, [full32, full32], (z, probs, q, g))
    dk, dv, dkv_left, dkv_right = local(
        grad_kv_kernel,
        "grad_kv",
        30,
        [full, full, two_sides, two_sides],
        (take, grad_near, grad_far, k, v, cols, dk_inner, dv_inner),
    )
    dkv_before, dkv_after = shifted(dkv_right, 1), shifted(dkv_left, -1)
    (normed,) = local(normed_kernel, "normed", 2, [full], (u, inverse, dk))
    (dq_own,) = local(
        functools.partial(own_kernel, capacity, 1), "own_q", 2, [full], (take, dq, dk)
    )
    grad_queries, order = local(
        functools.partial(finish_kernel, 1),
        "finish_q",
        2,
        [full, sds((16, 128))],
        (send, dq_before, dq_after, dq_own),
    )
    dk_own, dv_own = local(
        functools.partial(own_kernel, capacity, 2), "own_kv", 2, [full, full],
        (take, dk, dv, order),
    )
    grad_keys, grad_values = local(
        functools.partial(finish_kernel, 2),
        "finish_kv",
        2,
        [full, full],
        (send, dkv_before, dkv_after, dk_own, dv_own),
    )
    return normed, grad_queries, grad_keys, grad_values


def solution(mesh):
    both = P("seq", "head")
    in_specs = (both, both, both, both, P("head"), P("seq", None, None), P("seq"), P(), both)
    return jax.shard_map(
        on_device, mesh=mesh, in_specs=in_specs, out_specs=(both,) * 4, check_vma=False
    )
```

profile of v0, /device:TPU:0, one launch (start us, length us, event | category | flops | bytes accessed | tf_op | source)
XLA Modules:
  0.0 115.3 jit_solution(14260575370155374291)
XLA Ops:
  0.7 4.4 %pick.1 = (bf16[2,128,1024]{2,1,0:T(8,128)(2,1)}, bf16[2,128,1024]{2,1,0:T(8,128)(2,1)}, bf16[256,512]{1,0:T(8,128)(2,1)S(1)}) custom-call(s32[2,128]{1,0:T(2,128)} %bitcast.10, bf16[512,1024]{1,0:T(8,128)(2,1)} %k_ref.1, bf16[512,1024]{1,0:T(8,128)(2,1)} %v_ref.1), custom_call_target="tpu_custom_call" | custom-call | flops 2200000000 | bytes 1000000 | tf_op jit(solution)/shard_map/pick/pallas_call | solution.py:68
  5.1 5.7 %collective-permute-start.2 = (bf16[2,128,1024]{2,1,0:T(8,128)(2,1)}, bf16[2,128,1024]{2,1,0:T(8,128)(2,1)}, u32[]{:S(2)}, u32[]{:S(2)}) collective-permute-start(bf16[2,128,1024]{2,1,0:T(8,128)(2,1)} %get-tuple-element.51), channel_id=1, source_target_pairs={{0,4},{4,8},{8,12},{12,16},{16,20},{20,24},{24,28},{1,5},{5,9},{9,... | collective-permute-start | bytes 1572872 | tf_op jit(solution)/shard_map/ppermute | solution.py:409
  10.8 1.3 %collective-permute-start.3 = (bf16[2,128,1024]{2,1,0:T(8,128)(2,1)}, bf16[2,128,1024]{2,1,0:T(8,128)(2,1)}, u32[]{:S(2)}, u32[]{:S(2)}) collective-permute-start(bf16[2,128,1024]{2,1,0:T(8,128)(2,1)} %get-tuple-element.52), channel_id=1, source_target_pairs={{4,0},{8,4},{12,8},{16,12},{20,16},{24,20},{28,24},{5,1},{9,5},{13... | collective-permute-start | bytes 1572872 | tf_op jit(solution)/shard_map/ppermute | solution.py:409
  12.1 4.9 %prep.1 = (bf16[1,128,1024]{2,1,0:T(8,128)(2,1)S(1)}, bf16[1,128,1024]{2,1,0:T(8,128)(2,1)S(1)}, bf16[512,1024]{1,0:T(8,128)(2,1)S(1)}, bf16[512,1024]{1,0:T(8,1...) custom-call(s32[8]{0:T(128)S(1)} %copy-done.7, ...), custom_call_target="tpu_custom_call" | custom-call | flops 32999999488 | bytes 1000000 | tf_op jit(solution)/shard_map/prep/pallas_call | solution.py:68
  17.0 4.6 %collective-permute-start = (bf16[1,128,1024]{2,1,0:T(8,128)(2,1)S(1)}, bf16[1,128,1024]{2,1,0:T(8,128)(2,1)S(1)}, u32[]{:S(2)}, u32[]{:S(2)}) collective-permute-start(bf16[1,128,1024]{2,1,0:T(8,128)(2,1)S(1)} %get-tuple-element.48), channel_id=1, source_target_pairs={{0,4},{4,8},{8,12},{12,16},{16,20},{20,24},{24,28},{1,5},{5,9},{9,... | collective-permute-start | bytes 786440 | tf_op jit(solution)/shard_map/ppermute | solution.py:409
  21.6 1.3 %collective-permute-start.1 = (bf16[1,128,1024]{2,1,0:T(8,128)(2,1)S(1)}, bf16[1,128,1024]{2,1,0:T(8,128)(2,1)S(1)}, u32[]{:S(2)}, u32[]{:S(2)}) collective-permute-start(bf16[1,128,1024]{2,1,0:T(8,128)(2,1)S(1)} %get-tuple-element.49), channel_id=1, source_target_pairs={{4,0},{8,4},{12,8},{16,12},{20,16},{24,20},{28,24},{5,1},{9,5},{13... | collective-permute-start | bytes 786440 | tf_op jit(solution)/shard_map/ppermute | solution.py:409
  22.9 16.6 %collective-permute-done.2.left_ref = bf16[2,128,1024]{2,1,0:T(8,128)(2,1)} collective-permute-done((bf16[2,128,1024]{2,1,0:T(8,128)(2,1)}, bf16[2,128,1024]{2,1,0:T(8,128)(2,1)}, u32[]{:S(2)}, u32[]{:S(2)}) %collective-permute-start.2) | collective-permute-done | bytes 524320 | tf_op jit(solution)/shard_map/ppermute | solution.py:409
  39.5 2.1 %state.1._ = bf16[8,144,128]{2,1,0:T(8,128)(2,1)S(1)} custom-call(bf16[2,128,1024]{2,1,0:T(8,128)(2,1)} %collective-permute-done.2.left_ref, bf16[2,128,1024]{2,1,0:T(8,128)(2,1)} %collective-permute-done.3.right_ref, f32[256,128]{1,0:T(8,128)S(1)} %get-tuple-element.55.leave_ref, f32[8,128,128]{2,1,0:T(8,128)S(1)} %get-tuple-element.56.own_ref, ...), custom_call_target="tpu_custom_call" | custom-call | flops 32999999488 | bytes 1000000 | tf_op jit(solution)/shard_map/state/pallas_call | solution.py:68
  41.6 4.4 %collective-permute-start.4 = (bf16[8,144,128]{2,1,0:T(8,128)(2,1)S(1)}, bf16[8,144,128]{2,1,0:T(8,128)(2,1)S(1)}, u32[]{:S(2)}, u32[]{:S(2)}) collective-permute-start(bf16[8,144,128]{2,1,0:T(8,128)(2,1)S(1)} %state.1._), channel_id=1, source_target_pairs={{0,4},{4,8},{8,12},{12,16},{16,20},{20,24},{24,28},{1,5},{5,9},{9,... | collective-permute-start | bytes 884744 | tf_op jit(solution)/shard_map/ppermute | solution.py:409
  46.0 3.5 %collective-permute-start.5 = (bf16[8,144,128]{2,1,0:T(8,128)(2,1)S(1)}, bf16[8,144,128]{2,1,0:T(8,128)(2,1)S(1)}, u32[]{:S(2)}, u32[]{:S(2)}) collective-permute-start(bf16[8,144,128]{2,1,0:T(8,128)(2,1)S(1)} %state.1._), channel_id=1, source_target_pairs={{0,8},{4,12},{8,16},{12,20},{16,24},{20,28},{1,9},{5,13},{9,17},{1... | collective-permute-start | bytes 884744 | tf_op jit(solution)/shard_map/ppermute | solution.py:409
  49.5 1.9 %assemble.1 = (bf16[512,1024]{1,0:T(8,128)(2,1)S(1)}, bf16[512,1024]{1,0:T(8,128)(2,1)S(1)}) custom-call(bf16[512,256]{1,0:T(8,128)(2,1)S(1)} %get-tuple-element.47.hot_ref, bf16[2,128,1024]{2,1,0:T(8,128)(2,1)} %collective-permute-done.2.left_ref, bf16[2,128,1024]{2,1,0:T(8,128)(2,1)} %collective-permute-done.3.right_ref, ...), custom_call_target="tpu_custom_call" | custom-call | flops 5500000256 | bytes 1000000 | tf_op jit(solution)/shard_map/assemble/pallas_call | solution.py:68
  51.5 2.7 %inside.1 = (bf16[512,1024]{1,0:T(8,128)(2,1)S(1)}, bf16[8,512,512]{2,1,0:T(8,128)(2,1)S(1)}, f32[512,1024]{1,0:T(8,128)S(1)}) custom-call(bf16[512,256]{1,0:T(8,128)(2,1)S(1)} %get-tuple-element.47.hot_ref, bf16[1,128,1024]{2,1,0:T(8,128)(2,1)S(1)} %collective-permute-done.left_ref, bf16[1,128,1024]{2,1,0:T(8,128)(2,1)S(1)} %collective-permute-done.1.right_ref, ...), custom_call_target="tpu_custom_call" | custom-call | flops 32999999488 | bytes 1000000 | tf_op jit(solution)/shard_map/inside/pallas_call | solution.py:68
  54.2 1.7 %output.1 = (f32[512,1024]{1,0:T(8,128)S(1)}, bf16[8,128,128]{2,1,0:T(8,128)(2,1)S(1)}, f32[2,512]{1,0:T(2,128)S(1)}) custom-call(f32[8]{0:T(128)S(1)} %copy-done.8, f32[512,1024]{1,0:T(8,128)S(1)} %get-tuple-element.63.o_ref, bf16[512,1024]{1,0:T(8,128)(2,1)S(1)} %get-tuple-element.64.q_ref, bf16[8,144,128]{2,1,0:T(8,128)(2,1)S(1)} %collective-permute-done.4.near_ref, ...), custom_call_target="tpu_custom_call" | custom-call | flops 3300000000 | bytes 1000000 | tf_op jit(solution)/shard_map/output/pallas_call | solution.py:68
  55.9 1.6 %collective-permute-start.7 = (f32[2,512]{1,0:T(2,128)S(1)}, f32[2,512]{1,0:T(2,128)S(1)}, u32[]{:S(2)}, u32[]{:S(2)}) collective-permute-start(f32[2,512]{1,0:T(2,128)S(1)} %get-tuple-element.66.refs_0_), channel_id=1, source_target_pairs={{0,2},{1,3},{2,0},{3,1},{4,6},{5,7},{6,4},{7,5},{8,10},{9,11},{10,... | collective-permute-start | bytes 12296 | tf_op jit(solution)/shard_map/ppermute | solution.py:414
  57.5 1.4 %collective-permute-start.8 = (f32[2,512]{1,0:T(2,128)S(1)}, f32[2,512]{1,0:T(2,128)S(1)}, u32[]{:S(2)}, u32[]{:S(2)}) collective-permute-start(f32[2,512]{1,0:T(2,128)S(1)} %get-tuple-element.66.refs_0_), channel_id=1, source_target_pairs={{0,3},{1,0},{2,1},{3,2},{4,7},{5,4},{6,5},{7,6},{8,11},{9,8},{10,9... | collective-permute-start | bytes 12296 | tf_op jit(solution)/shard_map/ppermute | solution.py:414
  60.2 2.2 %norm.1 = (bf16[512,1024]{1,0:T(8,128)(2,1)S(1)}, bf16[8,144,128]{2,1,0:T(8,128)(2,1)S(1)}, f32[512,128]{1,0:T(8,128)S(1)}) custom-call(f32[8]{0:T(128)S(1)} %copy-done.8, f32[512,1024]{1,0:T(8,128)S(1)} %get-tuple-element.65.u_ref, bf16[512,1024]{1,0:T(8,128)(2,1)S(1)} %copy-done.3, bf16[512,1024]{1,0:T(8,128)(2,1)S(1)} %get-tuple-element.64.q_ref, ...), custom_call_target="tpu_custom_call" | custom-call | flops 4400000000 | bytes 1000000 | tf_op jit(solution)/shard_map/norm/pallas_call | solution.py:68
  62.4 1.3 %collective-permute-start.10 = (bf16[8,144,128]{2,1,0:T(8,128)(2,1)S(1)}, bf16[8,144,128]{2,1,0:T(8,128)(2,1)S(1)}, u32[]{:S(2)}, u32[]{:S(2)}) collective-permute-start(bf16[8,144,128]{2,1,0:T(8,128)(2,1)S(1)} %get-tuple-element.68), channel_id=1, source_target_pairs={{8,0},{12,4},{16,8},{20,12},{24,16},{28,20},{9,1},{13,5},{17,9},{2... | collective-permute-start | bytes 884744 | tf_op jit(solution)/shard_map/ppermute | solution.py:409
  63.7 1.3 %collective-permute-start.9 = (bf16[8,144,128]{2,1,0:T(8,128)(2,1)S(1)}, bf16[8,144,128]{2,1,0:T(8,128)(2,1)S(1)}, u32[]{:S(2)}, u32[]{:S(2)}) collective-permute-start(bf16[8,144,128]{2,1,0:T(8,128)(2,1)S(1)} %get-tuple-element.68), channel_id=1, source_target_pairs={{4,0},{8,4},{12,8},{16,12},{20,16},{24,20},{28,24},{5,1},{9,5},{13... | collective-permute-start | bytes 884744 | tf_op jit(solution)/shard_map/ppermute | solution.py:409
  65.0 3.1 %grad_q.1 = (bf16[512,1024]{1,0:T(8,128)(2,1)S(1)}, bf16[8,512,512]{2,1,0:T(8,128)(2,1)S(1)}, bf16[1,128,1024]{2,1,0:T(8,128)(2,1)S(1)}, bf16[1,128,1024]{2,1,0:T(8,128)(2,1)S(1)}) custom-call(s32[1,512]{1,0:T(1,128)S(1)} %bitcast.6, bf16[512,1024]{1,0:T(8,128)(2,1)S(1)} %get-tuple-element.69.g_ref, bf16[512,1024]{1,0:T(8,128)(2,1)S(1)} %get-tuple-element.58.k_ref, ...), custom_call_target="tpu_custom_call" | custom-call | flops 32999999488 | bytes 1000000 | tf_op jit(solution)/shard_map/grad_q/pallas_call | solution.py:68
  68.0 8.4 %collective-permute-start.11 = (bf16[1,128,1024]{2,1,0:T(8,128)(2,1)S(1)}, bf16[1,128,1024]{2,1,0:T(8,128)(2,1)S(1)}, u32[]{:S(2)}, u32[]{:S(2)}) collective-permute-start(bf16[1,128,1024]{2,1,0:T(8,128)(2,1)S(1)} %get-tuple-element.76), channel_id=1, source_target_pairs={{0,4},{4,8},{8,12},{12,16},{16,20},{20,24},{24,28},{1,5},{5,9},{9,... | collective-permute-start | bytes 786440 | tf_op jit(solution)/shard_map/ppermute | solution.py:409
  76.4 1.3 %collective-permute-start.12 = (bf16[1,128,1024]{2,1,0:T(8,128)(2,1)S(1)}, bf16[1,128,1024]{2,1,0:T(8,128)(2,1)S(1)}, u32[]{:S(2)}, u32[]{:S(2)}) collective-permute-start(bf16[1,128,1024]{2,1,0:T(8,128)(2,1)S(1)} %get-tuple-element.77), channel_id=1, source_target_pairs={{4,0},{8,4},{12,8},{16,12},{20,16},{24,20},{28,24},{5,1},{9,5},{13... | collective-permute-start | bytes 786440 | tf_op jit(solution)/shard_map/ppermute | solution.py:409
  77.7 1.9 %inner.1 = (f32[512,1024]{1,0:T(8,128)S(1)}, f32[512,1024]{1,0:T(8,128)S(1)}) custom-call(bf16[8,512,512]{2,1,0:T(8,128)(2,1)S(1)} %get-tuple-element.71.z_ref, bf16[8,512,512]{2,1,0:T(8,128)(2,1)S(1)} %get-tuple-element.72.p_ref, bf16[512,1024]{1,0:T(8,128)(2,1)S(1)} %get-tuple-element.64.q_ref, bf16[512,1024]{1,0:T(8,128)(2,1)S(1)} %get-tuple-element.69.g_ref), custom_call_target="tpu_custom_call" | custom-call | flops 5500000256 | bytes 1000000 | tf_op jit(solution)/shard_map/inner/pallas_call | solution.py:68
  79.6 1.8 %grad_kv.1 = (bf16[512,1024]{1,0:T(8,128)(2,1)S(1)}, bf16[512,1024]{1,0:T(8,128)(2,1)S(1)}, bf16[2,128,1024]{2,1,0:T(8,128)(2,1)S(1)}, bf16[2,128,1024]{2,1,0:T(8,128)(2,1)S(1)}) custom-call(s32[1,512]{1,0:T(1,128)S(1)} %bitcast.7, bf16[8,144,128]{2,1,0:T(8,128)(2,1)S(1)} %collective-permute-done.9.near_ref, ...), custom_call_target="tpu_custom_call" | custom-call | flops 32999999488 | bytes 1000000 | tf_op jit(solution)/shard_map/grad_kv/pallas_call | solution.py:68
  81.5 5.5 %collective-permute-start.13 = (bf16[2,128,1024]{2,1,0:T(8,128)(2,1)S(1)}, bf16[2,128,1024]{2,1,0:T(8,128)(2,1)S(1)}, u32[]{:S(2)}, u32[]{:S(2)}) collective-permute-start(bf16[2,128,1024]{2,1,0:T(8,128)(2,1)S(1)} %get-tuple-element.80), channel_id=1, source_target_pairs={{0,4},{4,8},{8,12},{12,16},{16,20},{20,24},{24,28},{1,5},{5,9},{9,... | collective-permute-start | bytes 1572872 | tf_op jit(solution)/shard_map/ppermute | solution.py:409
  87.0 1.3 %collective-permute-start.14 = (bf16[2,128,1024]{2,1,0:T(8,128)(2,1)S(1)}, bf16[2,128,1024]{2,1,0:T(8,128)(2,1)S(1)}, u32[]{:S(2)}, u32[]{:S(2)}) collective-permute-start(bf16[2,128,1024]{2,1,0:T(8,128)(2,1)S(1)} %get-tuple-element.81), channel_id=1, source_target_pairs={{4,0},{8,4},{12,8},{16,12},{20,16},{24,20},{28,24},{5,1},{9,5},{13... | collective-permute-start | bytes 1572872 | tf_op jit(solution)/shard_map/ppermute | solution.py:409
  88.3 0.7 own_q.1.refs_0_
  89.0 1.3 %normed.1 = bf16[512,1024]{1,0:T(8,128)(2,1)} custom-call(f32[512,1024]{1,0:T(8,128)S(1)} %get-tuple-element.65.u_ref, f32[512,128]{1,0:T(8,128)S(1)} %get-tuple-element.67.inverse_ref, bf16[512,1024]{1,0:T(8,128)(2,1)S(1)} %get-tuple-element.75._.refs_1_.refs_0_), custom_call_target="tpu_custom_call" | custom-call | flops 2200000000 | bytes 1000000 | tf_op jit(solution)/shard_map/normed/pallas_call | solution.py:68
  90.3 0.8 collective-permute-done.11.left_ref
  91.1 1.4 %finish_q.1 = (bf16[512,1024]{1,0:T(8,128)(2,1)}, bf16[16,128]{1,0:T(8,128)(2,1)S(1)}) custom-call(s32[2,128]{1,0:T(2,128)S(1)} %bitcast.11, bf16[1,128,1024]{2,1,0:T(8,128)(2,1)S(1)} %collective-permute-done.11.left_ref, bf16[1,128,1024]{2,1,0:T(8,128)(2,1)S(1)} %collective-permute-done.12.right_ref, bf16[512,1024]{1,0:T(8,128)(2,1)S(1)} %own_q.1.refs_0_), custom_call_target="tpu_custom_call" | custom-call | flops 2200000000 | bytes 1000000 | tf_op jit(solution)/shard_map/finish_q/pallas_call | solution.py:68
  92.5 1.2 %own_kv.1 = (bf16[512,1024]{1,0:T(8,128)(2,1)S(1)}, bf16[512,1024]{1,0:T(8,128)(2,1)S(1)}) custom-call(s32[1,512]{1,0:T(1,128)S(1)} %bitcast.9, bf16[512,1024]{1,0:T(8,128)(2,1)S(1)} %get-tuple-element.75._.refs_1_.refs_0_, bf16[512,1024]{1,0:T(8,128)(2,1)S(1)} %get-tuple-element.82.refs_1_, bf16[16,128]{1,0:T(8,128)(2,1)S(1)} %get-tuple-element.83.refs_2_), custom_call_target="tpu_custom_call" | custom-call | flops 2200000000 | bytes 1000000 | tf_op jit(solution)/shard_map/own_kv/pallas_call | solution.py:68
  93.8 19.8 %collective-permute-done.13.left_ref = bf16[2,128,1024]{2,1,0:T(8,128)(2,1)S(1)} collective-permute-done((bf16[2,128,1024]{2,1,0:T(8,128)(2,1)S(1)}, bf16[2,128,1024]{2,1,0:T(8,128)(2,1)S(1)}, u32[]{:S(2)}, u32[]{:S(2)}) %collective-permute-start.13) | collective-permute-done | bytes 524320 | tf_op jit(solution)/shard_map/ppermute | solution.py:409
  113.6 1.8 %finish_kv.1 = (bf16[512,1024]{1,0:T(8,128)(2,1)}, bf16[512,1024]{1,0:T(8,128)(2,1)}) custom-call(s32[2,128]{1,0:T(2,128)S(1)} %bitcast.12, bf16[2,128,1024]{2,1,0:T(8,128)(2,1)S(1)} %collective-permute-done.13.left_ref, bf16[2,128,1024]{2,1,0:T(8,128)(2,1)S(1)} %collective-permute-done.14.right_ref, bf16[512,1024]{1,0:T(8,128)(2,1)S(1)} %get-tuple-element.84.refs_0_, ...), custom_call_target="tpu_custom_call" | custom-call | flops 2200000000 | bytes 1000000 | tf_op jit(solution)/shard_map/finish_kv/pallas_call | solution.py:68
  (31 shorter events, 1.5 us)
Async XLA Ops:
  0.6 11.5 %copy-start = (bf16[512,1024]{1,0:T(8,128)(2,1)S(1)}, bf16[512,1024]{1,0:T(8,128)(2,1)}, u32[]{:S(2)}) copy-start(bf16[512,1024]{1,0:T(8,128)(2,1)} %k_ref.1) | copy-start | bytes 3145732
  0.6 11.5 %copy-start.1 = (bf16[512,1024]{1,0:T(8,128)(2,1)S(1)}, bf16[512,1024]{1,0:T(8,128)(2,1)}, u32[]{:S(2)}) copy-start(bf16[512,1024]{1,0:T(8,128)(2,1)} %v_ref.1) | copy-start | bytes 3145732
  0.7 11.5 %copy-start.2 = (bf16[512,1024]{1,0:T(8,128)(2,1)S(1)}, bf16[512,1024]{1,0:T(8,128)(2,1)}, u32[]{:S(2)}) copy-start(bf16[512,1024]{1,0:T(8,128)(2,1)} %q_ref.1) | copy-start | bytes 3145732
  0.7 11.5 %copy-start.4 = (f32[512,8]{0,1:T(8,128)S(1)}, f32[512,8]{0,1:T(8,128)}, u32[]{:S(2)}) copy-start(f32[512,8]{0,1:T(8,128)} %param.12) | copy-start | bytes 49156
  0.7 11.5 %copy-start.5 = (s32[512]{0:T(512)S(1)}, s32[512]{0:T(512)}, u32[]{:S(2)}) copy-start(s32[512]{0:T(512)} %param.15) | copy-start | bytes 6148
  0.7 11.5 %copy-start.7 = (s32[8]{0:T(128)S(1)}, s32[8]{0:T(128)}, u32[]{:S(2)}) copy-start(s32[8]{0:T(128)} %docs_ref.1) | copy-start | bytes 100
  5.1 34.4 %collective-permute-start.2 = (bf16[2,128,1024]{2,1,0:T(8,128)(2,1)}, bf16[2,128,1024]{2,1,0:T(8,128)(2,1)}, u32[]{:S(2)}, u32[]{:S(2)}) collective-permute-start(bf16[2,128,1024]{2,1,0:T(8,128)(2,1)} %get-tuple-element.51), channel_id=1, source_target_pairs={{0,4},{4,8},{8,12},{12,16},{16,20},{20,24},{24,28},{1,5},{5,9},{9,... | collective-permute-start | bytes 1572872 | tf_op jit(solution)/shard_map/ppermute | solution.py:409
  10.8 28.7 %collective-permute-start.3 = (bf16[2,128,1024]{2,1,0:T(8,128)(2,1)}, bf16[2,128,1024]{2,1,0:T(8,128)(2,1)}, u32[]{:S(2)}, u32[]{:S(2)}) collective-permute-start(bf16[2,128,1024]{2,1,0:T(8,128)(2,1)} %get-tuple-element.52), channel_id=1, source_target_pairs={{4,0},{8,4},{12,8},{16,12},{20,16},{24,20},{28,24},{5,1},{9,5},{13... | collective-permute-start | bytes 1572872 | tf_op jit(solution)/shard_map/ppermute | solution.py:409
  17.0 34.4 %collective-permute-start = (bf16[1,128,1024]{2,1,0:T(8,128)(2,1)S(1)}, bf16[1,128,1024]{2,1,0:T(8,128)(2,1)S(1)}, u32[]{:S(2)}, u32[]{:S(2)}) collective-permute-start(bf16[1,128,1024]{2,1,0:T(8,128)(2,1)S(1)} %get-tuple-element.48), channel_id=1, source_target_pairs={{0,4},{4,8},{8,12},{12,16},{16,20},{20,24},{24,28},{1,5},{5,9},{9,... | collective-permute-start | bytes 786440 | tf_op jit(solution)/shard_map/ppermute | solution.py:409
  21.6 29.9 %collective-permute-start.1 = (bf16[1,128,1024]{2,1,0:T(8,128)(2,1)S(1)}, bf16[1,128,1024]{2,1,0:T(8,128)(2,1)S(1)}, u32[]{:S(2)}, u32[]{:S(2)}) collective-permute-start(bf16[1,128,1024]{2,1,0:T(8,128)(2,1)S(1)} %get-tuple-element.49), channel_id=1, source_target_pairs={{4,0},{8,4},{12,8},{16,12},{20,16},{24,20},{28,24},{5,1},{9,5},{13... | collective-permute-start | bytes 786440 | tf_op jit(solution)/shard_map/ppermute | solution.py:409
  41.6 12.5 %collective-permute-start.4 = (bf16[8,144,128]{2,1,0:T(8,128)(2,1)S(1)}, bf16[8,144,128]{2,1,0:T(8,128)(2,1)S(1)}, u32[]{:S(2)}, u32[]{:S(2)}) collective-permute-start(bf16[8,144,128]{2,1,0:T(8,128)(2,1)S(1)} %state.1._), channel_id=1, source_target_pairs={{0,4},{4,8},{8,12},{12,16},{16,20},{20,24},{24,28},{1,5},{5,9},{9,... | collective-permute-start | bytes 884744 | tf_op jit(solution)/shard_map/ppermute | solution.py:409
  46.0 8.1 %collective-permute-start.5 = (bf16[8,144,128]{2,1,0:T(8,128)(2,1)S(1)}, bf16[8,144,128]{2,1,0:T(8,128)(2,1)S(1)}, u32[]{:S(2)}, u32[]{:S(2)}) collective-permute-start(bf16[8,144,128]{2,1,0:T(8,128)(2,1)S(1)} %state.1._), channel_id=1, source_target_pairs={{0,8},{4,12},{8,16},{12,20},{16,24},{20,28},{1,9},{5,13},{9,17},{1... | collective-permute-start | bytes 884744 | tf_op jit(solution)/shard_map/ppermute | solution.py:409
  51.5 2.7 %copy-start.3 = (bf16[512,1024]{1,0:T(8,128)(2,1)S(1)}, bf16[512,1024]{1,0:T(8,128)(2,1)}, u32[]{:S(2)}) copy-start(bf16[512,1024]{1,0:T(8,128)(2,1)} %ct_ref.3) | copy-start | bytes 3145732
  51.5 2.7 %copy-start.8 = (f32[8]{0:T(128)S(1)}, f32[8]{0:T(128)}, u32[]{:S(2)}) copy-start(f32[8]{0:T(128)} %scale_ref.3) | copy-start | bytes 100
  55.9 3.1 %collective-permute-start.6 = (f32[2,512]{1,0:T(2,128)S(1)}, f32[2,512]{1,0:T(2,128)S(1)}, u32[]{:S(2)}, u32[]{:S(2)}) collective-permute-start(f32[2,512]{1,0:T(2,128)S(1)} %get-tuple-element.66.refs_0_), channel_id=1, source_target_pairs={{0,1},{1,2},{2,3},{3,0},{4,5},{5,6},{6,7},{7,4},{8,9},{9,10},{10,1... | collective-permute-start | bytes 12296 | tf_op jit(solution)/shard_map/ppermute | solution.py:414
  55.9 3.7 %collective-permute-start.7 = (f32[2,512]{1,0:T(2,128)S(1)}, f32[2,512]{1,0:T(2,128)S(1)}, u32[]{:S(2)}, u32[]{:S(2)}) collective-permute-start(f32[2,512]{1,0:T(2,128)S(1)} %get-tuple-element.66.refs_0_), channel_id=1, source_target_pairs={{0,2},{1,3},{2,0},{3,1},{4,6},{5,7},{6,4},{7,5},{8,10},{9,11},{10,... | collective-permute-start | bytes 12296 | tf_op jit(solution)/shard_map/ppermute | solution.py:414
  57.5 2.7 %collective-permute-start.8 = (f32[2,512]{1,0:T(2,128)S(1)}, f32[2,512]{1,0:T(2,128)S(1)}, u32[]{:S(2)}, u32[]{:S(2)}) collective-permute-start(f32[2,512]{1,0:T(2,128)S(1)} %get-tuple-element.66.refs_0_), channel_id=1, source_target_pairs={{0,3},{1,0},{2,1},{3,2},{4,7},{5,4},{6,5},{7,6},{8,11},{9,8},{10,9... | collective-permute-start | bytes 12296 | tf_op jit(solution)/shard_map/ppermute | solution.py:414
  62.4 17.2 %collective-permute-start.10 = (bf16[8,144,128]{2,1,0:T(8,128)(2,1)S(1)}, bf16[8,144,128]{2,1,0:T(8,128)(2,1)S(1)}, u32[]{:S(2)}, u32[]{:S(2)}) collective-permute-start(bf16[8,144,128]{2,1,0:T(8,128)(2,1)S(1)} %get-tuple-element.68), channel_id=1, source_target_pairs={{8,0},{12,4},{16,8},{20,12},{24,16},{28,20},{9,1},{13,5},{17,9},{2... | collective-permute-start | bytes 884744 | tf_op jit(solution)/shard_map/ppermute | solution.py:409
  63.7 15.9 %collective-permute-start.9 = (bf16[8,144,128]{2,1,0:T(8,128)(2,1)S(1)}, bf16[8,144,128]{2,1,0:T(8,128)(2,1)S(1)}, u32[]{:S(2)}, u32[]{:S(2)}) collective-permute-start(bf16[8,144,128]{2,1,0:T(8,128)(2,1)S(1)} %get-tuple-element.68), channel_id=1, source_target_pairs={{4,0},{8,4},{12,8},{16,12},{20,16},{24,20},{28,24},{5,1},{9,5},{13... | collective-permute-start | bytes 884744 | tf_op jit(solution)/shard_map/ppermute | solution.py:409
  68.0 23.1 %collective-permute-start.11 = (bf16[1,128,1024]{2,1,0:T(8,128)(2,1)S(1)}, bf16[1,128,1024]{2,1,0:T(8,128)(2,1)S(1)}, u32[]{:S(2)}, u32[]{:S(2)}) collective-permute-start(bf16[1,128,1024]{2,1,0:T(8,128)(2,1)S(1)} %get-tuple-element.76), channel_id=1, source_target_pairs={{0,4},{4,8},{8,12},{12,16},{16,20},{20,24},{24,28},{1,5},{5,9},{9,... | collective-permute-start | bytes 786440 | tf_op jit(solution)/shard_map/ppermute | solution.py:409
  76.4 14.7 %collective-permute-start.12 = (bf16[1,128,1024]{2,1,0:T(8,128)(2,1)S(1)}, bf16[1,128,1024]{2,1,0:T(8,128)(2,1)S(1)}, u32[]{:S(2)}, u32[]{:S(2)}) collective-permute-start(bf16[1,128,1024]{2,1,0:T(8,128)(2,1)S(1)} %get-tuple-element.77), channel_id=1, source_target_pairs={{4,0},{8,4},{12,8},{16,12},{20,16},{24,20},{28,24},{5,1},{9,5},{13... | collective-permute-start | bytes 786440 | tf_op jit(solution)/shard_map/ppermute | solution.py:409
  81.5 32.1 %collective-permute-start.13 = (bf16[2,128,1024]{2,1,0:T(8,128)(2,1)S(1)}, bf16[2,128,1024]{2,1,0:T(8,128)(2,1)S(1)}, u32[]{:S(2)}, u32[]{:S(2)}) collective-permute-start(bf16[2,128,1024]{2,1,0:T(8,128)(2,1)S(1)} %get-tuple-element.80), channel_id=1, source_target_pairs={{0,4},{4,8},{8,12},{12,16},{16,20},{20,24},{24,28},{1,5},{5,9},{9,... | collective-permute-start | bytes 1572872 | tf_op jit(solution)/shard_map/ppermute | solution.py:409
  87.0 26.6 %collective-permute-start.14 = (bf16[2,128,1024]{2,1,0:T(8,128)(2,1)S(1)}, bf16[2,128,1024]{2,1,0:T(8,128)(2,1)S(1)}, u32[]{:S(2)}, u32[]{:S(2)}) collective-permute-start(bf16[2,128,1024]{2,1,0:T(8,128)(2,1)S(1)} %get-tuple-element.81), channel_id=1, source_target_pairs={{4,0},{8,4},{12,8},{16,12},{20,16},{24,20},{28,24},{5,1},{9,5},{13... | collective-permute-start | bytes 1572872 | tf_op jit(solution)/shard_map/ppermute | solution.py:409
  89.0 2.1 %copy-start.6 = (s32[1,2,128]{2,1,0:T(2,128)S(1)}, s32[1,2,128]{2,1,0:T(2,128)}, u32[]{:S(2)}) copy-start(s32[1,2,128]{2,1,0:T(2,128)} %param.14) | copy-start | bytes 3076
where the time goes:
time: 117 us; the launch traced here: 115 us
  starting transfers between devices  42.7 us (36%)
  waiting for transfers between devices  38.5 us (33%)
  Pallas kernels  33 us (28%)
    ppermute x12, starting transfers between devices, shifted(): lax.ppermute(array, 'seq', [(i, i + by) for i in range(peers) if 0 <= i +...  39.7 us
    ppermute x12, waiting for transfers between devices, shifted(): lax.ppermute(array, 'seq', [(i, i + by) for i in range(peers) if 0 <= i +...  37.2 us
    pallas_call x15, Pallas kernels, local(): pl.pallas_call(kernel, in_specs=specs, out_specs=[vmem] * len(out_shape),...  33 us
    ppermute x3, starting transfers between devices, turned_by(): lax.ppermute(array, 'head', [(i, (i + by) % peers) for i in range(peers)])  3.01 us
  transfers between devices with their start and end apart: 15, of which 6 were waited for; matrix products, arithmetic and copies ran while one was open for 0% of the time, Pallas kernels for 20%

commit v1 on v0

--- a/solution.py
+++ b/solution.py
@@ -134,7 +134,7 @@
 
 
 def prep_kernel(
-    docs_ref, first_ref, take_ref, log_ref, named_ref, q_ref, k_ref, v_ref,
+    docs_ref, take_ref, log_ref, named_ref, q_ref, k_ref, v_ref,
     left_ref, right_ref, qo_ref, ko_ref, vo_ref, hot_ref,
     mask_ref, cols_ref, rows_ref, through_ref, state_ref, leave_ref, own_ref,
 ):
@@ -146,7 +146,7 @@
         left_ref[0, :, part] = picked[:capacity]
         right_ref[0, :, part] = picked[capacity:]
 
-    first = first_ref[0]
+    first = (lax.axis_index("seq") * rows).astype(jnp.int32)
     position = first + iota((rows, 1), 0)
     position_row = first + iota((1, rows), 1)
     segment = jnp.zeros((rows, 1), jnp.int32)
@@ -202,7 +202,7 @@
         state_ref[h] = dot_tn(kf, vo_ref[:, part])
 
 
-def prep(docs, first, take, log_decay, named, q, k, v):
+def prep(docs, take, log_decay, named, q, k, v):
     rows, features = q.shape
     heads = log_decay.shape[0]
     width = features // heads
@@ -222,8 +222,8 @@
             sds((heads, width, width), F32),
             sds((2 * capacity, 128), F32),
         ],
-        (docs, first, take, log_decay, named, q, k, v),
-        scalars=2,
+        (docs, take, log_decay, named, q, k, v),
+        scalars=1,
         scratch=(pltpu.VMEM((rows, rows), BF),),
     )
 
@@ -270,19 +270,27 @@
             o_ref[here, part] = dot(p, v_ref[:reach, part])
 
 
-def joined(near_ref, far_ref, h, width):
+def shards_before(direction):
+    index = lax.axis_index("seq")
+    return index if direction > 0 else lax.axis_size("seq") - 1 - index
+
+
+def joined(before, near_ref, far_ref, h, width):
     through = jnp.sum(near_ref[h, width:, :].astype(F32), axis=0, keepdims=True)
     near = near_ref[h, :width, :].astype(F32)
-    return (near + through * far_ref[h, :width, :].astype(F32)).astype(BF)
+    far = through * far_ref[h, :width, :].astype(F32)
+    near = jnp.where(before >= 1, near, 0.0)
+    return (near + jnp.where(before >= 2, far, 0.0)).astype(BF)
 
 
 def output_kernel(scale_ref, o_ref, q_ref, near_ref, far_ref, cols_ref, ct_ref, u_ref, h_ref, sums_ref):
     rows, features = q_ref.shape
     heads, width = h_ref.shape[:2]
+    before = shards_before(1)
     squares = jnp.zeros((rows, width), F32)
     cross = jnp.zeros((rows, width), F32)
     for h, part in enumerate(head_slices(features, heads)):
-        carried_in = joined(near_ref, far_ref, h, width)
+        carried_in = joined(before, near_ref, far_ref, h, width)
         h_ref[h] = carried_in
         outer = dot(q_ref[:, part], carried_in) * cols_ref[1, :, h : h + 1]
         u = (o_ref[:, part] + outer) * scale_ref[h]
@@ -366,8 +374,9 @@
 def grad_kv_kernel(take_ref, near_ref, far_ref, k_ref, v_ref, cols_ref, dki_ref, dvi_ref, dk_ref, dv_ref, left_ref, right_ref):
     rows, features = k_ref.shape
     heads = near_ref.shape[0]
-    for h, part in enumerate(head_slices(features, heads)):
-        state_grad = joined(near_ref, far_ref, h, features // heads)
+    before = shards_before(-1)
+    for h, part in enumerate(head_slices(features, heads)):
+        state_grad = joined(before, near_ref, far_ref, h, features // heads)
         leaving = cols_ref[0, :, h : h + 1]
         dk_ref[:, part] = (dki_ref[:, part] + leaving * dot_nt(v_ref[:, part], state_grad)).astype(BF)
         dv_ref[:, part] = (dvi_ref[:, part] + leaving * dot(k_ref[:, part], state_grad)).astype(BF)
@@ -406,6 +415,11 @@
 
 def shifted(array, by):
     peers = lax.axis_size("seq")
+    return lax.ppermute(array, "seq", [(i, (i + by) % peers) for i in range(peers)])
+
+
+def shifted_open(array, by):
+    peers = lax.axis_size("seq")
     return lax.ppermute(array, "seq", [(i, i + by) for i in range(peers) if 0 <= i + by < peers])
 
 
@@ -415,7 +429,8 @@
 
 
 def carried(message, direction):
-    reach = lax.axis_size("seq") // 4
+    peers = lax.axis_size("seq")
+    reach = peers // 4
     if reach <= 2:
         return shifted(message, direction), shifted(message, 2 * direction)
     size = message.shape[2]
@@ -423,7 +438,7 @@
     through = jnp.sum(message[:, size:, :1].astype(F32), axis=1, keepdims=True)
 
     def relay(_, state_here):
-        return shifted((through * state_here + own_state).astype(BF), direction).astype(F32)
+        return shifted_open((through * state_here + own_state).astype(BF), direction).astype(F32)
 
     incoming = lax.fori_loop(0, reach, relay, jnp.zeros_like(own_state)).astype(BF)
     near = jnp.concatenate([incoming, jnp.zeros_like(message[:, size:])], axis=1)
@@ -440,7 +455,6 @@
     capacity = send_rows.shape[2]
     send = send_rows.reshape(2, capacity)
     take = take_rows.reshape(1, rows)
-    first = (lax.axis_index("seq") * rows).astype(jnp.int32).reshape(1)
     total = features * lax.axis_size("head")
     full, full32 = sds((rows, features)), sds((rows, features), F32)
     squares = sds((heads, rows, rows))
@@ -451,7 +465,7 @@
     kv_before, kv_after = shifted(kv_right, 1), shifted(kv_left, -1)
     (
         q_left, q_right, q_own, k_own, v_own, hot, mask, cols, turned, through, state_own, leave
-    ) = prep(doc_lengths, first, take, log_decay.T, named, queries, key_vectors, value_vectors)
+    ) = prep(doc_lengths, take, log_decay.T, named, queries, key_vectors, value_vectors)
     q_before, q_after = shifted(q_right, 1), shifted(q_left, -1)
     (message,) = local(
         state_kernel, "state", 30, [message_shape], (kv_before, kv_after, leave, state_own, through)

time: 117 us -> 111 us (0.949); the launches traced: 115 us -> 111 us
  starting transfers between devices: 42.7 us -> 32.1 us
  waiting for transfers between devices: 38.5 us -> 47.4 us
  Pallas kernels: 33 us -> 30.2 us
    ppermute x12, starting transfers between devices: 39.7 us -> 29.1 us  [shifted(): lax.ppermute(array, 'seq', [(i, (i + by) % peers) for i in range(peers)])]
    ppermute x12, waiting for transfers between devices: 37.2 us -> 46.1 us  [shifted(): lax.ppermute(array, 'seq', [(i, (i + by) % peers) for i in range(peers)])]
    pallas_call x15, Pallas kernels: 33 us -> 30.2 us  [local(): pl.pallas_call(kernel, in_specs=specs, out_specs=[vmem] * len(out_shape),...]
  transfers between devices with their start and end apart: 15 -> 15, of which waited for: 6 -> 10; matrix products, arithmetic and copies ran while one was open for 0% -> 0% of each run, Pallas kernels for 20% -> 19%
where the time goes in v1:
time: 111 us
  waiting for transfers between devices  47.4 us (43%)
  starting transfers between devices  32.1 us (29%)
  Pallas kernels  30.2 us (27%)
    ppermute x12, waiting for transfers between devices, shifted(): lax.ppermute(array, 'seq', [(i, (i + by) % peers) for i in range(peers)])  46.1 us
    pallas_call x15, Pallas kernels, local(): pl.pallas_call(kernel, in_specs=specs, out_specs=[vmem] * len(out_shape),...  30.2 us
    ppermute x12, starting transfers between devices, shifted(): lax.ppermute(array, 'seq', [(i, (i + by) % peers) for i in range(peers)])  29.1 us
    ppermute x3, starting transfers between devices, turned_by(): lax.ppermute(array, 'head', [(i, (i + by) % peers) for i in range(peers)])  3 us
  transfers between devices with their start and end apart: 15, of which 10 were waited for; matrix products, arithmetic and copies ran while one was open for 0% of the time, Pallas kernels for 19%

profile of v1, /device:TPU:0, one launch (start us, length us, event | category | flops | bytes accessed | tf_op | source)
XLA Modules:
  0.0 110.6 jit_solution(15451093793834583069)
XLA Ops:
  0.7 3.5 %pick.1 = (bf16[2,128,1024]{2,1,0:T(8,128)(2,1)S(1)}, bf16[2,128,1024]{2,1,0:T(8,128)(2,1)S(1)}, bf16[256,512]{1,0:T(8,128)(2,1)S(1)}) custom-call(s32[2,128]{1,0:T(2,128)} %bitcast.9, bf16[512,1024]{1,0:T(8,128)(2,1)} %k_ref.1, bf16[512,1024]{1,0:T(8,128)(2,1)} %v_ref.1), custom_call_target="tpu_custom_call" | custom-call | flops 2200000000 | bytes 1000000 | tf_op jit(solution)/shard_map/pick/pallas_call | solution.py:68
  4.2 3.0 %collective-permute-start.2 = (bf16[2,128,1024]{2,1,0:T(8,128)(2,1)S(1)}, bf16[2,128,1024]{2,1,0:T(8,128)(2,1)S(1)}, u32[]{:S(2)}, u32[]{:S(2)}) collective-permute-start(bf16[2,128,1024]{2,1,0:T(8,128)(2,1)S(1)} %get-tuple-element.51), channel_id=1, source_target_pairs={{0,4},{4,8},{8,12},{12,16},{16,20},{20,24},{24,28},{28,0},{1,5},{5... | collective-permute-start | bytes 1572872 | tf_op jit(solution)/shard_map/ppermute | solution.py:418
  7.2 3.1 %collective-permute-start.3 = (bf16[2,128,1024]{2,1,0:T(8,128)(2,1)S(1)}, bf16[2,128,1024]{2,1,0:T(8,128)(2,1)S(1)}, u32[]{:S(2)}, u32[]{:S(2)}) collective-permute-start(bf16[2,128,1024]{2,1,0:T(8,128)(2,1)S(1)} %get-tuple-element.52), channel_id=1, source_target_pairs={{0,28},{4,0},{8,4},{12,8},{16,12},{20,16},{24,20},{28,24},{1,29},{... | collective-permute-start | bytes 1572872 | tf_op jit(solution)/shard_map/ppermute | solution.py:418
  10.4 4.9 %prep.1 = (bf16[1,128,1024]{2,1,0:T(8,128)(2,1)S(1)}, bf16[1,128,1024]{2,1,0:T(8,128)(2,1)S(1)}, bf16[512,1024]{1,0:T(8,128)(2,1)S(1)}, bf16[512,1024]{1,0:T(8,1...) custom-call(s32[8]{0:T(128)S(1)} %copy-done.7, ...), custom_call_target="tpu_custom_call" | custom-call | flops 32999999488 | bytes 1000000 | tf_op jit(solution)/shard_map/prep/pallas_call | solution.py:68
  15.4 4.7 %collective-permute-start.1 = (bf16[1,128,1024]{2,1,0:T(8,128)(2,1)S(1)}, bf16[1,128,1024]{2,1,0:T(8,128)(2,1)S(1)}, u32[]{:S(2)}, u32[]{:S(2)}) collective-permute-start(bf16[1,128,1024]{2,1,0:T(8,128)(2,1)S(1)} %get-tuple-element.49), channel_id=1, source_target_pairs={{0,28},{4,0},{8,4},{12,8},{16,12},{20,16},{24,20},{28,24},{1,29},{... | collective-permute-start | bytes 786440 | tf_op jit(solution)/shard_map/ppermute | solution.py:418
  20.1 16.3 %collective-permute-done.2.left_ref = bf16[2,128,1024]{2,1,0:T(8,128)(2,1)S(1)} collective-permute-done((bf16[2,128,1024]{2,1,0:T(8,128)(2,1)S(1)}, bf16[2,128,1024]{2,1,0:T(8,128)(2,1)S(1)}, u32[]{:S(2)}, u32[]{:S(2)}) %collective-permute-start.2) | collective-permute-done | bytes 524320 | tf_op jit(solution)/shard_map/ppermute | solution.py:418
  36.4 2.5 %collective-permute-done.3.right_ref = bf16[2,128,1024]{2,1,0:T(8,128)(2,1)S(1)} collective-permute-done((bf16[2,128,1024]{2,1,0:T(8,128)(2,1)S(1)}, bf16[2,128,1024]{2,1,0:T(8,128)(2,1)S(1)}, u32[]{:S(2)}, u32[]{:S(2)}) %collective-permute-start.3) | collective-permute-done | bytes 524320 | tf_op jit(solution)/shard_map/ppermute | solution.py:418
  38.9 0.9 state.1._
  39.9 1.5 %collective-permute-start.5 = (bf16[8,144,128]{2,1,0:T(8,128)(2,1)S(1)}, bf16[8,144,128]{2,1,0:T(8,128)(2,1)S(1)}, u32[]{:S(2)}, u32[]{:S(2)}) collective-permute-start(bf16[8,144,128]{2,1,0:T(8,128)(2,1)S(1)} %state.1._), channel_id=1, source_target_pairs={{0,8},{4,12},{8,16},{12,20},{16,24},{20,28},{24,0},{28,4},{1,9},{5... | collective-permute-start | bytes 884744 | tf_op jit(solution)/shard_map/ppermute | solution.py:418
  41.4 0.7 assemble.1
  42.2 4.0 %collective-permute-done.1.right_ref = bf16[1,128,1024]{2,1,0:T(8,128)(2,1)S(1)} collective-permute-done((bf16[1,128,1024]{2,1,0:T(8,128)(2,1)S(1)}, bf16[1,128,1024]{2,1,0:T(8,128)(2,1)S(1)}, u32[]{:S(2)}, u32[]{:S(2)}) %collective-permute-start.1) | collective-permute-done | bytes 262176 | tf_op jit(solution)/shard_map/ppermute | solution.py:418
  46.2 2.7 %inside.1 = (bf16[512,1024]{1,0:T(8,128)(2,1)S(1)}, bf16[8,512,512]{2,1,0:T(8,128)(2,1)S(1)}, f32[512,1024]{1,0:T(8,128)S(1)}) custom-call(bf16[512,256]{1,0:T(8,128)(2,1)S(1)} %get-tuple-element.47.hot_ref, bf16[1,128,1024]{2,1,0:T(8,128)(2,1)S(1)} %collective-permute-done.left_ref, bf16[1,128,1024]{2,1,0:T(8,128)(2,1)S(1)} %collective-permute-done.1.right_ref, ...), custom_call_target="tpu_custom_call" | custom-call | flops 32999999488 | bytes 1000000 | tf_op jit(solution)/shard_map/inside/pallas_call | solution.py:68
  48.9 3.0 %collective-permute-done.4.near_ref = bf16[8,144,128]{2,1,0:T(8,128)(2,1)S(1)} collective-permute-done((bf16[8,144,128]{2,1,0:T(8,128)(2,1)S(1)}, bf16[8,144,128]{2,1,0:T(8,128)(2,1)S(1)}, u32[]{:S(2)}, u32[]{:S(2)}) %collective-permute-start.4) | collective-permute-done | bytes 294944 | tf_op jit(solution)/shard_map/ppermute | solution.py:418
  51.9 1.7 %output.1 = (f32[512,1024]{1,0:T(8,128)S(1)}, bf16[8,128,128]{2,1,0:T(8,128)(2,1)S(1)}, f32[2,512]{1,0:T(2,128)S(1)}) custom-call(f32[8]{0:T(128)S(1)} %copy-done.8, f32[512,1024]{1,0:T(8,128)S(1)} %get-tuple-element.63.o_ref, bf16[512,1024]{1,0:T(8,128)(2,1)S(1)} %get-tuple-element.64.q_ref, bf16[8,144,128]{2,1,0:T(8,128)(2,1)S(1)} %collective-permute-done.4.near_ref, ...), custom_call_target="tpu_custom_call" | custom-call | flops 3300000000 | bytes 1000000 | tf_op jit(solution)/shard_map/output/pallas_call | solution.py:68
  53.7 1.6 %collective-permute-start.7 = (f32[2,512]{1,0:T(2,128)S(1)}, f32[2,512]{1,0:T(2,128)S(1)}, u32[]{:S(2)}, u32[]{:S(2)}) collective-permute-start(f32[2,512]{1,0:T(2,128)S(1)} %get-tuple-element.66.refs_0_), channel_id=1, source_target_pairs={{0,2},{1,3},{2,0},{3,1},{4,6},{5,7},{6,4},{7,5},{8,10},{9,11},{10,... | collective-permute-start | bytes 12296 | tf_op jit(solution)/shard_map/ppermute | solution.py:428
  55.3 1.4 %collective-permute-start.8 = (f32[2,512]{1,0:T(2,128)S(1)}, f32[2,512]{1,0:T(2,128)S(1)}, u32[]{:S(2)}, u32[]{:S(2)}) collective-permute-start(f32[2,512]{1,0:T(2,128)S(1)} %get-tuple-element.66.refs_0_), channel_id=1, source_target_pairs={{0,3},{1,0},{2,1},{3,2},{4,7},{5,4},{6,5},{7,6},{8,11},{9,8},{10,9... | collective-permute-start | bytes 12296 | tf_op jit(solution)/shard_map/ppermute | solution.py:428
  58.0 2.3 %norm.1 = (bf16[512,1024]{1,0:T(8,128)(2,1)S(1)}, bf16[8,144,128]{2,1,0:T(8,128)(2,1)S(1)}, f32[512,128]{1,0:T(8,128)S(1)}) custom-call(f32[8]{0:T(128)S(1)} %copy-done.8, f32[512,1024]{1,0:T(8,128)S(1)} %get-tuple-element.65.u_ref, bf16[512,1024]{1,0:T(8,128)(2,1)S(1)} %copy-done.3, bf16[512,1024]{1,0:T(8,128)(2,1)S(1)} %get-tuple-element.64.q_ref, ...), custom_call_target="tpu_custom_call" | custom-call | flops 4400000000 | bytes 1000000 | tf_op jit(solution)/shard_map/norm/pallas_call | solution.py:68
  60.2 3.5 %collective-permute-start.10 = (bf16[8,144,128]{2,1,0:T(8,128)(2,1)S(1)}, bf16[8,144,128]{2,1,0:T(8,128)(2,1)S(1)}, u32[]{:S(2)}, u32[]{:S(2)}) collective-permute-start(bf16[8,144,128]{2,1,0:T(8,128)(2,1)S(1)} %get-tuple-element.68), channel_id=1, source_target_pairs={{0,24},{4,28},{8,0},{12,4},{16,8},{20,12},{24,16},{28,20},{1,25},{... | collective-permute-start | bytes 884744 | tf_op jit(solution)/shard_map/ppermute | solution.py:418
  63.8 3.0 %collective-permute-start.9 = (bf16[8,144,128]{2,1,0:T(8,128)(2,1)S(1)}, bf16[8,144,128]{2,1,0:T(8,128)(2,1)S(1)}, u32[]{:S(2)}, u32[]{:S(2)}) collective-permute-start(bf16[8,144,128]{2,1,0:T(8,128)(2,1)S(1)} %get-tuple-element.68), channel_id=1, source_target_pairs={{0,28},{4,0},{8,4},{12,8},{16,12},{20,16},{24,20},{28,24},{1,29},{... | collective-permute-start | bytes 884744 | tf_op jit(solution)/shard_map/ppermute | solution.py:418
  66.7 3.3 %grad_q.1 = (bf16[512,1024]{1,0:T(8,128)(2,1)S(1)}, bf16[8,512,512]{2,1,0:T(8,128)(2,1)S(1)}, bf16[1,128,1024]{2,1,0:T(8,128)(2,1)S(1)}, bf16[1,128,1024]{2,1,0:T(8,128)(2,1)S(1)}) custom-call(s32[1,512]{1,0:T(1,128)S(1)} %bitcast.5, bf16[512,1024]{1,0:T(8,128)(2,1)S(1)} %get-tuple-element.69.g_ref, bf16[512,1024]{1,0:T(8,128)(2,1)S(1)} %get-tuple-element.58.k_ref, ...), custom_call_target="tpu_custom_call" | custom-call | flops 32999999488 | bytes 1000000 | tf_op jit(solution)/shard_map/grad_q/pallas_call | solution.py:68
  70.2 4.6 %collective-permute-start.12 = (bf16[1,128,1024]{2,1,0:T(8,128)(2,1)S(1)}, bf16[1,128,1024]{2,1,0:T(8,128)(2,1)S(1)}, u32[]{:S(2)}, u32[]{:S(2)}) collective-permute-start(bf16[1,128,1024]{2,1,0:T(8,128)(2,1)S(1)} %get-tuple-element.77), channel_id=1, source_target_pairs={{0,28},{4,0},{8,4},{12,8},{16,12},{20,16},{24,20},{28,24},{1,29},{... | collective-permute-start | bytes 786440 | tf_op jit(solution)/shard_map/ppermute | solution.py:418
  74.8 1.9 %inner.1 = (f32[512,1024]{1,0:T(8,128)S(1)}, f32[512,1024]{1,0:T(8,128)S(1)}) custom-call(bf16[8,512,512]{2,1,0:T(8,128)(2,1)S(1)} %get-tuple-element.71.z_ref, bf16[8,512,512]{2,1,0:T(8,128)(2,1)S(1)} %get-tuple-element.72.p_ref, bf16[512,1024]{1,0:T(8,128)(2,1)S(1)} %get-tuple-element.64.q_ref, bf16[512,1024]{1,0:T(8,128)(2,1)S(1)} %get-tuple-element.69.g_ref), custom_call_target="tpu_custom_call" | custom-call | flops 5500000256 | bytes 1000000 | tf_op jit(solution)/shard_map/inner/pallas_call | solution.py:68
  76.7 0.7 collective-permute-done.9.near_ref
  77.4 1.8 %grad_kv.1 = (bf16[512,1024]{1,0:T(8,128)(2,1)S(1)}, bf16[512,1024]{1,0:T(8,128)(2,1)S(1)}, bf16[2,128,1024]{2,1,0:T(8,128)(2,1)S(1)}, bf16[2,128,1024]{2,1,0:T(8,128)(2,1)S(1)}) custom-call(s32[1,512]{1,0:T(1,128)S(1)} %bitcast.6, bf16[8,144,128]{2,1,0:T(8,128)(2,1)S(1)} %collective-permute-done.9.near_ref, ...), custom_call_target="tpu_custom_call" | custom-call | flops 32999999488 | bytes 1000000 | tf_op jit(solution)/shard_map/grad_kv/pallas_call | solution.py:68
  79.8 4.8 %collective-permute-start.14 = (bf16[2,128,1024]{2,1,0:T(8,128)(2,1)S(1)}, bf16[2,128,1024]{2,1,0:T(8,128)(2,1)S(1)}, u32[]{:S(2)}, u32[]{:S(2)}) collective-permute-start(bf16[2,128,1024]{2,1,0:T(8,128)(2,1)S(1)} %get-tuple-element.81), channel_id=1, source_target_pairs={{0,28},{4,0},{8,4},{12,8},{16,12},{20,16},{24,20},{28,24},{1,29},{... | collective-permute-start | bytes 1572872 | tf_op jit(solution)/shard_map/ppermute | solution.py:418
  84.6 0.7 own_q.1.refs_0_
  85.3 1.3 %normed.1 = bf16[512,1024]{1,0:T(8,128)(2,1)} custom-call(f32[512,1024]{1,0:T(8,128)S(1)} %get-tuple-element.65.u_ref, f32[512,128]{1,0:T(8,128)S(1)} %get-tuple-element.67.inverse_ref, bf16[512,1024]{1,0:T(8,128)(2,1)S(1)} %get-tuple-element.75._.refs_1_.refs_0_), custom_call_target="tpu_custom_call" | custom-call | flops 2200000000 | bytes 1000000 | tf_op jit(solution)/shard_map/normed/pallas_call | solution.py:68
  86.7 11.0 %collective-permute-done.11.left_ref = bf16[1,128,1024]{2,1,0:T(8,128)(2,1)S(1)} collective-permute-done((bf16[1,128,1024]{2,1,0:T(8,128)(2,1)S(1)}, bf16[1,128,1024]{2,1,0:T(8,128)(2,1)S(1)}, u32[]{:S(2)}, u32[]{:S(2)}) %collective-permute-start.11) | collective-permute-done | bytes 262176 | tf_op jit(solution)/shard_map/ppermute | solution.py:418
  97.7 1.4 %finish_q.1 = (bf16[512,1024]{1,0:T(8,128)(2,1)}, bf16[16,128]{1,0:T(8,128)(2,1)S(1)}) custom-call(s32[2,128]{1,0:T(2,128)S(1)} %bitcast.10, bf16[1,128,1024]{2,1,0:T(8,128)(2,1)S(1)} %collective-permute-done.11.left_ref, bf16[1,128,1024]{2,1,0:T(8,128)(2,1)S(1)} %collective-permute-done.12.right_ref, bf16[512,1024]{1,0:T(8,128)(2,1)S(1)} %own_q.1.refs_0_), custom_call_target="tpu_custom_call" | custom-call | flops 2200000000 | bytes 1000000 | tf_op jit(solution)/shard_map/finish_q/pallas_call | solution.py:68
  99.1 1.2 %own_kv.1 = (bf16[512,1024]{1,0:T(8,128)(2,1)S(1)}, bf16[512,1024]{1,0:T(8,128)(2,1)S(1)}) custom-call(s32[1,512]{1,0:T(1,128)S(1)} %bitcast.8, bf16[512,1024]{1,0:T(8,128)(2,1)S(1)} %get-tuple-element.75._.refs_1_.refs_0_, bf16[512,1024]{1,0:T(8,128)(2,1)S(1)} %get-tuple-element.82.refs_1_, bf16[16,128]{1,0:T(8,128)(2,1)S(1)} %get-tuple-element.83.refs_2_), custom_call_target="tpu_custom_call" | custom-call | flops 2200000000 | bytes 1000000 | tf_op jit(solution)/shard_map/own_kv/pallas_call | solution.py:68
  100.3 8.5 %collective-permute-done.13.left_ref = bf16[2,128,1024]{2,1,0:T(8,128)(2,1)S(1)} collective-permute-done((bf16[2,128,1024]{2,1,0:T(8,128)(2,1)S(1)}, bf16[2,128,1024]{2,1,0:T(8,128)(2,1)S(1)}, u32[]{:S(2)}, u32[]{:S(2)}) %collective-permute-start.13) | collective-permute-done | bytes 524320 | tf_op jit(solution)/shard_map/ppermute | solution.py:418
  108.8 1.8 %finish_kv.1 = (bf16[512,1024]{1,0:T(8,128)(2,1)}, bf16[512,1024]{1,0:T(8,128)(2,1)}) custom-call(s32[2,128]{1,0:T(2,128)S(1)} %bitcast.11, bf16[2,128,1024]{2,1,0:T(8,128)(2,1)S(1)} %collective-permute-done.13.left_ref, bf16[2,128,1024]{2,1,0:T(8,128)(2,1)S(1)} %collective-permute-done.14.right_ref, bf16[512,1024]{1,0:T(8,128)(2,1)S(1)} %get-tuple-element.84.refs_0_, ...), custom_call_target="tpu_custom_call" | custom-call | flops 2200000000 | bytes 1000000 | tf_op jit(solution)/shard_map/finish_kv/pallas_call | solution.py:68
  (31 shorter events, 2.3 us)
Async XLA Ops:
  0.6 9.7 %copy-start = (bf16[512,1024]{1,0:T(8,128)(2,1)S(1)}, bf16[512,1024]{1,0:T(8,128)(2,1)}, u32[]{:S(2)}) copy-start(bf16[512,1024]{1,0:T(8,128)(2,1)} %k_ref.1) | copy-start | bytes 3145732
  0.6 9.7 %copy-start.1 = (bf16[512,1024]{1,0:T(8,128)(2,1)S(1)}, bf16[512,1024]{1,0:T(8,128)(2,1)}, u32[]{:S(2)}) copy-start(bf16[512,1024]{1,0:T(8,128)(2,1)} %v_ref.1) | copy-start | bytes 3145732
  0.7 9.7 %copy-start.2 = (bf16[512,1024]{1,0:T(8,128)(2,1)S(1)}, bf16[512,1024]{1,0:T(8,128)(2,1)}, u32[]{:S(2)}) copy-start(bf16[512,1024]{1,0:T(8,128)(2,1)} %q_ref.1) | copy-start | bytes 3145732
  0.7 9.7 %copy-start.4 = (f32[512,8]{0,1:T(8,128)S(1)}, f32[512,8]{0,1:T(8,128)}, u32[]{:S(2)}) copy-start(f32[512,8]{0,1:T(8,128)} %param.12) | copy-start | bytes 49156
  0.7 9.7 %copy-start.5 = (s32[512]{0:T(512)S(1)}, s32[512]{0:T(512)}, u32[]{:S(2)}) copy-start(s32[512]{0:T(512)} %param.15) | copy-start | bytes 6148
  0.7 9.7 %copy-start.7 = (s32[8]{0:T(128)S(1)}, s32[8]{0:T(128)}, u32[]{:S(2)}) copy-start(s32[8]{0:T(128)} %docs_ref.1) | copy-start | bytes 100
  4.2 32.2 %collective-permute-start.2 = (bf16[2,128,1024]{2,1,0:T(8,128)(2,1)S(1)}, bf16[2,128,1024]{2,1,0:T(8,128)(2,1)S(1)}, u32[]{:S(2)}, u32[]{:S(2)}) collective-permute-start(bf16[2,128,1024]{2,1,0:T(8,128)(2,1)S(1)} %get-tuple-element.51), channel_id=1, source_target_pairs={{0,4},{4,8},{8,12},{12,16},{16,20},{20,24},{24,28},{28,0},{1,5},{5... | collective-permute-start | bytes 1572872 | tf_op jit(solution)/shard_map/ppermute | solution.py:418
  7.2 31.7 %collective-permute-start.3 = (bf16[2,128,1024]{2,1,0:T(8,128)(2,1)S(1)}, bf16[2,128,1024]{2,1,0:T(8,128)(2,1)S(1)}, u32[]{:S(2)}, u32[]{:S(2)}) collective-permute-start(bf16[2,128,1024]{2,1,0:T(8,128)(2,1)S(1)} %get-tuple-element.52), channel_id=1, source_target_pairs={{0,28},{4,0},{8,4},{12,8},{16,12},{20,16},{24,20},{28,24},{1,29},{... | collective-permute-start | bytes 1572872 | tf_op jit(solution)/shard_map/ppermute | solution.py:418
  15.3 26.9 %collective-permute-start = (bf16[1,128,1024]{2,1,0:T(8,128)(2,1)S(1)}, bf16[1,128,1024]{2,1,0:T(8,128)(2,1)S(1)}, u32[]{:S(2)}, u32[]{:S(2)}) collective-permute-start(bf16[1,128,1024]{2,1,0:T(8,128)(2,1)S(1)} %get-tuple-element.48), channel_id=1, source_target_pairs={{0,4},{4,8},{8,12},{12,16},{16,20},{20,24},{24,28},{28,0},{1,5},{5... | collective-permute-start | bytes 786440 | tf_op jit(solution)/shard_map/ppermute | solution.py:418
  15.4 30.9 %collective-permute-start.1 = (bf16[1,128,1024]{2,1,0:T(8,128)(2,1)S(1)}, bf16[1,128,1024]{2,1,0:T(8,128)(2,1)S(1)}, u32[]{:S(2)}, u32[]{:S(2)}) collective-permute-start(bf16[1,128,1024]{2,1,0:T(8,128)(2,1)S(1)} %get-tuple-element.49), channel_id=1, source_target_pairs={{0,28},{4,0},{8,4},{12,8},{16,12},{20,16},{24,20},{28,24},{1,29},{... | collective-permute-start | bytes 786440 | tf_op jit(solution)/shard_map/ppermute | solution.py:418
  39.9 12.0 %collective-permute-start.4 = (bf16[8,144,128]{2,1,0:T(8,128)(2,1)S(1)}, bf16[8,144,128]{2,1,0:T(8,128)(2,1)S(1)}, u32[]{:S(2)}, u32[]{:S(2)}) collective-permute-start(bf16[8,144,128]{2,1,0:T(8,128)(2,1)S(1)} %state.1._), channel_id=1, source_target_pairs={{0,4},{4,8},{8,12},{12,16},{16,20},{20,24},{24,28},{28,0},{1,5},{5... | collective-permute-start | bytes 884744 | tf_op jit(solution)/shard_map/ppermute | solution.py:418
  39.9 12.0 %collective-permute-start.5 = (bf16[8,144,128]{2,1,0:T(8,128)(2,1)S(1)}, bf16[8,144,128]{2,1,0:T(8,128)(2,1)S(1)}, u32[]{:S(2)}, u32[]{:S(2)}) collective-permute-start(bf16[8,144,128]{2,1,0:T(8,128)(2,1)S(1)} %state.1._), channel_id=1, source_target_pairs={{0,8},{4,12},{8,16},{12,20},{16,24},{20,28},{24,0},{28,4},{1,9},{5... | collective-permute-start | bytes 884744 | tf_op jit(solution)/shard_map/ppermute | solution.py:418
  46.2 5.7 %copy-start.3 = (bf16[512,1024]{1,0:T(8,128)(2,1)S(1)}, bf16[512,1024]{1,0:T(8,128)(2,1)}, u32[]{:S(2)}) copy-start(bf16[512,1024]{1,0:T(8,128)(2,1)} %ct_ref.3) | copy-start | bytes 3145732
  46.2 5.7 %copy-start.8 = (f32[8]{0:T(128)S(1)}, f32[8]{0:T(128)}, u32[]{:S(2)}) copy-start(f32[8]{0:T(128)} %scale_ref.3) | copy-start | bytes 100
  53.6 3.1 %collective-permute-start.6 = (f32[2,512]{1,0:T(2,128)S(1)}, f32[2,512]{1,0:T(2,128)S(1)}, u32[]{:S(2)}, u32[]{:S(2)}) collective-permute-start(f32[2,512]{1,0:T(2,128)S(1)} %get-tuple-element.66.refs_0_), channel_id=1, source_target_pairs={{0,1},{1,2},{2,3},{3,0},{4,5},{5,6},{6,7},{7,4},{8,9},{9,10},{10,1... | collective-permute-start | bytes 12296 | tf_op jit(solution)/shard_map/ppermute | solution.py:428
  53.7 3.7 %collective-permute-start.7 = (f32[2,512]{1,0:T(2,128)S(1)}, f32[2,512]{1,0:T(2,128)S(1)}, u32[]{:S(2)}, u32[]{:S(2)}) collective-permute-start(f32[2,512]{1,0:T(2,128)S(1)} %get-tuple-element.66.refs_0_), channel_id=1, source_target_pairs={{0,2},{1,3},{2,0},{3,1},{4,6},{5,7},{6,4},{7,5},{8,10},{9,11},{10,... | collective-permute-start | bytes 12296 | tf_op jit(solution)/shard_map/ppermute | solution.py:428
  55.3 2.7 %collective-permute-start.8 = (f32[2,512]{1,0:T(2,128)S(1)}, f32[2,512]{1,0:T(2,128)S(1)}, u32[]{:S(2)}, u32[]{:S(2)}) collective-permute-start(f32[2,512]{1,0:T(2,128)S(1)} %get-tuple-element.66.refs_0_), channel_id=1, source_target_pairs={{0,3},{1,0},{2,1},{3,2},{4,7},{5,4},{6,5},{7,6},{8,11},{9,8},{10,9... | collective-permute-start | bytes 12296 | tf_op jit(solution)/shard_map/ppermute | solution.py:428
  60.2 16.5 %collective-permute-start.10 = (bf16[8,144,128]{2,1,0:T(8,128)(2,1)S(1)}, bf16[8,144,128]{2,1,0:T(8,128)(2,1)S(1)}, u32[]{:S(2)}, u32[]{:S(2)}) collective-permute-start(bf16[8,144,128]{2,1,0:T(8,128)(2,1)S(1)} %get-tuple-element.68), channel_id=1, source_target_pairs={{0,24},{4,28},{8,0},{12,4},{16,8},{20,12},{24,16},{28,20},{1,25},{... | collective-permute-start | bytes 884744 | tf_op jit(solution)/shard_map/ppermute | solution.py:418
  63.8 13.6 %collective-permute-start.9 = (bf16[8,144,128]{2,1,0:T(8,128)(2,1)S(1)}, bf16[8,144,128]{2,1,0:T(8,128)(2,1)S(1)}, u32[]{:S(2)}, u32[]{:S(2)}) collective-permute-start(bf16[8,144,128]{2,1,0:T(8,128)(2,1)S(1)} %get-tuple-element.68), channel_id=1, source_target_pairs={{0,28},{4,0},{8,4},{12,8},{16,12},{20,16},{24,20},{28,24},{1,29},{... | collective-permute-start | bytes 884744 | tf_op jit(solution)/shard_map/ppermute | solution.py:418
  70.1 27.6 %collective-permute-start.11 = (bf16[1,128,1024]{2,1,0:T(8,128)(2,1)S(1)}, bf16[1,128,1024]{2,1,0:T(8,128)(2,1)S(1)}, u32[]{:S(2)}, u32[]{:S(2)}) collective-permute-start(bf16[1,128,1024]{2,1,0:T(8,128)(2,1)S(1)} %get-tuple-element.76), channel_id=1, source_target_pairs={{0,4},{4,8},{8,12},{12,16},{16,20},{20,24},{24,28},{28,0},{1,5},{5... | collective-permute-start | bytes 786440 | tf_op jit(solution)/shard_map/ppermute | solution.py:418
  70.2 27.4 %collective-permute-start.12 = (bf16[1,128,1024]{2,1,0:T(8,128)(2,1)S(1)}, bf16[1,128,1024]{2,1,0:T(8,128)(2,1)S(1)}, u32[]{:S(2)}, u32[]{:S(2)}) collective-permute-start(bf16[1,128,1024]{2,1,0:T(8,128)(2,1)S(1)} %get-tuple-element.77), channel_id=1, source_target_pairs={{0,28},{4,0},{8,4},{12,8},{16,12},{20,16},{24,20},{28,24},{1,29},{... | collective-permute-start | bytes 786440 | tf_op jit(solution)/shard_map/ppermute | solution.py:418
  79.2 29.6 %collective-permute-start.13 = (bf16[2,128,1024]{2,1,0:T(8,128)(2,1)S(1)}, bf16[2,128,1024]{2,1,0:T(8,128)(2,1)S(1)}, u32[]{:S(2)}, u32[]{:S(2)}) collective-permute-start(bf16[2,128,1024]{2,1,0:T(8,128)(2,1)S(1)} %get-tuple-element.80), channel_id=1, source_target_pairs={{0,4},{4,8},{8,12},{12,16},{16,20},{20,24},{24,28},{28,0},{1,5},{5... | collective-permute-start | bytes 1572872 | tf_op jit(solution)/shard_map/ppermute | solution.py:418
  79.8 29.0 %collective-permute-start.14 = (bf16[2,128,1024]{2,1,0:T(8,128)(2,1)S(1)}, bf16[2,128,1024]{2,1,0:T(8,128)(2,1)S(1)}, u32[]{:S(2)}, u32[]{:S(2)}) collective-permute-start(bf16[2,128,1024]{2,1,0:T(8,128)(2,1)S(1)} %get-tuple-element.81), channel_id=1, source_target_pairs={{0,28},{4,0},{8,4},{12,8},{16,12},{20,16},{24,20},{28,24},{1,29},{... | collective-permute-start | bytes 1572872 | tf_op jit(solution)/shard_map/ppermute | solution.py:418
  85.3 12.3 %copy-start.6 = (s32[1,2,128]{2,1,0:T(2,128)S(1)}, s32[1,2,128]{2,1,0:T(2,128)}, u32[]{:S(2)}) copy-start(s32[1,2,128]{2,1,0:T(2,128)} %param.14) | copy-start | bytes 3076

commit v2 on v1

--- a/solution.py
+++ b/solution.py
@@ -90,10 +90,9 @@
     named_copy.start()
     copies = []
     for source, target in ((k_hbm, k_ref), (v_hbm, v_ref)):
-        for part in chunks(features):
-            copy = pltpu.make_async_copy(
-                source.at[:, part], target.at[:, part], sem.at[1 + len(copies)]
-            )
+        for start in range(0, rows, 128):
+            part = slice(start, start + 128)
+            copy = pltpu.make_async_copy(source.at[part], target.at[part], sem.at[1 + len(copies)])
             copy.start()
             copies.append(copy)
     named_copy.wait()
@@ -104,10 +103,10 @@
             hot_ref[side * capacity : (side + 1) * capacity, start : start + 128] = one_hot(
                 named == lane + start
             )
-    parts = chunks(features)
     for index, target in enumerate((k_ref, v_ref)):
-        for number, part in enumerate(parts):
-            copies[index * len(parts) + number].wait()
+        for copy in copies[index * len(copies) // 2 : (index + 1) * len(copies) // 2]:
+            copy.wait()
+        for part in chunks(features):
             picked = dot(hot_ref[...], target[:, part]).astype(BF)
             left_ref[index, :, part] = picked[:capacity]
             right_ref[index, :, part] = picked[capacity:]
@@ -127,7 +126,7 @@
             pltpu.VMEM((2, capacity), jnp.int32),
             pltpu.VMEM((rows, features), BF),
             pltpu.VMEM((rows, features), BF),
-            pltpu.SemaphoreType.DMA((1 + 2 * len(chunks(features)),)),
+            pltpu.SemaphoreType.DMA((1 + 2 * (rows // 128),)),
         ),
         spaces=(pl.ANY, pl.ANY, pl.ANY),
     )
@@ -136,7 +135,7 @@
 def prep_kernel(
     docs_ref, take_ref, log_ref, named_ref, q_ref, k_ref, v_ref,
     left_ref, right_ref, qo_ref, ko_ref, vo_ref, hot_ref,
-    mask_ref, cols_ref, rows_ref, through_ref, state_ref, leave_ref, own_ref,
+    mask_ref, cols_ref, rows_ref, facts_ref, state_ref, leave_ref, own_ref,
 ):
     rows, features = q_ref.shape
     heads = log_ref.shape[0]
@@ -179,14 +178,6 @@
     entering = jnp.where(keep_e, jnp.exp2(running + scale), 0.0)
     through = jnp.where(opens == 0, jnp.exp2(final), 0.0)
     cols_ref[0], cols_ref[1], cols_ref[2] = leaving, entering, running
-    parts = [x.astype(F32) for x in pieces(through)]
-    line = iota((16, 128), 0)
-    for h in range(heads):
-        high, middle, low = [jnp.broadcast_to(x[:, h : h + 1], (16, 128)) for x in parts]
-        through_ref[h] = jnp.where(
-            line == 0, high, jnp.where(line == 1, middle, jnp.where(line == 2, low, 0.0))
-        ).astype(BF)
-
     lane = iota((rows, 128), 1)
     taken = along_rows(take_ref[...])
     for start_row in range(0, rows, 128):
@@ -194,6 +185,8 @@
     hot_ref[:, :capacity] = one_hot(taken == lane)
     hot_ref[:, capacity:] = one_hot(taken - (capacity + rows) == lane)
     leave_ref[...] = sum(dot_tn(hot_ref[...], piece) for piece in pieces(leaving))
+    facts_ref[:heads] = leave_ref[capacity:, :].T[:heads]
+    facts_ref[heads:] = along_rows(through, capacity)[:heads]
     for part in chunks(features):
         for source, target in ((k_ref, ko_ref), (v_ref, vo_ref), (q_ref, qo_ref)):
             target[:, part] = dot(own_ref[...], source[:, part]).astype(BF)
@@ -218,7 +211,7 @@
             sds((rows, rows), F32),
             sds((3, rows, 128), F32),
             sds((heads, rows), F32),
-            sds((heads, 16, 128)),
+            sds((2 * heads, capacity), F32),
             sds((heads, width, width), F32),
             sds((2 * capacity, 128), F32),
         ],
@@ -228,14 +221,13 @@
     )
 
 
-def state_kernel(left_ref, right_ref, leave_ref, own_ref, through_ref, message_ref):
+def state_kernel(left_ref, right_ref, leave_ref, own_ref, message_ref):
     heads, width = own_ref.shape[:2]
     for h, part in enumerate(head_slices(heads * width, heads)):
         k = jnp.concatenate([left_ref[0, :, part], right_ref[0, :, part]], axis=0)
         v = jnp.concatenate([left_ref[1, :, part], right_ref[1, :, part]], axis=0)
         kf = (k.astype(F32) * leave_ref[:, h : h + 1]).astype(BF)
-        message_ref[h, :width, :] = (own_ref[h] + dot_tn(kf, v)).astype(BF)
-        message_ref[h, width:, :] = through_ref[h]
+        message_ref[h] = (own_ref[h] + dot_tn(kf, v)).astype(BF)
 
 
 def assemble(hot_ref, left_ref, right_ref, index, own_rows, target):
@@ -244,7 +236,7 @@
         target[:, part] = own_rows[:, part] + dot(hot_ref[...], extra).astype(BF)
 
 
-def assemble_kernel(hot_ref, left_ref, right_ref, ko_ref, vo_ref, _, k_ref, v_ref):
+def assemble_kernel(hot_ref, left_ref, right_ref, ko_ref, vo_ref, _, _before, _after, k_ref, v_ref):
     assemble(hot_ref, left_ref, right_ref, 0, ko_ref, k_ref)
     assemble(hot_ref, left_ref, right_ref, 1, vo_ref, v_ref)
 
@@ -255,7 +247,7 @@
     return jnp.exp2((column - row) + mask_ref[top : top + half, :reach])
 
 
-def inside_kernel(hot_ref, left_ref, right_ref, qo_ref, k_ref, v_ref, mask_ref, cols_ref, rows_ref, q_ref, p_ref, o_ref):
+def inside_kernel(hot_ref, left_ref, right_ref, qo_ref, k_ref, v_ref, mask_ref, cols_ref, rows_ref, q_ref, qe_ref, weight_ref, p_ref, o_ref):
     rows, features = k_ref.shape
     assemble(hot_ref, left_ref, right_ref, 0, qo_ref, q_ref)
     heads, half = p_ref.shape[0], rows // 2
@@ -265,9 +257,12 @@
             here = slice(top, top + half)
             scores = dot_nt(q_ref[here, part], k_ref[:reach, part])
             weight = decay(mask_ref, cols_ref, rows_ref, h, top, half, reach)
+            weight_ref[h, here, :reach] = weight
             p = (scores * weight).astype(BF)
             p_ref[h, here, :reach] = p
             o_ref[here, part] = dot(p, v_ref[:reach, part])
+        qe = (q_ref[:, part].astype(F32) * cols_ref[1, :, h : h + 1]).astype(BF)
+        qe_ref[h] = qe.T
 
 
 def shards_before(direction):
@@ -275,22 +270,30 @@
     return index if direction > 0 else lax.axis_size("seq") - 1 - index
 
 
-def joined(before, near_ref, far_ref, h, width):
-    through = jnp.sum(near_ref[h, width:, :].astype(F32), axis=0, keepdims=True)
-    near = near_ref[h, :width, :].astype(F32)
-    far = through * far_ref[h, :width, :].astype(F32)
+def decayed(facts_ref, h, state):
+    heads, width = facts_ref.shape[0] // 2, state.shape[1]
+    return facts_ref[heads + h : heads + h + 1, :width] * state
+
+
+def carried_sum(before, facts_ref, near_ref, far_ref, h):
+    near = near_ref[h].astype(F32)
+    far = decayed(facts_ref, h, far_ref[h].astype(F32))
     near = jnp.where(before >= 1, near, 0.0)
-    return (near + jnp.where(before >= 2, far, 0.0)).astype(BF)
-
-
-def output_kernel(scale_ref, o_ref, q_ref, near_ref, far_ref, cols_ref, ct_ref, u_ref, h_ref, sums_ref):
+    return near + jnp.where(before >= 2, far, 0.0)
+
+
+def joined(before, facts_ref, near_ref, far_ref, h):
+    return carried_sum(before, facts_ref, near_ref, far_ref, h).astype(BF)
+
+
+def output_kernel(scale_ref, o_ref, q_ref, facts_ref, near_ref, far_ref, cols_ref, ct_ref, u_ref, h_ref, sums_ref):
     rows, features = q_ref.shape
     heads, width = h_ref.shape[:2]
     before = shards_before(1)
     squares = jnp.zeros((rows, width), F32)
     cross = jnp.zeros((rows, width), F32)
     for h, part in enumerate(head_slices(features, heads)):
-        carried_in = joined(before, near_ref, far_ref, h, width)
+        carried_in = joined(before, facts_ref, near_ref, far_ref, h)
         h_ref[h] = carried_in
         outer = dot(q_ref[:, part], carried_in) * cols_ref[1, :, h : h + 1]
         u = (o_ref[:, part] + outer) * scale_ref[h]
@@ -301,11 +304,10 @@
     sums_ref[1:2, :] = jnp.sum(cross.T, axis=0, keepdims=True)
 
 
-def norm_kernel(total, scale_ref, u_ref, ct_ref, q_ref, cols_ref, through_ref, *refs):
+def norm_kernel(total, scale_ref, u_ref, ct_ref, qe_ref, *refs):
     *sums, g_ref, message_ref, inverse_ref = refs
-    rows, features = q_ref.shape
-    heads = through_ref.shape[0]
-    width = features // heads
+    features = u_ref.shape[1]
+    heads, width = qe_ref.shape[:2]
     summed = sums[0][...]
     for more in sums[1:]:
         summed += more[...]
@@ -316,9 +318,7 @@
         g = (inverse * ct_ref[:, part].astype(F32) - u_ref[:, part] * mean) * scale_ref[h]
         g = g.astype(BF)
         g_ref[:, part] = g
-        qe = (q_ref[:, part].astype(F32) * cols_ref[1, :, h : h + 1]).astype(BF)
-        message_ref[h, :width, :] = dot_tn(qe, g).astype(BF)
-        message_ref[h, width:, :] = through_ref[h]
+        message_ref[h] = dot(qe_ref[h], g).astype(BF)
 
 
 def normed_kernel(u_ref, inverse_ref, _, normed_ref):
@@ -345,7 +345,7 @@
     )
 
 
-def grad_q_kernel(take_ref, g_ref, k_ref, v_ref, h_ref, mask_ref, cols_ref, rows_ref, dq_ref, z_ref, left_ref, right_ref):
+def grad_q_kernel(take_ref, g_ref, k_ref, v_ref, h_ref, weight_ref, cols_ref, dq_ref, z_ref, left_ref, right_ref):
     rows, features = k_ref.shape
     heads, half = h_ref.shape[0], rows // 2
     for h, part in enumerate(head_slices(features, heads)):
@@ -353,8 +353,7 @@
             top, reach = i * half, (i + 1) * half
             here = slice(top, top + half)
             g = g_ref[here, part]
-            weight = decay(mask_ref, cols_ref, rows_ref, h, top, half, reach)
-            z = (dot_nt(g, v_ref[:reach, part]) * weight).astype(BF)
+            z = (dot_nt(g, v_ref[:reach, part]) * weight_ref[h, here, :reach]).astype(BF)
             z_ref[h, here, :reach] = z
             outer = dot_nt(g, h_ref[h]) * cols_ref[1, here, h : h + 1]
             dq_ref[here, part] = (dot(z, k_ref[:reach, part]) + outer).astype(BF)
@@ -371,18 +370,39 @@
                 target[here, part] = dot_tn(square[h, j * half :, here], source[j * half :, part])
 
 
-def grad_kv_kernel(take_ref, near_ref, far_ref, k_ref, v_ref, cols_ref, dki_ref, dvi_ref, dk_ref, dv_ref, left_ref, right_ref):
+def right_kernel(take_ref, dk_ref, dv_ref, _, right_ref):
+    capacity, features = right_ref.shape[1:]
+    hot = slots_hot(take_ref, capacity)[capacity:]
+    for index, source in enumerate((dk_ref, dv_ref)):
+        for part in chunks(features):
+            right_ref[index, :, part] = dot(hot, source[:, part].astype(BF)).astype(BF)
+
+
+def grad_kv_kernel(take_ref, far_ref, near_ref, facts_ref, k_ref, v_ref, cols_ref, dki_ref, dvi_ref, dk_ref, dv_ref, left_ref):
     rows, features = k_ref.shape
     heads = near_ref.shape[0]
     before = shards_before(-1)
     for h, part in enumerate(head_slices(features, heads)):
-        state_grad = joined(before, near_ref, far_ref, h, features // heads)
+        state_grad = joined(before, facts_ref, near_ref, far_ref, h)
         leaving = cols_ref[0, :, h : h + 1]
         dk_ref[:, part] = (dki_ref[:, part] + leaving * dot_nt(v_ref[:, part], state_grad)).astype(BF)
         dv_ref[:, part] = (dvi_ref[:, part] + leaving * dot(k_ref[:, part], state_grad)).astype(BF)
-    hot = slots_hot(take_ref, left_ref.shape[1])
-    send_back(hot, dk_ref, left_ref, right_ref, 0)
-    send_back(hot, dv_ref, left_ref, right_ref, 1)
+    hot = slots_hot(take_ref, left_ref.shape[1])[: left_ref.shape[1]]
+    for index, source in enumerate((dk_ref, dv_ref)):
+        for part in chunks(features):
+            left_ref[index, :, part] = dot(hot, source[:, part]).astype(BF)
+
+
+def lend_kernel(facts_ref, after_ref, near_ref, far_ref, message_ref, lent_ref, rows_ref, _, dk_ref, dv_ref):
+    features = dk_ref.shape[1]
+    heads, width = message_ref.shape[:2]
+    before = shards_before(-1)
+    for h, part in enumerate(head_slices(features, heads)):
+        after = carried_sum(before, after_ref, near_ref, far_ref, h)
+        state_grad = (message_ref[h].astype(F32) + decayed(facts_ref, h, after)).astype(BF)
+        leaving = along_rows(lent_ref[h : h + 1, :], width)
+        dk_ref[:, part] = leaving * dot_nt(rows_ref[1, :, part], state_grad)
+        dv_ref[:, part] = leaving * dot(rows_ref[0, :, part], state_grad)
 
 
 def own_kernel(capacity, count, take_ref, *refs):
@@ -394,7 +414,8 @@
             target[:, part] = dot(hot, source[:, part]).astype(BF)
 
 
-def finish_kernel(count, send_ref, left_ref, right_ref, *refs):
+def finish_kernel(count, lending, send_ref, left_ref, right_ref, *refs):
+    lent, refs = refs[:lending], refs[lending:]
     rows = refs[0].shape[0]
     capacity = send_ref.shape[1]
     line = iota((rows, capacity), 0)
@@ -407,7 +428,10 @@
     )
     for index, (source, target) in enumerate(zip(refs[:count], refs[count : 2 * count])):
         for part in chunks(source.shape[1]):
-            back = jnp.concatenate([left_ref[index, :, part], right_ref[index, :, part]], axis=0)
+            left = left_ref[index, :, part]
+            if lending:
+                left = (left.astype(F32) + lent[index][:, part]).astype(BF)
+            back = jnp.concatenate([left, right_ref[index, :, part]], axis=0)
             target[:, part] = source[:, part] + dot(hot, back).astype(BF)
     for order in refs[2 * count :]:
         order[...] = jnp.zeros_like(order)
@@ -423,26 +447,36 @@
     return lax.ppermute(array, "seq", [(i, i + by) for i in range(peers) if 0 <= i + by < peers])
 
 
-def turned_by(array, by):
+def add_kernel(a_ref, b_ref, sum_ref):
+    sum_ref[...] = a_ref[...] + b_ref[...]
+
+
+def over_heads(sums):
     peers = lax.axis_size("head")
-    return lax.ppermute(array, "head", [(i, (i + by) % peers) for i in range(peers)])
-
-
-def carried(message, direction):
+    distance = 1
+    pair = (sums,)
+    while distance < peers:
+        if len(pair) == 2:
+            pair = local(add_kernel, "add", 1, [sds(sums.shape, F32)], pair)
+        pairs = [(i, i ^ distance) for i in range(peers)]
+        pair = (pair[0], lax.ppermute(pair[0], "head", pairs))
+        distance *= 2
+    return pair
+
+
+def carried(message, facts, direction):
     peers = lax.axis_size("seq")
     reach = peers // 4
     if reach <= 2:
         return shifted(message, direction), shifted(message, 2 * direction)
-    size = message.shape[2]
-    own_state = message[:, :size].astype(F32)
-    through = jnp.sum(message[:, size:, :1].astype(F32), axis=1, keepdims=True)
+    own_state = message.astype(F32)
+    through = facts[message.shape[0] :, :1, None]
 
     def relay(_, state_here):
         return shifted_open((through * state_here + own_state).astype(BF), direction).astype(F32)
 
     incoming = lax.fori_loop(0, reach, relay, jnp.zeros_like(own_state)).astype(BF)
-    near = jnp.concatenate([incoming, jnp.zeros_like(message[:, size:])], axis=1)
-    return near, jnp.zeros_like(message)
+    return incoming, jnp.zeros_like(message)
 
 
 def on_device(
@@ -458,31 +492,32 @@
     total = features * lax.axis_size("head")
     full, full32 = sds((rows, features)), sds((rows, features), F32)
     squares = sds((heads, rows, rows))
-    message_shape = sds((heads, width + 16, width))
+    message_shape = sds((heads, width, width))
     one_side, two_sides = sds((1, capacity, features)), sds((2, capacity, features))
 
     kv_left, kv_right, named = pick(send, key_vectors, value_vectors)
     kv_before, kv_after = shifted(kv_right, 1), shifted(kv_left, -1)
     (
-        q_left, q_right, q_own, k_own, v_own, hot, mask, cols, turned, through, state_own, leave
+        q_left, q_right, q_own, k_own, v_own, hot, mask, cols, turned, facts, state_own, leave
     ) = prep(doc_lengths, take, log_decay.T, named, queries, key_vectors, value_vectors)
     q_before, q_after = shifted(q_right, 1), shifted(q_left, -1)
     (message,) = local(
-        state_kernel, "state", 30, [message_shape], (kv_before, kv_after, leave, state_own, through)
-    )
-    near, far = carried(message, 1)
+        state_kernel, "state", 30, [message_shape], (kv_before, kv_after, leave, state_own)
+    )
+    near, far = carried(message, facts, 1)
+    facts_before, facts_after = shifted(facts, 1), shifted(facts, -1)
     k, v = local(
         assemble_kernel,
         "assemble",
         5,
         [full, full],
-        (hot, kv_before, kv_after, k_own, v_own, message),
-    )
-    q, probs, o_inside = local(
+        (hot, kv_before, kv_after, k_own, v_own, message, facts_before, facts_after),
+    )
+    q, qe, weight, probs, o_inside = local(
         inside_kernel,
         "inside",
         30,
-        [full, squares, full32],
+        [full, sds((heads, width, rows)), sds((heads, rows, rows), F32), squares, full32],
         (hot, q_before, q_after, q_own, k, v, mask, cols, turned),
     )
     u, state_low, sums = local(
@@ -490,42 +525,54 @@
         "output",
         3,
         [full32, sds((heads, width, width)), sds((2, rows), F32)],
-        (head_scale, o_inside, q, near, far, cols, cotangent),
+        (head_scale, o_inside, q, facts_before, near, far, cols, cotangent),
         scalars=1,
     )
-    others = [turned_by(sums, by) for by in range(1, lax.axis_size("head"))]
+    sums = over_heads(sums)
     g, grad_message, inverse = local(
         functools.partial(norm_kernel, total),
         "norm",
         4,
         [full, message_shape, sds((rows, width), F32)],
-        (head_scale, u, cotangent, q, cols, through, sums, *others),
+        (head_scale, u, cotangent, qe, *sums),
         scalars=1,
     )
-    grad_near, grad_far = carried(grad_message, -1)
+    grad_near, grad_far = carried(grad_message, facts, -1)
     dq, z, dq_left, dq_right = local(
         grad_q_kernel,
         "grad_q",
         30,
         [full, squares, one_side, one_side],
-        (take, g, k, v, state_low, mask, cols, turned),
+        (take, g, k, v, state_low, weight, cols),
     )
     dq_before, dq_after = shifted(dq_right, 1), shifted(dq_left, -1)
     dk_inner, dv_inner = local(inner_kernel, "inner", 5, [full32, full32], (z, probs, q, g))
-    dk, dv, dkv_left, dkv_right = local(
+    (dkv_right,) = local(
+        right_kernel, "right", 30, [two_sides], (take, dk_inner, dv_inner, grad_near)
+    )
+    dkv_before = shifted(dkv_right, 1)
+    dk, dv, dkv_left = local(
         grad_kv_kernel,
         "grad_kv",
-        30,
-        [full, full, two_sides, two_sides],
-        (take, grad_near, grad_far, k, v, cols, dk_inner, dv_inner),
-    )
-    dkv_before, dkv_after = shifted(dkv_right, 1), shifted(dkv_left, -1)
+        3,
+        [full, full, two_sides],
+        (take, grad_far, grad_near, facts_after, k, v, cols, dk_inner, dv_inner),
+    )
+    dkv_after = shifted(dkv_left, -1)
+    lent_rows = sds((capacity, features), F32)
+    dk_lent, dv_lent = local(
+        lend_kernel,
+        "lend",
+        2,
+        [lent_rows, lent_rows],
+        (facts, facts_after, grad_near, grad_far, grad_message, facts_before, kv_left, dk),
+    )
     (normed,) = local(normed_kernel, "normed", 2, [full], (u, inverse, dk))
     (dq_own,) = local(
         functools.partial(own_kernel, capacity, 1), "own_q", 2, [full], (take, dq, dk)
     )
     grad_queries, order = local(
-        functools.partial(finish_kernel, 1),
+        functools.partial(finish_kernel, 1, 0),
         "finish_q",
         2,
         [full, sds((16, 128))],
@@ -536,11 +583,11 @@
         (take, dk, dv, order),
     )
     grad_keys, grad_values = local(
-        functools.partial(finish_kernel, 2),
+        functools.partial(finish_kernel, 2, 2),
         "finish_kv",
         2,
         [full, full],
-        (send, dkv_before, dkv_after, dk_own, dv_own),
+        (send, dkv_before, dkv_after, dk_lent, dv_lent, dk_own, dv_own),
     )
     return normed, grad_queries, grad_keys, grad_values
 

time: 111 us -> 103 us (0.928)
  starting transfers between devices: 32.1 us -> 24.4 us
    ppermute x12 -> x14, starting transfers between devices: 29.1 us -> 22.8 us  [shifted(): lax.ppermute(array, 'seq', [(i, (i + by) % peers) for i in range(peers)])]
    ppermute x3 -> x2, waiting for transfers between devices: 1.33 us -> 3.27 us  [over_heads(): pair = (pair[0], lax.ppermute(pair[0], 'head', pairs))]
    ppermute x3 -> x2, starting transfers between devices: 3 us -> 1.56 us  [over_heads(): pair = (pair[0], lax.ppermute(pair[0], 'head', pairs))]
    ppermute x12 -> x14, waiting for transfers between devices: 46.1 us -> 45.2 us  [shifted(): lax.ppermute(array, 'seq', [(i, (i + by) % peers) for i in range(peers)])]
    pallas_call x15 -> x18, Pallas kernels: 30.2 us -> 29.4 us  [local(): pl.pallas_call(kernel, in_specs=specs, out_specs=[vmem] * len(out_shape),...]
  transfers between devices with their start and end apart: 15 -> 16, of which waited for: 10 -> 12; matrix products, arithmetic and copies ran while one was open for 0% -> 0% of each run, Pallas kernels for 19% -> 21%
where the time goes in v2:
time: 103 us
  waiting for transfers between devices  48.4 us (47%)
  Pallas kernels  29.4 us (29%)
  starting transfers between devices  24.4 us (24%)
    ppermute x14, waiting for transfers between devices, shifted(): lax.ppermute(array, 'seq', [(i, (i + by) % peers) for i in range(peers)])  45.2 us
    pallas_call x18, Pallas kernels, local(): pl.pallas_call(kernel, in_specs=specs, out_specs=[vmem] * len(out_shape),...  29.4 us
    ppermute x14, starting transfers between devices, shifted(): lax.ppermute(array, 'seq', [(i, (i + by) % peers) for i in range(peers)])  22.8 us
    ppermute x2, waiting for transfers between devices, over_heads(): pair = (pair[0], lax.ppermute(pair[0], 'head', pairs))  3.27 us
  transfers between devices with their start and end apart: 16, of which 12 were waited for; matrix products, arithmetic and copies ran while one was open for 0% of the time, Pallas kernels for 21%

profile of v2, /device:TPU:0, one launch (start us, length us, event | category | flops | bytes accessed | tf_op | source)
XLA Modules:
  0.0 103.2 jit_solution(3897659305017930462)
XLA Ops:
  0.7 2.3 %pick.1 = (bf16[2,128,1024]{2,1,0:T(8,128)(2,1)S(1)}, bf16[2,128,1024]{2,1,0:T(8,128)(2,1)S(1)}, bf16[256,512]{1,0:T(8,128)(2,1)S(1)}) custom-call(s32[2,128]{1,0:T(2,128)} %bitcast.10, bf16[512,1024]{1,0:T(8,128)(2,1)} %k_ref.1, bf16[512,1024]{1,0:T(8,128)(2,1)} %v_ref.1), custom_call_target="tpu_custom_call" | custom-call | flops 2200000000 | bytes 1000000 | tf_op jit(solution)/shard_map/pick/pallas_call | solution.py:68
  3.0 3.0 %collective-permute-start.2 = (bf16[2,128,1024]{2,1,0:T(8,128)(2,1)S(1)}, bf16[2,128,1024]{2,1,0:T(8,128)(2,1)S(1)}, u32[]{:S(2)}, u32[]{:S(2)}) collective-permute-start(bf16[2,128,1024]{2,1,0:T(8,128)(2,1)S(1)} %get-tuple-element.54), channel_id=1, source_target_pairs={{0,4},{4,8},{8,12},{12,16},{16,20},{20,24},{24,28},{28,0},{1,5},{5... | collective-permute-start | bytes 1572872 | tf_op jit(solution)/shard_map/ppermute | solution.py:442
  6.1 3.1 %collective-permute-start.3 = (bf16[2,128,1024]{2,1,0:T(8,128)(2,1)S(1)}, bf16[2,128,1024]{2,1,0:T(8,128)(2,1)S(1)}, u32[]{:S(2)}, u32[]{:S(2)}) collective-permute-start(bf16[2,128,1024]{2,1,0:T(8,128)(2,1)S(1)} %get-tuple-element.55.rows_ref), channel_id=1, source_target_pairs={{0,28},{4,0},{8,4},{12,8},{16,12},{20,16},{24,20},{28,24},{1,29},{... | collective-permute-start | bytes 1572872 | tf_op jit(solution)/shard_map/ppermute | solution.py:442
  9.2 4.9 %prep.1 = (bf16[1,128,1024]{2,1,0:T(8,128)(2,1)S(1)}, bf16[1,128,1024]{2,1,0:T(8,128)(2,1)S(1)}, bf16[512,1024]{1,0:T(8,128)(2,1)S(1)}, bf16[512,1024]{1,0:T(8,1...) custom-call(s32[8]{0:T(128)S(1)} %copy-done.9, ...), custom_call_target="tpu_custom_call" | custom-call | flops 32999999488 | bytes 1000000 | tf_op jit(solution)/shard_map/prep/pallas_call | solution.py:68
  14.1 2.0 %collective-permute-start.5 = (f32[16,128]{1,0:T(8,128)S(1)}, f32[16,128]{1,0:T(8,128)S(1)}, u32[]{:S(2)}, u32[]{:S(2)}) collective-permute-start(f32[16,128]{1,0:T(8,128)S(1)} %get-tuple-element.60.facts_ref), channel_id=1, source_target_pairs={{0,28},{4,0},{8,4},{12,8},{16,12},{20,16},{24,20},{28,24},{1,29},{... | collective-permute-start | bytes 24584 | tf_op jit(solution)/shard_map/ppermute | solution.py:442
  16.2 13.6 %collective-permute-done.2.left_ref = bf16[2,128,1024]{2,1,0:T(8,128)(2,1)S(1)} collective-permute-done((bf16[2,128,1024]{2,1,0:T(8,128)(2,1)S(1)}, bf16[2,128,1024]{2,1,0:T(8,128)(2,1)S(1)}, u32[]{:S(2)}, u32[]{:S(2)}) %collective-permute-start.2) | collective-permute-done | bytes 524320 | tf_op jit(solution)/shard_map/ppermute | solution.py:442
  29.8 5.5 %collective-permute-start.1 = (bf16[1,128,1024]{2,1,0:T(8,128)(2,1)S(1)}, bf16[1,128,1024]{2,1,0:T(8,128)(2,1)S(1)}, u32[]{:S(2)}, u32[]{:S(2)}) collective-permute-start(bf16[1,128,1024]{2,1,0:T(8,128)(2,1)S(1)} %get-tuple-element.52), channel_id=1, source_target_pairs={{0,28},{4,0},{8,4},{12,8},{16,12},{20,16},{24,20},{28,24},{1,29},{... | collective-permute-start | bytes 786440 | tf_op jit(solution)/shard_map/ppermute | solution.py:442
  35.3 2.6 %collective-permute-done.3.right_ref = bf16[2,128,1024]{2,1,0:T(8,128)(2,1)S(1)} collective-permute-done((bf16[2,128,1024]{2,1,0:T(8,128)(2,1)S(1)}, bf16[2,128,1024]{2,1,0:T(8,128)(2,1)S(1)}, u32[]{:S(2)}, u32[]{:S(2)}) %collective-permute-start.3) | collective-permute-done | bytes 524320 | tf_op jit(solution)/shard_map/ppermute | solution.py:442
  39.8 1.4 %collective-permute-done.left_ref = bf16[1,128,1024]{2,1,0:T(8,128)(2,1)S(1)} collective-permute-done((bf16[1,128,1024]{2,1,0:T(8,128)(2,1)S(1)}, bf16[1,128,1024]{2,1,0:T(8,128)(2,1)S(1)}, u32[]{:S(2)}, u32[]{:S(2)}) %collective-permute-start) | collective-permute-done | bytes 262176 | tf_op jit(solution)/shard_map/ppermute | solution.py:442
  41.2 1.0 %collective-permute-done.1.right_ref = bf16[1,128,1024]{2,1,0:T(8,128)(2,1)S(1)} collective-permute-done((bf16[1,128,1024]{2,1,0:T(8,128)(2,1)S(1)}, bf16[1,128,1024]{2,1,0:T(8,128)(2,1)S(1)}, u32[]{:S(2)}, u32[]{:S(2)}) %collective-permute-start.1) | collective-permute-done | bytes 262176 | tf_op jit(solution)/shard_map/ppermute | solution.py:442
  42.3 3.4 %inside.1 = (bf16[512,1024]{1,0:T(8,128)(2,1)S(1)}, bf16[8,128,512]{2,1,0:T(8,128)(2,1)S(1)}, f32[8,512,512]{2,1,0:T(8,128)S(1)}, bf16[8,512,512]{2,1,0:T(8,128)(2,1)S(1)}, f32[512,1024]{1,0:T(8,128)S(1)}) custom-call(bf16[512,256]{1,0:T(8,128)(2,1)S(1)} %get-tuple-element.50.hot_ref, bf16[1,128,1024]{2,1,0:T(8,128)(2,1)S(1)} %collective-permute-done.left_ref, ...), custom_call_target="tpu_custom_call" | custom-call | flops 32999999488 | bytes 1000000 | tf_op jit(solution)/shard_map/inside/pallas_call | solution.py:68
  45.6 1.6 %collective-permute-done.7.far_ref = bf16[8,128,128]{2,1,0:T(8,128)(2,1)S(1)} collective-permute-done((bf16[8,128,128]{2,1,0:T(8,128)(2,1)S(1)}, bf16[8,128,128]{2,1,0:T(8,128)(2,1)S(1)}, u32[]{:S(2)}, u32[]{:S(2)}) %collective-permute-start.7) | collective-permute-done | bytes 262176 | tf_op jit(solution)/shard_map/ppermute | solution.py:442
  47.2 4.6 %collective-permute-done.6.near_ref = bf16[8,128,128]{2,1,0:T(8,128)(2,1)S(1)} collective-permute-done((bf16[8,128,128]{2,1,0:T(8,128)(2,1)S(1)}, bf16[8,128,128]{2,1,0:T(8,128)(2,1)S(1)}, u32[]{:S(2)}, u32[]{:S(2)}) %collective-permute-start.6) | collective-permute-done | bytes 262176 | tf_op jit(solution)/shard_map/ppermute | solution.py:442
  51.8 1.7 %output.1 = (f32[512,1024]{1,0:T(8,128)S(1)}, bf16[8,128,128]{2,1,0:T(8,128)(2,1)S(1)}, f32[2,512]{1,0:T(2,128)S(1)}) custom-call(f32[8]{0:T(128)S(1)} %copy-done.10, f32[512,1024]{1,0:T(8,128)S(1)} %get-tuple-element.66.o_ref, bf16[512,1024]{1,0:T(8,128)(2,1)S(1)} %get-tuple-element.67.q_ref, ...), custom_call_target="tpu_custom_call" | custom-call | flops 3300000000 | bytes 1000000 | tf_op jit(solution)/shard_map/output/pallas_call | solution.py:68
  53.6 1.2 %collective-permute-done.8.b_ref = f32[2,512]{1,0:T(2,128)S(1)} collective-permute-done((f32[2,512]{1,0:T(2,128)S(1)}, f32[2,512]{1,0:T(2,128)S(1)}, u32[]{:S(2)}, u32[]{:S(2)}) %collective-permute-start.8) | collective-permute-done | bytes 4128 | tf_op jit(solution)/shard_map/ppermute | solution.py:462
  54.7 1.5 %collective-permute-start.9 = (f32[2,512]{1,0:T(2,128)S(1)}, f32[2,512]{1,0:T(2,128)S(1)}, u32[]{:S(2)}, u32[]{:S(2)}) collective-permute-start(f32[2,512]{1,0:T(2,128)S(1)} %add.1.refs_0_), channel_id=1, source_target_pairs={{0,2},{1,3},{2,0},{3,1},{4,6},{5,7},{6,4},{7,5},{8,10},{9,11},{10,... | collective-permute-start | bytes 12296 | tf_op jit(solution)/shard_map/ppermute | solution.py:462
  56.2 2.1 %collective-permute-done.9.refs_1_ = f32[2,512]{1,0:T(2,128)S(1)} collective-permute-done((f32[2,512]{1,0:T(2,128)S(1)}, f32[2,512]{1,0:T(2,128)S(1)}, u32[]{:S(2)}, u32[]{:S(2)}) %collective-permute-start.9) | collective-permute-done | bytes 4128 | tf_op jit(solution)/shard_map/ppermute | solution.py:462
  58.3 1.6 %norm.1 = (bf16[512,1024]{1,0:T(8,128)(2,1)S(1)}, bf16[8,128,128]{2,1,0:T(8,128)(2,1)S(1)}, f32[512,128]{1,0:T(8,128)S(1)}) custom-call(f32[8]{0:T(128)S(1)} %copy-done.10, f32[512,1024]{1,0:T(8,128)S(1)} %get-tuple-element.68.u_ref, bf16[512,1024]{1,0:T(8,128)(2,1)S(1)} %copy-done.3, bf16[8,128,512]{2,1,0:T(8,128)(2,1)S(1)} %get-tuple-element.69.qe_ref, ...), custom_call_target="tpu_custom_call" | custom-call | flops 4400000000 | bytes 1000000 | tf_op jit(solution)/shard_map/norm/pallas_call | solution.py:68
  60.0 2.0 %collective-permute-start.10 = (bf16[8,128,128]{2,1,0:T(8,128)(2,1)S(1)}, bf16[8,128,128]{2,1,0:T(8,128)(2,1)S(1)}, u32[]{:S(2)}, u32[]{:S(2)}) collective-permute-start(bf16[8,128,128]{2,1,0:T(8,128)(2,1)S(1)} %get-tuple-element.72.message_ref), channel_id=1, source_target_pairs={{0,24},{4,28},{8,0},{12,4},{16,8},{20,12},{24,16},{28,20},{1,25},{... | collective-permute-start | bytes 786440 | tf_op jit(solution)/shard_map/ppermute | solution.py:442
  62.0 3.1 %grad_q.1 = (bf16[512,1024]{1,0:T(8,128)(2,1)S(1)}, bf16[8,512,512]{2,1,0:T(8,128)(2,1)S(1)}, bf16[1,128,1024]{2,1,0:T(8,128)(2,1)S(1)}, bf16[1,128,1024]{2,1,0:T(8,128)(2,1)S(1)}) custom-call(s32[1,512]{1,0:T(1,128)S(1)} %bitcast.5, bf16[512,1024]{1,0:T(8,128)(2,1)S(1)} %get-tuple-element.73.g_ref, bf16[512,1024]{1,0:T(8,128)(2,1)S(1)} %get-tuple-element.61.k_ref, ...), custom_call_target="tpu_custom_call" | custom-call | flops 32999999488 | bytes 1000000 | tf_op jit(solution)/shard_map/grad_q/pallas_call | solution.py:68
  65.1 1.8 %collective-permute-start.12 = (bf16[1,128,1024]{2,1,0:T(8,128)(2,1)S(1)}, bf16[1,128,1024]{2,1,0:T(8,128)(2,1)S(1)}, u32[]{:S(2)}, u32[]{:S(2)}) collective-permute-start(bf16[1,128,1024]{2,1,0:T(8,128)(2,1)S(1)} %get-tuple-element.81), channel_id=1, source_target_pairs={{0,4},{4,8},{8,12},{12,16},{16,20},{20,24},{24,28},{28,0},{1,5},{5... | collective-permute-start | bytes 786440 | tf_op jit(solution)/shard_map/ppermute | solution.py:442
  66.9 2.9 %collective-permute-start.13 = (bf16[1,128,1024]{2,1,0:T(8,128)(2,1)S(1)}, bf16[1,128,1024]{2,1,0:T(8,128)(2,1)S(1)}, u32[]{:S(2)}, u32[]{:S(2)}) collective-permute-start(bf16[1,128,1024]{2,1,0:T(8,128)(2,1)S(1)} %get-tuple-element.82), channel_id=1, source_target_pairs={{0,28},{4,0},{8,4},{12,8},{16,12},{20,16},{24,20},{28,24},{1,29},{... | collective-permute-start | bytes 786440 | tf_op jit(solution)/shard_map/ppermute | solution.py:442
  69.8 1.9 %inner.1 = (f32[512,1024]{1,0:T(8,128)S(1)}, f32[512,1024]{1,0:T(8,128)S(1)}) custom-call(bf16[8,512,512]{2,1,0:T(8,128)(2,1)S(1)} %get-tuple-element.76.z_ref, bf16[8,512,512]{2,1,0:T(8,128)(2,1)S(1)} %get-tuple-element.77.p_ref, bf16[512,1024]{1,0:T(8,128)(2,1)S(1)} %get-tuple-element.67.q_ref, bf16[512,1024]{1,0:T(8,128)(2,1)S(1)} %get-tuple-element.73.g_ref), custom_call_target="tpu_custom_call" | custom-call | flops 5500000256 | bytes 1000000 | tf_op jit(solution)/shard_map/inner/pallas_call | solution.py:68
  72.6 1.6 %grad_kv.1 = (bf16[512,1024]{1,0:T(8,128)(2,1)S(1)}, bf16[512,1024]{1,0:T(8,128)(2,1)S(1)}, bf16[2,128,1024]{2,1,0:T(8,128)(2,1)S(1)}) custom-call(s32[1,512]{1,0:T(1,128)S(1)} %bitcast.6, bf16[8,128,128]{2,1,0:T(8,128)(2,1)S(1)} %collective-permute-done.10.far_ref, bf16[8,128,128]{2,1,0:T(8,128)(2,1)S(1)} %collective-permute-done.11.near_ref._, ...), custom_call_target="tpu_custom_call" | custom-call | flops 3300000000 | bytes 1000000 | tf_op jit(solution)/shard_map/grad_kv/pallas_call | solution.py:68
  74.2 1.7 %collective-permute-start.15 = (bf16[2,128,1024]{2,1,0:T(8,128)(2,1)S(1)}, bf16[2,128,1024]{2,1,0:T(8,128)(2,1)S(1)}, u32[]{:S(2)}, u32[]{:S(2)}) collective-permute-start(bf16[2,128,1024]{2,1,0:T(8,128)(2,1)S(1)} %get-tuple-element.85), channel_id=1, source_target_pairs={{0,28},{4,0},{8,4},{12,8},{16,12},{20,16},{24,20},{28,24},{1,29},{... | collective-permute-start | bytes 1572872 | tf_op jit(solution)/shard_map/ppermute | solution.py:442
  76.8 1.3 %normed.1 = bf16[512,1024]{1,0:T(8,128)(2,1)} custom-call(f32[512,1024]{1,0:T(8,128)S(1)} %get-tuple-element.68.u_ref, f32[512,128]{1,0:T(8,128)S(1)} %get-tuple-element.71.inverse_ref, bf16[512,1024]{1,0:T(8,128)(2,1)S(1)} %get-tuple-element.80._.refs_1_.refs_0_), custom_call_target="tpu_custom_call" | custom-call | flops 2200000000 | bytes 1000000 | tf_op jit(solution)/shard_map/normed/pallas_call | solution.py:68
  78.8 10.7 %collective-permute-done.12.left_ref = bf16[1,128,1024]{2,1,0:T(8,128)(2,1)S(1)} collective-permute-done((bf16[1,128,1024]{2,1,0:T(8,128)(2,1)S(1)}, bf16[1,128,1024]{2,1,0:T(8,128)(2,1)S(1)}, u32[]{:S(2)}, u32[]{:S(2)}) %collective-permute-start.12) | collective-permute-done | bytes 262176 | tf_op jit(solution)/shard_map/ppermute | solution.py:442
  89.5 2.3 %collective-permute-done.13.right_ref = bf16[1,128,1024]{2,1,0:T(8,128)(2,1)S(1)} collective-permute-done((bf16[1,128,1024]{2,1,0:T(8,128)(2,1)S(1)}, bf16[1,128,1024]{2,1,0:T(8,128)(2,1)S(1)}, u32[]{:S(2)}, u32[]{:S(2)}) %collective-permute-start.13) | collective-permute-done | bytes 262176 | tf_op jit(solution)/shard_map/ppermute | solution.py:442
  91.8 1.4 %finish_q.1 = (bf16[512,1024]{1,0:T(8,128)(2,1)}, bf16[16,128]{1,0:T(8,128)(2,1)S(1)}) custom-call(s32[2,128]{1,0:T(2,128)S(1)} %bitcast.11, bf16[1,128,1024]{2,1,0:T(8,128)(2,1)S(1)} %collective-permute-done.12.left_ref, bf16[1,128,1024]{2,1,0:T(8,128)(2,1)S(1)} %collective-permute-done.13.right_ref, bf16[512,1024]{1,0:T(8,128)(2,1)S(1)} %own_q.1.refs_0_), custom_call_target="tpu_custom_call" | custom-call | flops 2200000000 | bytes 1000000 | tf_op jit(solution)/shard_map/finish_q/pallas_call | solution.py:68
  93.2 1.2 %own_kv.1 = (bf16[512,1024]{1,0:T(8,128)(2,1)S(1)}, bf16[512,1024]{1,0:T(8,128)(2,1)S(1)}) custom-call(s32[1,512]{1,0:T(1,128)S(1)} %bitcast.9, bf16[512,1024]{1,0:T(8,128)(2,1)S(1)} %get-tuple-element.80._.refs_1_.refs_0_, bf16[512,1024]{1,0:T(8,128)(2,1)S(1)} %get-tuple-element.88.refs_1_, bf16[16,128]{1,0:T(8,128)(2,1)S(1)} %get-tuple-element.89.refs_2_), custom_call_target="tpu_custom_call" | custom-call | flops 2200000000 | bytes 1000000 | tf_op jit(solution)/shard_map/own_kv/pallas_call | solution.py:68
  94.8 6.5 %collective-permute-done.15.right_ref = bf16[2,128,1024]{2,1,0:T(8,128)(2,1)S(1)} collective-permute-done((bf16[2,128,1024]{2,1,0:T(8,128)(2,1)S(1)}, bf16[2,128,1024]{2,1,0:T(8,128)(2,1)S(1)}, u32[]{:S(2)}, u32[]{:S(2)}) %collective-permute-start.15) | collective-permute-done | bytes 524320 | tf_op jit(solution)/shard_map/ppermute | solution.py:442
  101.4 1.8 %finish_kv.1 = (bf16[512,1024]{1,0:T(8,128)(2,1)}, bf16[512,1024]{1,0:T(8,128)(2,1)}) custom-call(s32[2,128]{1,0:T(2,128)S(1)} %bitcast.12, bf16[2,128,1024]{2,1,0:T(8,128)(2,1)S(1)} %collective-permute-done.14.left_ref, bf16[2,128,1024]{2,1,0:T(8,128)(2,1)S(1)} %collective-permute-done.15.right_ref, f32[128,1024]{1,0:T(8,128)S(1)} %get-tuple-element.86.refs_0_, ...), custom_call_target="tpu_custom_call" | custom-call | flops 2200000000 | bytes 1000000 | tf_op jit(solution)/shard_map/finish_kv/pallas_call | solution.py:68
  (40 shorter events, 4.8 us)
Async XLA Ops:
  0.6 8.5 %copy-start = (bf16[512,1024]{1,0:T(8,128)(2,1)S(1)}, bf16[512,1024]{1,0:T(8,128)(2,1)}, u32[]{:S(2)}) copy-start(bf16[512,1024]{1,0:T(8,128)(2,1)} %k_ref.1) | copy-start | bytes 3145732
  0.6 8.5 %copy-start.1 = (bf16[512,1024]{1,0:T(8,128)(2,1)S(1)}, bf16[512,1024]{1,0:T(8,128)(2,1)}, u32[]{:S(2)}) copy-start(bf16[512,1024]{1,0:T(8,128)(2,1)} %v_ref.1) | copy-start | bytes 3145732
  0.7 8.5 %copy-start.2 = (bf16[512,1024]{1,0:T(8,128)(2,1)S(1)}, bf16[512,1024]{1,0:T(8,128)(2,1)}, u32[]{:S(2)}) copy-start(bf16[512,1024]{1,0:T(8,128)(2,1)} %q_ref.1) | copy-start | bytes 3145732
  0.7 8.5 %copy-start.6 = (f32[512,8]{0,1:T(8,128)S(1)}, f32[512,8]{0,1:T(8,128)}, u32[]{:S(2)}) copy-start(f32[512,8]{0,1:T(8,128)} %param.12) | copy-start | bytes 49156
  0.7 8.5 %copy-start.7 = (s32[512]{0:T(512)S(1)}, s32[512]{0:T(512)}, u32[]{:S(2)}) copy-start(s32[512]{0:T(512)} %param.15) | copy-start | bytes 6148
  0.7 8.5 %copy-start.9 = (s32[8]{0:T(128)S(1)}, s32[8]{0:T(128)}, u32[]{:S(2)}) copy-start(s32[8]{0:T(128)} %docs_ref.1) | copy-start | bytes 100
  3.0 11.1 %copy-start.4 = (bf16[2,128,1024]{2,1,0:T(8,128)(2,1)}, bf16[2,128,1024]{2,1,0:T(8,128)(2,1)S(1)}, u32[]{:S(2)}) copy-start(bf16[2,128,1024]{2,1,0:T(8,128)(2,1)S(1)} %get-tuple-element.55.rows_ref) | copy-start | bytes 1572868
  3.0 26.8 %collective-permute-start.2 = (bf16[2,128,1024]{2,1,0:T(8,128)(2,1)S(1)}, bf16[2,128,1024]{2,1,0:T(8,128)(2,1)S(1)}, u32[]{:S(2)}, u32[]{:S(2)}) collective-permute-start(bf16[2,128,1024]{2,1,0:T(8,128)(2,1)S(1)} %get-tuple-element.54), channel_id=1, source_target_pairs={{0,4},{4,8},{8,12},{12,16},{16,20},{20,24},{24,28},{28,0},{1,5},{5... | collective-permute-start | bytes 1572872 | tf_op jit(solution)/shard_map/ppermute | solution.py:442
  6.1 31.9 %collective-permute-start.3 = (bf16[2,128,1024]{2,1,0:T(8,128)(2,1)S(1)}, bf16[2,128,1024]{2,1,0:T(8,128)(2,1)S(1)}, u32[]{:S(2)}, u32[]{:S(2)}) collective-permute-start(bf16[2,128,1024]{2,1,0:T(8,128)(2,1)S(1)} %get-tuple-element.55.rows_ref), channel_id=1, source_target_pairs={{0,28},{4,0},{8,4},{12,8},{16,12},{20,16},{24,20},{28,24},{1,29},{... | collective-permute-start | bytes 1572872 | tf_op jit(solution)/shard_map/ppermute | solution.py:442
  14.1 24.9 %collective-permute-start.5 = (f32[16,128]{1,0:T(8,128)S(1)}, f32[16,128]{1,0:T(8,128)S(1)}, u32[]{:S(2)}, u32[]{:S(2)}) collective-permute-start(f32[16,128]{1,0:T(8,128)S(1)} %get-tuple-element.60.facts_ref), channel_id=1, source_target_pairs={{0,28},{4,0},{8,4},{12,8},{16,12},{20,16},{24,20},{28,24},{1,29},{... | collective-permute-start | bytes 24584 | tf_op jit(solution)/shard_map/ppermute | solution.py:442
  16.1 22.9 %collective-permute-start.4 = (f32[16,128]{1,0:T(8,128)S(1)}, f32[16,128]{1,0:T(8,128)S(1)}, u32[]{:S(2)}, u32[]{:S(2)}) collective-permute-start(f32[16,128]{1,0:T(8,128)S(1)} %get-tuple-element.60.facts_ref), channel_id=1, source_target_pairs={{0,4},{4,8},{8,12},{12,16},{16,20},{20,24},{24,28},{28,0},{1,5},{5... | collective-permute-start | bytes 24584 | tf_op jit(solution)/shard_map/ppermute | solution.py:442
  16.2 25.0 %collective-permute-start = (bf16[1,128,1024]{2,1,0:T(8,128)(2,1)S(1)}, bf16[1,128,1024]{2,1,0:T(8,128)(2,1)S(1)}, u32[]{:S(2)}, u32[]{:S(2)}) collective-permute-start(bf16[1,128,1024]{2,1,0:T(8,128)(2,1)S(1)} %get-tuple-element.51), channel_id=1, source_target_pairs={{0,4},{4,8},{8,12},{12,16},{16,20},{20,24},{24,28},{28,0},{1,5},{5... | collective-permute-start | bytes 786440 | tf_op jit(solution)/shard_map/ppermute | solution.py:442
  29.8 12.5 %collective-permute-start.1 = (bf16[1,128,1024]{2,1,0:T(8,128)(2,1)S(1)}, bf16[1,128,1024]{2,1,0:T(8,128)(2,1)S(1)}, u32[]{:S(2)}, u32[]{:S(2)}) collective-permute-start(bf16[1,128,1024]{2,1,0:T(8,128)(2,1)S(1)} %get-tuple-element.52), channel_id=1, source_target_pairs={{0,28},{4,0},{8,4},{12,8},{16,12},{20,16},{24,20},{28,24},{1,29},{... | collective-permute-start | bytes 786440 | tf_op jit(solution)/shard_map/ppermute | solution.py:442
  38.9 8.3 %collective-permute-start.7 = (bf16[8,128,128]{2,1,0:T(8,128)(2,1)S(1)}, bf16[8,128,128]{2,1,0:T(8,128)(2,1)S(1)}, u32[]{:S(2)}, u32[]{:S(2)}) collective-permute-start(bf16[8,128,128]{2,1,0:T(8,128)(2,1)S(1)} %state.1._), channel_id=1, source_target_pairs={{0,8},{4,12},{8,16},{12,20},{16,24},{20,28},{24,0},{28,4},{1,9},{5... | collective-permute-start | bytes 786440 | tf_op jit(solution)/shard_map/ppermute | solution.py:442
  39.0 12.9 %collective-permute-start.6 = (bf16[8,128,128]{2,1,0:T(8,128)(2,1)S(1)}, bf16[8,128,128]{2,1,0:T(8,128)(2,1)S(1)}, u32[]{:S(2)}, u32[]{:S(2)}) collective-permute-start(bf16[8,128,128]{2,1,0:T(8,128)(2,1)S(1)} %state.1._), channel_id=1, source_target_pairs={{0,4},{4,8},{8,12},{12,16},{16,20},{20,24},{24,28},{28,0},{1,5},{5... | collective-permute-start | bytes 786440 | tf_op jit(solution)/shard_map/ppermute | solution.py:442
  42.3 9.5 %copy-start.3 = (bf16[512,1024]{1,0:T(8,128)(2,1)S(1)}, bf16[512,1024]{1,0:T(8,128)(2,1)}, u32[]{:S(2)}) copy-start(bf16[512,1024]{1,0:T(8,128)(2,1)} %ct_ref.3) | copy-start | bytes 3145732
  42.3 9.5 %copy-start.10 = (f32[8]{0:T(128)S(1)}, f32[8]{0:T(128)}, u32[]{:S(2)}) copy-start(f32[8]{0:T(128)} %scale_ref.3) | copy-start | bytes 100
  53.5 1.2 %collective-permute-start.8 = (f32[2,512]{1,0:T(2,128)S(1)}, f32[2,512]{1,0:T(2,128)S(1)}, u32[]{:S(2)}, u32[]{:S(2)}) collective-permute-start(f32[2,512]{1,0:T(2,128)S(1)} %get-tuple-element.70.a_ref), channel_id=1, source_target_pairs={{0,1},{1,0},{2,3},{3,2},{4,5},{5,4},{6,7},{7,6},{8,9},{9,8},{10,11... | collective-permute-start | bytes 12296 | tf_op jit(solution)/shard_map/ppermute | solution.py:462
  54.7 3.6 %collective-permute-start.9 = (f32[2,512]{1,0:T(2,128)S(1)}, f32[2,512]{1,0:T(2,128)S(1)}, u32[]{:S(2)}, u32[]{:S(2)}) collective-permute-start(f32[2,512]{1,0:T(2,128)S(1)} %add.1.refs_0_), channel_id=1, source_target_pairs={{0,2},{1,3},{2,0},{3,1},{4,6},{5,7},{6,4},{7,5},{8,10},{9,11},{10,... | collective-permute-start | bytes 12296 | tf_op jit(solution)/shard_map/ppermute | solution.py:462
  59.9 11.8 %collective-permute-start.11 = (bf16[8,128,128]{2,1,0:T(8,128)(2,1)S(1)}, bf16[8,128,128]{2,1,0:T(8,128)(2,1)S(1)}, u32[]{:S(2)}, u32[]{:S(2)}) collective-permute-start(bf16[8,128,128]{2,1,0:T(8,128)(2,1)S(1)} %get-tuple-element.72.message_ref), channel_id=1, source_target_pairs={{0,28},{4,0},{8,4},{12,8},{16,12},{20,16},{24,20},{28,24},{1,29},{... | collective-permute-start | bytes 786440 | tf_op jit(solution)/shard_map/ppermute | solution.py:442
  60.0 12.5 %collective-permute-start.10 = (bf16[8,128,128]{2,1,0:T(8,128)(2,1)S(1)}, bf16[8,128,128]{2,1,0:T(8,128)(2,1)S(1)}, u32[]{:S(2)}, u32[]{:S(2)}) collective-permute-start(bf16[8,128,128]{2,1,0:T(8,128)(2,1)S(1)} %get-tuple-element.72.message_ref), channel_id=1, source_target_pairs={{0,24},{4,28},{8,0},{12,4},{16,8},{20,12},{24,16},{28,20},{1,25},{... | collective-permute-start | bytes 786440 | tf_op jit(solution)/shard_map/ppermute | solution.py:442
  65.1 24.4 %collective-permute-start.12 = (bf16[1,128,1024]{2,1,0:T(8,128)(2,1)S(1)}, bf16[1,128,1024]{2,1,0:T(8,128)(2,1)S(1)}, u32[]{:S(2)}, u32[]{:S(2)}) collective-permute-start(bf16[1,128,1024]{2,1,0:T(8,128)(2,1)S(1)} %get-tuple-element.81), channel_id=1, source_target_pairs={{0,4},{4,8},{8,12},{12,16},{16,20},{20,24},{24,28},{28,0},{1,5},{5... | collective-permute-start | bytes 786440 | tf_op jit(solution)/shard_map/ppermute | solution.py:442
  66.9 24.9 %collective-permute-start.13 = (bf16[1,128,1024]{2,1,0:T(8,128)(2,1)S(1)}, bf16[1,128,1024]{2,1,0:T(8,128)(2,1)S(1)}, u32[]{:S(2)}, u32[]{:S(2)}) collective-permute-start(bf16[1,128,1024]{2,1,0:T(8,128)(2,1)S(1)} %get-tuple-element.82), channel_id=1, source_target_pairs={{0,28},{4,0},{8,4},{12,8},{16,12},{20,16},{24,20},{28,24},{1,29},{... | collective-permute-start | bytes 786440 | tf_op jit(solution)/shard_map/ppermute | solution.py:442
  74.2 27.2 %collective-permute-start.15 = (bf16[2,128,1024]{2,1,0:T(8,128)(2,1)S(1)}, bf16[2,128,1024]{2,1,0:T(8,128)(2,1)S(1)}, u32[]{:S(2)}, u32[]{:S(2)}) collective-permute-start(bf16[2,128,1024]{2,1,0:T(8,128)(2,1)S(1)} %get-tuple-element.85), channel_id=1, source_target_pairs={{0,28},{4,0},{8,4},{12,8},{16,12},{20,16},{24,20},{28,24},{1,29},{... | collective-permute-start | bytes 1572872 | tf_op jit(solution)/shard_map/ppermute | solution.py:442
  76.4 25.0 %collective-permute-start.14 = (bf16[2,128,1024]{2,1,0:T(8,128)(2,1)S(1)}, bf16[2,128,1024]{2,1,0:T(8,128)(2,1)S(1)}, u32[]{:S(2)}, u32[]{:S(2)}) collective-permute-start(bf16[2,128,1024]{2,1,0:T(8,128)(2,1)S(1)} %right.1), channel_id=1, source_target_pairs={{0,4},{4,8},{8,12},{12,16},{16,20},{20,24},{24,28},{28,0},{1,5},{5... | collective-permute-start | bytes 1572872 | tf_op jit(solution)/shard_map/ppermute | solution.py:442
  78.1 13.7 %copy-start.8 = (s32[1,2,128]{2,1,0:T(2,128)S(1)}, s32[1,2,128]{2,1,0:T(2,128)}, u32[]{:S(2)}) copy-start(s32[1,2,128]{2,1,0:T(2,128)} %param.14) | copy-start | bytes 3076
  93.2 1.3 %copy-start.5 = (bf16[2,128,1024]{2,1,0:T(8,128)(2,1)S(1)}, bf16[2,128,1024]{2,1,0:T(8,128)(2,1)}, u32[]{:S(2)}) copy-start(bf16[2,128,1024]{2,1,0:T(8,128)(2,1)} %copy-done.4) | copy-start | bytes 1572868

commit v3 on v2

--- a/solution.py
+++ b/solution.py
@@ -83,7 +83,11 @@
     return jax.ShapeDtypeStruct(shape, dtype)
 
 
-def pick_kernel(send_hbm, k_hbm, v_hbm, left_ref, right_ref, hot_ref, send_ref, k_ref, v_ref, sem):
+def is_odd():
+    return lax.rem(lax.axis_index("seq"), 2) == 1
+
+
+def pick_kernel(send_hbm, k_hbm, v_hbm, pair_ref, other_ref, hot_ref, send_ref, k_ref, v_ref, sem):
     rows, features = k_ref.shape
     capacity = send_ref.shape[1]
     named_copy = pltpu.make_async_copy(send_hbm, send_ref, sem.at[0])
@@ -98,7 +102,8 @@
     named_copy.wait()
     lane = iota((capacity, 128), 1)
     for side in range(2):
-        named = along_rows(send_ref[side : side + 1, :])
+        slots = jnp.where(is_odd(), send_ref[side : side + 1, :], send_ref[1 - side : 2 - side, :])
+        named = along_rows(slots)
         for start in range(0, rows, 128):
             hot_ref[side * capacity : (side + 1) * capacity, start : start + 128] = one_hot(
                 named == lane + start
@@ -108,8 +113,8 @@
             copy.wait()
         for part in chunks(features):
             picked = dot(hot_ref[...], target[:, part]).astype(BF)
-            left_ref[index, :, part] = picked[:capacity]
-            right_ref[index, :, part] = picked[capacity:]
+            pair_ref[index, :, part] = picked[:capacity]
+            other_ref[index, :, part] = picked[capacity:]
 
 
 def pick(send, k, v):
@@ -182,10 +187,12 @@
     taken = along_rows(take_ref[...])
     for start_row in range(0, rows, 128):
         own_ref[:, start_row : start_row + 128] = one_hot(taken - capacity == lane + start_row)
-    hot_ref[:, :capacity] = one_hot(taken == lane)
-    hot_ref[:, capacity:] = one_hot(taken - (capacity + rows) == lane)
+    right = capacity + rows
+    odd = is_odd()
+    hot_ref[:, :capacity] = one_hot(taken - jnp.where(odd, 0, right) == lane)
+    hot_ref[:, capacity:] = one_hot(taken - jnp.where(odd, right, 0) == lane)
     leave_ref[...] = sum(dot_tn(hot_ref[...], piece) for piece in pieces(leaving))
-    facts_ref[:heads] = leave_ref[capacity:, :].T[:heads]
+    facts_ref[:heads] = jnp.where(odd, leave_ref[capacity:, :], leave_ref[:capacity, :]).T[:heads]
     facts_ref[heads:] = along_rows(through, capacity)[:heads]
     for part in chunks(features):
         for source, target in ((k_ref, ko_ref), (v_ref, vo_ref), (q_ref, qo_ref)):
@@ -393,7 +400,7 @@
             left_ref[index, :, part] = dot(hot, source[:, part]).astype(BF)
 
 
-def lend_kernel(facts_ref, after_ref, near_ref, far_ref, message_ref, lent_ref, rows_ref, _, dk_ref, dv_ref):
+def lend_kernel(facts_ref, after_ref, near_ref, far_ref, message_ref, lent_ref, pair_ref, other_ref, _, dk_ref, dv_ref):
     features = dk_ref.shape[1]
     heads, width = message_ref.shape[:2]
     before = shards_before(-1)
@@ -401,8 +408,12 @@
         after = carried_sum(before, after_ref, near_ref, far_ref, h)
         state_grad = (message_ref[h].astype(F32) + decayed(facts_ref, h, after)).astype(BF)
         leaving = along_rows(lent_ref[h : h + 1, :], width)
-        dk_ref[:, part] = leaving * dot_nt(rows_ref[1, :, part], state_grad)
-        dv_ref[:, part] = leaving * dot(rows_ref[0, :, part], state_grad)
+        k, v = [
+            jnp.where(is_odd(), pair_ref[index, :, part], other_ref[index, :, part])
+            for index in range(2)
+        ]
+        dk_ref[:, part] = leaving * dot_nt(v, state_grad)
+        dv_ref[:, part] = leaving * dot(k, state_grad)
 
 
 def own_kernel(capacity, count, take_ref, *refs):
@@ -414,7 +425,7 @@
             target[:, part] = dot(hot, source[:, part]).astype(BF)
 
 
-def finish_kernel(count, lending, send_ref, left_ref, right_ref, *refs):
+def finish_kernel(count, lending, send_ref, right_ref, left_ref, *refs):
     lent, refs = refs[:lending], refs[lending:]
     rows = refs[0].shape[0]
     capacity = send_ref.shape[1]
@@ -440,6 +451,14 @@
 def shifted(array, by):
     peers = lax.axis_size("seq")
     return lax.ppermute(array, "seq", [(i, (i + by) % peers) for i in range(peers)])
+
+
+def swapped(array, first):
+    peers = lax.axis_size("seq")
+    partners = [(i - first ^ 1) + first for i in range(peers)]
+    return lax.ppermute(
+        array, "seq", [(i, j if 0 <= j < peers else i) for i, j in enumerate(partners)]
+    )
 
 
 def shifted_open(array, by):
@@ -495,14 +514,14 @@
     message_shape = sds((heads, width, width))
     one_side, two_sides = sds((1, capacity, features)), sds((2, capacity, features))
 
-    kv_left, kv_right, named = pick(send, key_vectors, value_vectors)
-    kv_before, kv_after = shifted(kv_right, 1), shifted(kv_left, -1)
+    kv_pair, kv_other, named = pick(send, key_vectors, value_vectors)
+    kv_first, kv_second = swapped(kv_pair, 0), swapped(kv_other, 1)
     (
-        q_left, q_right, q_own, k_own, v_own, hot, mask, cols, turned, facts, state_own, leave
+        q_pair, q_other, q_own, k_own, v_own, hot, mask, cols, turned, facts, state_own, leave
     ) = prep(doc_lengths, take, log_decay.T, named, queries, key_vectors, value_vectors)
-    q_before, q_after = shifted(q_right, 1), shifted(q_left, -1)
+    q_first, q_second = swapped(q_pair, 0), swapped(q_other, 1)
     (message,) = local(
-        state_kernel, "state", 30, [message_shape], (kv_before, kv_after, leave, state_own)
+        state_kernel, "state", 30, [message_shape], (kv_first, kv_second, leave, state_own)
     )
     near, far = carried(message, facts, 1)
     facts_before, facts_after = shifted(facts, 1), shifted(facts, -1)
@@ -511,14 +530,14 @@
         "assemble",
         5,
         [full, full],
-        (hot, kv_before, kv_after, k_own, v_own, message, facts_before, facts_after),
+        (hot, kv_first, kv_second, k_own, v_own, message, facts_before, facts_after),
     )
     q, qe, weight, probs, o_inside = local(
         inside_kernel,
         "inside",
         30,
         [full, sds((heads, width, rows)), sds((heads, rows, rows), F32), squares, full32],
-        (hot, q_before, q_after, q_own, k, v, mask, cols, turned),
+        (hot, q_first, q_second, q_own, k, v, mask, cols, turned),
     )
     u, state_low, sums = local(
         output_kernel,
@@ -528,7 +547,10 @@
         (head_scale, o_inside, q, facts_before, near, far, cols, cotangent),
         scalars=1,
     )
-    sums = over_heads(sums)
+    peers = lax.axis_size("head")
+    sums = [sums] + [
+        lax.ppermute(sums, "head", [(i, i ^ by) for i in range(peers)]) for by in range(1, peers)
+    ]
     g, grad_message, inverse = local(
         functools.partial(norm_kernel, total),
         "norm",
@@ -565,7 +587,7 @@
         "lend",
         2,
         [lent_rows, lent_rows],
-        (facts, facts_after, grad_near, grad_far, grad_message, facts_before, kv_left, dk),
+        (facts, facts_after, grad_near, grad_far, grad_message, facts_before, kv_pair, kv_other, dk),
     )
     (normed,) = local(normed_kernel, "normed", 2, [full], (u, inverse, dk))
     (dq_own,) = local(
@@ -576,7 +598,7 @@
         "finish_q",
         2,
         [full, sds((16, 128))],
-        (send, dq_before, dq_after, dq_own),
+        (send, dq_after, dq_before, dq_own),
     )
     dk_own, dv_own = local(
         functools.partial(own_kernel, capacity, 2), "own_kv", 2, [full, full],
@@ -587,7 +609,7 @@
         "finish_kv",
         2,
         [full, full],
-        (send, dkv_before, dkv_after, dk_lent, dv_lent, dk_own, dv_own),
+        (send, dkv_after, dkv_before, dk_lent, dv_lent, dk_own, dv_own),
     )
     return normed, grad_queries, grad_keys, grad_values
 

time: 103 us -> 103 us (level)
  starting transfers between devices: 24.4 us -> 30.1 us
  waiting for transfers between devices: 48.4 us -> 42.7 us
    ppermute x14 -> x10, waiting for transfers between devices: 45.2 us -> 27.8 us  [shifted(): lax.ppermute(array, 'seq', [(i, (i + by) % peers) for i in range(peers)])]
    ppermute x2 -> x7, waiting for transfers between devices: 3.27 us -> 14.9 us  [the longest x4 13 us: swapped(): lax.ppermute(array, 'seq', [(i, j if 0 <= j < peers else i) for i, j in e...]
    ppermute x2 -> x7, starting transfers between devices: 1.56 us -> 9.16 us  [the longest x4 7.24 us: swapped(): lax.ppermute(array, 'seq', [(i, j if 0 <= j < peers else i) for i, j in e...]
    ppermute x14 -> x10, starting transfers between devices: 22.8 us -> 20.9 us  [shifted(): lax.ppermute(array, 'seq', [(i, (i + by) % peers) for i in range(peers)])]
    pallas_call x18 -> x17, Pallas kernels: 29.4 us -> 29.4 us  [local(): pl.pallas_call(kernel, in_specs=specs, out_specs=[vmem] * len(out_shape),...]
  transfers between devices with their start and end apart: 16 -> 17, of which waited for: 12 -> 10; matrix products, arithmetic and copies ran while one was open for 0% -> 0% of each run, Pallas kernels for 21% -> 21%
where the time goes in v3:
time: 103 us
  waiting for transfers between devices  42.7 us (41%)
  starting transfers between devices  30.1 us (29%)
  Pallas kernels  29.4 us (29%)
    pallas_call x17, Pallas kernels, local(): pl.pallas_call(kernel, in_specs=specs, out_specs=[vmem] * len(out_shape),...  29.4 us
    ppermute x10, waiting for transfers between devices, shifted(): lax.ppermute(array, 'seq', [(i, (i + by) % peers) for i in range(peers)])  27.8 us
    ppermute x10, starting transfers between devices, shifted(): lax.ppermute(array, 'seq', [(i, (i + by) % peers) for i in range(peers)])  20.9 us
    ppermute x4, waiting for transfers between devices, swapped(): lax.ppermute(array, 'seq', [(i, j if 0 <= j < peers else i) for i, j in e...  13 us
    ppermute x4, starting transfers between devices, swapped(): lax.ppermute(array, 'seq', [(i, j if 0 <= j < peers else i) for i, j in e...  7.24 us
  transfers between devices with their start and end apart: 17, of which 10 were waited for; matrix products, arithmetic and copies ran while one was open for 0% of the time, Pallas kernels for 21%

profile of v3, /device:TPU:0, one launch (start us, length us, event | category | flops | bytes accessed | tf_op | source)
XLA Modules:
  0.0 103.1 jit_solution(123180763879011843)
XLA Ops:
  0.7 2.3 %pick.1 = (bf16[2,128,1024]{2,1,0:T(8,128)(2,1)S(1)}, bf16[2,128,1024]{2,1,0:T(8,128)(2,1)S(1)}, bf16[256,512]{1,0:T(8,128)(2,1)S(1)}) custom-call(s32[2,128]{1,0:T(2,128)} %bitcast.10, bf16[512,1024]{1,0:T(8,128)(2,1)} %k_ref.1, bf16[512,1024]{1,0:T(8,128)(2,1)} %v_ref.1), custom_call_target="tpu_custom_call" | custom-call | flops 2200000000 | bytes 1000000 | tf_op jit(solution)/shard_map/pick/pallas_call | solution.py:68
  3.0 3.0 %collective-permute-start.2 = (bf16[2,128,1024]{2,1,0:T(8,128)(2,1)S(1)}, bf16[2,128,1024]{2,1,0:T(8,128)(2,1)S(1)}, u32[]{:S(2)}, u32[]{:S(2)}) collective-permute-start(bf16[2,128,1024]{2,1,0:T(8,128)(2,1)S(1)} %get-tuple-element.54.pair_ref), channel_id=1, source_target_pairs={{0,4},{4,0},{8,12},{12,8},{16,20},{20,16},{24,28},{28,24},{1,5},{5... | collective-permute-start | bytes 1572872 | tf_op jit(solution)/shard_map/ppermute | solution.py:459
  6.8 4.9 %prep.1 = (bf16[1,128,1024]{2,1,0:T(8,128)(2,1)S(1)}, bf16[1,128,1024]{2,1,0:T(8,128)(2,1)S(1)}, bf16[512,1024]{1,0:T(8,128)(2,1)S(1)}, bf16[512,1024]{1,0:T(8,1...) custom-call(s32[8]{0:T(128)S(1)} %copy-done.11, ...), custom_call_target="tpu_custom_call" | custom-call | flops 32999999488 | bytes 1000000 | tf_op jit(solution)/shard_map/prep/pallas_call | solution.py:68
  11.7 3.6 %collective-permute-start.5 = (f32[16,128]{1,0:T(8,128)S(1)}, f32[16,128]{1,0:T(8,128)S(1)}, u32[]{:S(2)}, u32[]{:S(2)}) collective-permute-start(f32[16,128]{1,0:T(8,128)S(1)} %get-tuple-element.60.facts_ref), channel_id=1, source_target_pairs={{0,28},{4,0},{8,4},{12,8},{16,12},{20,16},{24,20},{28,24},{1,29},{... | collective-permute-start | bytes 24584 | tf_op jit(solution)/shard_map/ppermute | solution.py:453
  16.1 2.9 %collective-permute-start = (bf16[1,128,1024]{2,1,0:T(8,128)(2,1)S(1)}, bf16[1,128,1024]{2,1,0:T(8,128)(2,1)S(1)}, u32[]{:S(2)}, u32[]{:S(2)}) collective-permute-start(bf16[1,128,1024]{2,1,0:T(8,128)(2,1)S(1)} %get-tuple-element.51), channel_id=1, source_target_pairs={{0,4},{4,0},{8,12},{12,8},{16,20},{20,16},{24,28},{28,24},{1,5},{5... | collective-permute-start | bytes 786440 | tf_op jit(solution)/shard_map/ppermute | solution.py:459
  19.0 10.8 %collective-permute-done.2.left_ref = bf16[2,128,1024]{2,1,0:T(8,128)(2,1)S(1)} collective-permute-done((bf16[2,128,1024]{2,1,0:T(8,128)(2,1)S(1)}, bf16[2,128,1024]{2,1,0:T(8,128)(2,1)S(1)}, u32[]{:S(2)}, u32[]{:S(2)}) %collective-permute-start.2) | collective-permute-done | bytes 524320 | tf_op jit(solution)/shard_map/ppermute | solution.py:459
  31.5 5.2 %collective-permute-start.7 = (bf16[8,128,128]{2,1,0:T(8,128)(2,1)S(1)}, bf16[8,128,128]{2,1,0:T(8,128)(2,1)S(1)}, u32[]{:S(2)}, u32[]{:S(2)}) collective-permute-start(bf16[8,128,128]{2,1,0:T(8,128)(2,1)S(1)} %state.1._), channel_id=1, source_target_pairs={{0,8},{4,12},{8,16},{12,20},{16,24},{20,28},{24,0},{28,4},{1,9},{5... | collective-permute-start | bytes 786440 | tf_op jit(solution)/shard_map/ppermute | solution.py:453
  36.7 1.6 %collective-permute-start.6 = (bf16[8,128,128]{2,1,0:T(8,128)(2,1)S(1)}, bf16[8,128,128]{2,1,0:T(8,128)(2,1)S(1)}, u32[]{:S(2)}, u32[]{:S(2)}) collective-permute-start(bf16[8,128,128]{2,1,0:T(8,128)(2,1)S(1)} %state.1._), channel_id=1, source_target_pairs={{0,4},{4,8},{8,12},{12,16},{16,20},{20,24},{24,28},{28,0},{1,5},{5... | collective-permute-start | bytes 786440 | tf_op jit(solution)/shard_map/ppermute | solution.py:453
  39.0 2.2 %collective-permute-done.left_ref = bf16[1,128,1024]{2,1,0:T(8,128)(2,1)S(1)} collective-permute-done((bf16[1,128,1024]{2,1,0:T(8,128)(2,1)S(1)}, bf16[1,128,1024]{2,1,0:T(8,128)(2,1)S(1)}, u32[]{:S(2)}, u32[]{:S(2)}) %collective-permute-start) | collective-permute-done | bytes 262176 | tf_op jit(solution)/shard_map/ppermute | solution.py:459
  41.2 3.3 %inside.1 = (bf16[512,1024]{1,0:T(8,128)(2,1)S(1)}, bf16[8,128,512]{2,1,0:T(8,128)(2,1)S(1)}, f32[8,512,512]{2,1,0:T(8,128)S(1)}, bf16[8,512,512]{2,1,0:T(8,128)(2,1)S(1)}, f32[512,1024]{1,0:T(8,128)S(1)}) custom-call(bf16[512,256]{1,0:T(8,128)(2,1)S(1)} %get-tuple-element.50.hot_ref, bf16[1,128,1024]{2,1,0:T(8,128)(2,1)S(1)} %collective-permute-done.left_ref, ...), custom_call_target="tpu_custom_call" | custom-call | flops 32999999488 | bytes 1000000 | tf_op jit(solution)/shard_map/inside/pallas_call | solution.py:68
  44.6 2.8 %collective-permute-done.7.far_ref = bf16[8,128,128]{2,1,0:T(8,128)(2,1)S(1)} collective-permute-done((bf16[8,128,128]{2,1,0:T(8,128)(2,1)S(1)}, bf16[8,128,128]{2,1,0:T(8,128)(2,1)S(1)}, u32[]{:S(2)}, u32[]{:S(2)}) %collective-permute-start.7) | collective-permute-done | bytes 262176 | tf_op jit(solution)/shard_map/ppermute | solution.py:453
  47.3 2.0 %collective-permute-done.6.near_ref = bf16[8,128,128]{2,1,0:T(8,128)(2,1)S(1)} collective-permute-done((bf16[8,128,128]{2,1,0:T(8,128)(2,1)S(1)}, bf16[8,128,128]{2,1,0:T(8,128)(2,1)S(1)}, u32[]{:S(2)}, u32[]{:S(2)}) %collective-permute-start.6) | collective-permute-done | bytes 262176 | tf_op jit(solution)/shard_map/ppermute | solution.py:453
  49.3 1.7 %output.1 = (f32[512,1024]{1,0:T(8,128)S(1)}, bf16[8,128,128]{2,1,0:T(8,128)(2,1)S(1)}, f32[2,512]{1,0:T(2,128)S(1)}) custom-call(f32[8]{0:T(128)S(1)} %copy-done.12, f32[512,1024]{1,0:T(8,128)S(1)} %get-tuple-element.66.o_ref, bf16[512,1024]{1,0:T(8,128)(2,1)S(1)} %get-tuple-element.67.q_ref, ...), custom_call_target="tpu_custom_call" | custom-call | flops 3300000000 | bytes 1000000 | tf_op jit(solution)/shard_map/output/pallas_call | solution.py:68
  51.1 1.6 %collective-permute-start.9 = (f32[2,512]{1,0:T(2,128)S(1)}, f32[2,512]{1,0:T(2,128)S(1)}, u32[]{:S(2)}, u32[]{:S(2)}) collective-permute-start(f32[2,512]{1,0:T(2,128)S(1)} %get-tuple-element.70.refs_0_), channel_id=1, source_target_pairs={{0,2},{1,3},{2,0},{3,1},{4,6},{5,7},{6,4},{7,5},{8,10},{9,11},{10,... | collective-permute-start | bytes 12296 | tf_op jit(solution)/shard_map/ppermute | solution.py:552
  52.9 1.2 %collective-permute-done.10.refs_3_ = f32[2,512]{1,0:T(2,128)S(1)} collective-permute-done((f32[2,512]{1,0:T(2,128)S(1)}, f32[2,512]{1,0:T(2,128)S(1)}, u32[]{:S(2)}, u32[]{:S(2)}) %collective-permute-start.10) | collective-permute-done | bytes 4128 | tf_op jit(solution)/shard_map/ppermute | solution.py:552
  54.8 1.6 %norm.1 = (bf16[512,1024]{1,0:T(8,128)(2,1)S(1)}, bf16[8,128,128]{2,1,0:T(8,128)(2,1)S(1)}, f32[512,128]{1,0:T(8,128)S(1)}) custom-call(f32[8]{0:T(128)S(1)} %copy-done.12, f32[512,1024]{1,0:T(8,128)S(1)} %get-tuple-element.68.u_ref, bf16[512,1024]{1,0:T(8,128)(2,1)S(1)} %copy-done.3, bf16[8,128,512]{2,1,0:T(8,128)(2,1)S(1)} %get-tuple-element.69.qe_ref, ...), custom_call_target="tpu_custom_call" | custom-call | flops 4400000000 | bytes 1000000 | tf_op jit(solution)/shard_map/norm/pallas_call | solution.py:68
  56.4 2.4 %collective-permute-start.12 = (bf16[8,128,128]{2,1,0:T(8,128)(2,1)S(1)}, bf16[8,128,128]{2,1,0:T(8,128)(2,1)S(1)}, u32[]{:S(2)}, u32[]{:S(2)}) collective-permute-start(bf16[8,128,128]{2,1,0:T(8,128)(2,1)S(1)} %get-tuple-element.72.message_ref), channel_id=1, source_target_pairs={{0,28},{4,0},{8,4},{12,8},{16,12},{20,16},{24,20},{28,24},{1,29},{... | collective-permute-start | bytes 786440 | tf_op jit(solution)/shard_map/ppermute | solution.py:453
  58.8 3.0 %collective-permute-start.11 = (bf16[8,128,128]{2,1,0:T(8,128)(2,1)S(1)}, bf16[8,128,128]{2,1,0:T(8,128)(2,1)S(1)}, u32[]{:S(2)}, u32[]{:S(2)}) collective-permute-start(bf16[8,128,128]{2,1,0:T(8,128)(2,1)S(1)} %get-tuple-element.72.message_ref), channel_id=1, source_target_pairs={{0,24},{4,28},{8,0},{12,4},{16,8},{20,12},{24,16},{28,20},{1,25},{... | collective-permute-start | bytes 786440 | tf_op jit(solution)/shard_map/ppermute | solution.py:453
  61.8 3.1 %grad_q.1 = (bf16[512,1024]{1,0:T(8,128)(2,1)S(1)}, bf16[8,512,512]{2,1,0:T(8,128)(2,1)S(1)}, bf16[1,128,1024]{2,1,0:T(8,128)(2,1)S(1)}, bf16[1,128,1024]{2,1,0:T(8,128)(2,1)S(1)}) custom-call(s32[1,512]{1,0:T(1,128)S(1)} %bitcast.5, bf16[512,1024]{1,0:T(8,128)(2,1)S(1)} %get-tuple-element.73.g_ref, bf16[512,1024]{1,0:T(8,128)(2,1)S(1)} %get-tuple-element.61.k_ref, ...), custom_call_target="tpu_custom_call" | custom-call | flops 32999999488 | bytes 1000000 | tf_op jit(solution)/shard_map/grad_q/pallas_call | solution.py:68
  64.9 1.7 %collective-permute-start.13 = (bf16[1,128,1024]{2,1,0:T(8,128)(2,1)S(1)}, bf16[1,128,1024]{2,1,0:T(8,128)(2,1)S(1)}, u32[]{:S(2)}, u32[]{:S(2)}) collective-permute-start(bf16[1,128,1024]{2,1,0:T(8,128)(2,1)S(1)} %get-tuple-element.81), channel_id=1, source_target_pairs={{0,28},{4,0},{8,4},{12,8},{16,12},{20,16},{24,20},{28,24},{1,29},{... | collective-permute-start | bytes 786440 | tf_op jit(solution)/shard_map/ppermute | solution.py:453
  67.0 1.9 %inner.1 = (f32[512,1024]{1,0:T(8,128)S(1)}, f32[512,1024]{1,0:T(8,128)S(1)}) custom-call(bf16[8,512,512]{2,1,0:T(8,128)(2,1)S(1)} %get-tuple-element.76.z_ref, bf16[8,512,512]{2,1,0:T(8,128)(2,1)S(1)} %get-tuple-element.77.p_ref, bf16[512,1024]{1,0:T(8,128)(2,1)S(1)} %get-tuple-element.67.q_ref, bf16[512,1024]{1,0:T(8,128)(2,1)S(1)} %get-tuple-element.73.g_ref), custom_call_target="tpu_custom_call" | custom-call | flops 5500000256 | bytes 1000000 | tf_op jit(solution)/shard_map/inner/pallas_call | solution.py:68
  68.9 3.4 %collective-permute-done.11.far_ref = bf16[8,128,128]{2,1,0:T(8,128)(2,1)S(1)} collective-permute-done((bf16[8,128,128]{2,1,0:T(8,128)(2,1)S(1)}, bf16[8,128,128]{2,1,0:T(8,128)(2,1)S(1)}, u32[]{:S(2)}, u32[]{:S(2)}) %collective-permute-start.11) | collective-permute-done | bytes 262176 | tf_op jit(solution)/shard_map/ppermute | solution.py:453
  72.3 1.6 %grad_kv.1 = (bf16[512,1024]{1,0:T(8,128)(2,1)S(1)}, bf16[512,1024]{1,0:T(8,128)(2,1)S(1)}, bf16[2,128,1024]{2,1,0:T(8,128)(2,1)S(1)}) custom-call(s32[1,512]{1,0:T(1,128)S(1)} %bitcast.6, bf16[8,128,128]{2,1,0:T(8,128)(2,1)S(1)} %collective-permute-done.11.far_ref, bf16[8,128,128]{2,1,0:T(8,128)(2,1)S(1)} %collective-permute-done.12.near_ref._, ...), custom_call_target="tpu_custom_call" | custom-call | flops 3300000000 | bytes 1000000 | tf_op jit(solution)/shard_map/grad_kv/pallas_call | solution.py:68
  73.9 1.0 collective-permute-start.15
  75.4 1.1 %collective-permute-start.16 = (bf16[2,128,1024]{2,1,0:T(8,128)(2,1)S(1)}, bf16[2,128,1024]{2,1,0:T(8,128)(2,1)S(1)}, u32[]{:S(2)}, u32[]{:S(2)}) collective-permute-start(bf16[2,128,1024]{2,1,0:T(8,128)(2,1)S(1)} %right.1), channel_id=1, source_target_pairs={{0,4},{4,8},{8,12},{12,16},{16,20},{20,24},{24,28},{28,0},{1,5},{5... | collective-permute-start | bytes 1572872 | tf_op jit(solution)/shard_map/ppermute | solution.py:453
  76.5 1.3 %normed.1 = bf16[512,1024]{1,0:T(8,128)(2,1)} custom-call(f32[512,1024]{1,0:T(8,128)S(1)} %get-tuple-element.68.u_ref, f32[512,128]{1,0:T(8,128)S(1)} %get-tuple-element.71.inverse_ref, bf16[512,1024]{1,0:T(8,128)(2,1)S(1)} %get-tuple-element.80._.refs_1_.refs_0_), custom_call_target="tpu_custom_call" | custom-call | flops 2200000000 | bytes 1000000 | tf_op jit(solution)/shard_map/normed/pallas_call | solution.py:68
  78.5 1.2 %collective-permute-done.13.right_ref = bf16[1,128,1024]{2,1,0:T(8,128)(2,1)S(1)} collective-permute-done((bf16[1,128,1024]{2,1,0:T(8,128)(2,1)S(1)}, bf16[1,128,1024]{2,1,0:T(8,128)(2,1)S(1)}, u32[]{:S(2)}, u32[]{:S(2)}) %collective-permute-start.13) | collective-permute-done | bytes 262176 | tf_op jit(solution)/shard_map/ppermute | solution.py:453
  79.8 10.8 %collective-permute-done.14.left_ref = bf16[1,128,1024]{2,1,0:T(8,128)(2,1)S(1)} collective-permute-done((bf16[1,128,1024]{2,1,0:T(8,128)(2,1)S(1)}, bf16[1,128,1024]{2,1,0:T(8,128)(2,1)S(1)}, u32[]{:S(2)}, u32[]{:S(2)}) %collective-permute-start.14) | collective-permute-done | bytes 262176 | tf_op jit(solution)/shard_map/ppermute | solution.py:453
  90.6 1.4 %finish_q.1 = (bf16[512,1024]{1,0:T(8,128)(2,1)}, bf16[16,128]{1,0:T(8,128)(2,1)S(1)}) custom-call(s32[2,128]{1,0:T(2,128)S(1)} %bitcast.11, bf16[1,128,1024]{2,1,0:T(8,128)(2,1)S(1)} %collective-permute-done.13.right_ref, bf16[1,128,1024]{2,1,0:T(8,128)(2,1)S(1)} %collective-permute-done.14.left_ref, bf16[512,1024]{1,0:T(8,128)(2,1)S(1)} %own_q.1.refs_0_), custom_call_target="tpu_custom_call" | custom-call | flops 2200000000 | bytes 1000000 | tf_op jit(solution)/shard_map/finish_q/pallas_call | solution.py:68
  92.0 1.3 %own_kv.1 = (bf16[512,1024]{1,0:T(8,128)(2,1)S(1)}, bf16[512,1024]{1,0:T(8,128)(2,1)S(1)}) custom-call(s32[1,512]{1,0:T(1,128)S(1)} %bitcast.9, bf16[512,1024]{1,0:T(8,128)(2,1)S(1)} %get-tuple-element.80._.refs_1_.refs_0_, bf16[512,1024]{1,0:T(8,128)(2,1)S(1)} %get-tuple-element.88.refs_1_, bf16[16,128]{1,0:T(8,128)(2,1)S(1)} %get-tuple-element.89.refs_2_), custom_call_target="tpu_custom_call" | custom-call | flops 2200000000 | bytes 1000000 | tf_op jit(solution)/shard_map/own_kv/pallas_call | solution.py:68
  93.7 7.7 %collective-permute-done.15.right_ref = bf16[2,128,1024]{2,1,0:T(8,128)(2,1)S(1)} collective-permute-done((bf16[2,128,1024]{2,1,0:T(8,128)(2,1)S(1)}, bf16[2,128,1024]{2,1,0:T(8,128)(2,1)S(1)}, u32[]{:S(2)}, u32[]{:S(2)}) %collective-permute-start.15) | collective-permute-done | bytes 524320 | tf_op jit(solution)/shard_map/ppermute | solution.py:453
  101.3 1.8 %finish_kv.1 = (bf16[512,1024]{1,0:T(8,128)(2,1)}, bf16[512,1024]{1,0:T(8,128)(2,1)}) custom-call(s32[2,128]{1,0:T(2,128)S(1)} %bitcast.12, bf16[2,128,1024]{2,1,0:T(8,128)(2,1)S(1)} %collective-permute-done.15.right_ref, bf16[2,128,1024]{2,1,0:T(8,128)(2,1)S(1)} %collective-permute-done.16.left_ref, f32[128,1024]{1,0:T(8,128)S(1)} %get-tuple-element.86.refs_0_, ...), custom_call_target="tpu_custom_call" | custom-call | flops 2200000000 | bytes 1000000 | tf_op jit(solution)/shard_map/finish_kv/pallas_call | solution.py:68
  (45 shorter events, 6.8 us)
Async XLA Ops:
  0.6 6.1 %copy-start = (bf16[512,1024]{1,0:T(8,128)(2,1)S(1)}, bf16[512,1024]{1,0:T(8,128)(2,1)}, u32[]{:S(2)}) copy-start(bf16[512,1024]{1,0:T(8,128)(2,1)} %k_ref.1) | copy-start | bytes 3145732
  0.6 6.1 %copy-start.1 = (bf16[512,1024]{1,0:T(8,128)(2,1)S(1)}, bf16[512,1024]{1,0:T(8,128)(2,1)}, u32[]{:S(2)}) copy-start(bf16[512,1024]{1,0:T(8,128)(2,1)} %v_ref.1) | copy-start | bytes 3145732
  0.7 6.1 %copy-start.2 = (bf16[512,1024]{1,0:T(8,128)(2,1)S(1)}, bf16[512,1024]{1,0:T(8,128)(2,1)}, u32[]{:S(2)}) copy-start(bf16[512,1024]{1,0:T(8,128)(2,1)} %q_ref.1) | copy-start | bytes 3145732
  0.7 6.1 %copy-start.8 = (f32[512,8]{0,1:T(8,128)S(1)}, f32[512,8]{0,1:T(8,128)}, u32[]{:S(2)}) copy-start(f32[512,8]{0,1:T(8,128)} %param.12) | copy-start | bytes 49156
  0.7 6.1 %copy-start.9 = (s32[512]{0:T(512)S(1)}, s32[512]{0:T(512)}, u32[]{:S(2)}) copy-start(s32[512]{0:T(512)} %param.15) | copy-start | bytes 6148
  0.7 6.1 %copy-start.11 = (s32[8]{0:T(128)S(1)}, s32[8]{0:T(128)}, u32[]{:S(2)}) copy-start(s32[8]{0:T(128)} %docs_ref.1) | copy-start | bytes 100
  3.0 8.7 %copy-start.4 = (bf16[2,128,1024]{2,1,0:T(8,128)(2,1)}, bf16[2,128,1024]{2,1,0:T(8,128)(2,1)S(1)}, u32[]{:S(2)}) copy-start(bf16[2,128,1024]{2,1,0:T(8,128)(2,1)S(1)} %get-tuple-element.54.pair_ref) | copy-start | bytes 1572868
  3.0 8.7 %copy-start.6 = (bf16[2,128,1024]{2,1,0:T(8,128)(2,1)}, bf16[2,128,1024]{2,1,0:T(8,128)(2,1)S(1)}, u32[]{:S(2)}) copy-start(bf16[2,128,1024]{2,1,0:T(8,128)(2,1)S(1)} %get-tuple-element.55.other_ref) | copy-start | bytes 1572868
  3.0 26.8 %collective-permute-start.2 = (bf16[2,128,1024]{2,1,0:T(8,128)(2,1)S(1)}, bf16[2,128,1024]{2,1,0:T(8,128)(2,1)S(1)}, u32[]{:S(2)}, u32[]{:S(2)}) collective-permute-start(bf16[2,128,1024]{2,1,0:T(8,128)(2,1)S(1)} %get-tuple-element.54.pair_ref), channel_id=1, source_target_pairs={{0,4},{4,0},{8,12},{12,8},{16,20},{20,16},{24,28},{28,24},{1,5},{5... | collective-permute-start | bytes 1572872 | tf_op jit(solution)/shard_map/ppermute | solution.py:459
  6.1 24.4 %collective-permute-start.3 = (bf16[2,128,1024]{2,1,0:T(8,128)(2,1)S(1)}, bf16[2,128,1024]{2,1,0:T(8,128)(2,1)S(1)}, u32[]{:S(2)}, u32[]{:S(2)}) collective-permute-start(bf16[2,128,1024]{2,1,0:T(8,128)(2,1)S(1)} %get-tuple-element.55.other_ref), channel_id=1, source_target_pairs={{0,0},{4,8},{8,4},{12,16},{16,12},{20,24},{24,20},{28,28},{1,1},{5... | collective-permute-start | bytes 1572872 | tf_op jit(solution)/shard_map/ppermute | solution.py:459
  11.7 24.9 %collective-permute-start.5 = (f32[16,128]{1,0:T(8,128)S(1)}, f32[16,128]{1,0:T(8,128)S(1)}, u32[]{:S(2)}, u32[]{:S(2)}) collective-permute-start(f32[16,128]{1,0:T(8,128)S(1)} %get-tuple-element.60.facts_ref), channel_id=1, source_target_pairs={{0,28},{4,0},{8,4},{12,8},{16,12},{20,16},{24,20},{28,24},{1,29},{... | collective-permute-start | bytes 24584 | tf_op jit(solution)/shard_map/ppermute | solution.py:453
  15.3 23.0 %collective-permute-start.4 = (f32[16,128]{1,0:T(8,128)S(1)}, f32[16,128]{1,0:T(8,128)S(1)}, u32[]{:S(2)}, u32[]{:S(2)}) collective-permute-start(f32[16,128]{1,0:T(8,128)S(1)} %get-tuple-element.60.facts_ref), channel_id=1, source_target_pairs={{0,4},{4,8},{8,12},{12,16},{16,20},{20,24},{24,28},{28,0},{1,5},{5... | collective-permute-start | bytes 24584 | tf_op jit(solution)/shard_map/ppermute | solution.py:453
  16.1 25.1 %collective-permute-start = (bf16[1,128,1024]{2,1,0:T(8,128)(2,1)S(1)}, bf16[1,128,1024]{2,1,0:T(8,128)(2,1)S(1)}, u32[]{:S(2)}, u32[]{:S(2)}) collective-permute-start(bf16[1,128,1024]{2,1,0:T(8,128)(2,1)S(1)} %get-tuple-element.51), channel_id=1, source_target_pairs={{0,4},{4,0},{8,12},{12,8},{16,20},{20,16},{24,28},{28,24},{1,5},{5... | collective-permute-start | bytes 786440 | tf_op jit(solution)/shard_map/ppermute | solution.py:459
  29.8 11.4 %collective-permute-start.1 = (bf16[1,128,1024]{2,1,0:T(8,128)(2,1)S(1)}, bf16[1,128,1024]{2,1,0:T(8,128)(2,1)S(1)}, u32[]{:S(2)}, u32[]{:S(2)}) collective-permute-start(bf16[1,128,1024]{2,1,0:T(8,128)(2,1)S(1)} %get-tuple-element.52), channel_id=1, source_target_pairs={{0,0},{4,8},{8,4},{12,16},{16,12},{20,24},{24,20},{28,28},{1,1},{5... | collective-permute-start | bytes 786440 | tf_op jit(solution)/shard_map/ppermute | solution.py:459
  31.5 15.9 %collective-permute-start.7 = (bf16[8,128,128]{2,1,0:T(8,128)(2,1)S(1)}, bf16[8,128,128]{2,1,0:T(8,128)(2,1)S(1)}, u32[]{:S(2)}, u32[]{:S(2)}) collective-permute-start(bf16[8,128,128]{2,1,0:T(8,128)(2,1)S(1)} %state.1._), channel_id=1, source_target_pairs={{0,8},{4,12},{8,16},{12,20},{16,24},{20,28},{24,0},{28,4},{1,9},{5... | collective-permute-start | bytes 786440 | tf_op jit(solution)/shard_map/ppermute | solution.py:453
  36.7 12.6 %collective-permute-start.6 = (bf16[8,128,128]{2,1,0:T(8,128)(2,1)S(1)}, bf16[8,128,128]{2,1,0:T(8,128)(2,1)S(1)}, u32[]{:S(2)}, u32[]{:S(2)}) collective-permute-start(bf16[8,128,128]{2,1,0:T(8,128)(2,1)S(1)} %state.1._), channel_id=1, source_target_pairs={{0,4},{4,8},{8,12},{12,16},{16,20},{20,24},{24,28},{28,0},{1,5},{5... | collective-permute-start | bytes 786440 | tf_op jit(solution)/shard_map/ppermute | solution.py:453
  41.2 8.1 %copy-start.3 = (bf16[512,1024]{1,0:T(8,128)(2,1)S(1)}, bf16[512,1024]{1,0:T(8,128)(2,1)}, u32[]{:S(2)}) copy-start(bf16[512,1024]{1,0:T(8,128)(2,1)} %ct_ref.3) | copy-start | bytes 3145732
  41.2 8.1 %copy-start.12 = (f32[8]{0:T(128)S(1)}, f32[8]{0:T(128)}, u32[]{:S(2)}) copy-start(f32[8]{0:T(128)} %scale_ref.3) | copy-start | bytes 100
  51.0 3.1 %collective-permute-start.10 = (f32[2,512]{1,0:T(2,128)S(1)}, f32[2,512]{1,0:T(2,128)S(1)}, u32[]{:S(2)}, u32[]{:S(2)}) collective-permute-start(f32[2,512]{1,0:T(2,128)S(1)} %get-tuple-element.70.refs_0_), channel_id=1, source_target_pairs={{0,3},{1,2},{2,1},{3,0},{4,7},{5,6},{6,5},{7,4},{8,11},{9,10},{10,... | collective-permute-start | bytes 12296 | tf_op jit(solution)/shard_map/ppermute | solution.py:552
  51.1 3.7 %collective-permute-start.9 = (f32[2,512]{1,0:T(2,128)S(1)}, f32[2,512]{1,0:T(2,128)S(1)}, u32[]{:S(2)}, u32[]{:S(2)}) collective-permute-start(f32[2,512]{1,0:T(2,128)S(1)} %get-tuple-element.70.refs_0_), channel_id=1, source_target_pairs={{0,2},{1,3},{2,0},{3,1},{4,6},{5,7},{6,4},{7,5},{8,10},{9,11},{10,... | collective-permute-start | bytes 12296 | tf_op jit(solution)/shard_map/ppermute | solution.py:552
  52.6 2.1 %collective-permute-start.8 = (f32[2,512]{1,0:T(2,128)S(1)}, f32[2,512]{1,0:T(2,128)S(1)}, u32[]{:S(2)}, u32[]{:S(2)}) collective-permute-start(f32[2,512]{1,0:T(2,128)S(1)} %get-tuple-element.70.refs_0_), channel_id=1, source_target_pairs={{0,1},{1,0},{2,3},{3,2},{4,5},{5,4},{6,7},{7,6},{8,9},{9,8},{10,11... | collective-permute-start | bytes 12296 | tf_op jit(solution)/shard_map/ppermute | solution.py:552
  56.4 12.5 %collective-permute-start.12 = (bf16[8,128,128]{2,1,0:T(8,128)(2,1)S(1)}, bf16[8,128,128]{2,1,0:T(8,128)(2,1)S(1)}, u32[]{:S(2)}, u32[]{:S(2)}) collective-permute-start(bf16[8,128,128]{2,1,0:T(8,128)(2,1)S(1)} %get-tuple-element.72.message_ref), channel_id=1, source_target_pairs={{0,28},{4,0},{8,4},{12,8},{16,12},{20,16},{24,20},{28,24},{1,29},{... | collective-permute-start | bytes 786440 | tf_op jit(solution)/shard_map/ppermute | solution.py:453
  58.8 13.5 %collective-permute-start.11 = (bf16[8,128,128]{2,1,0:T(8,128)(2,1)S(1)}, bf16[8,128,128]{2,1,0:T(8,128)(2,1)S(1)}, u32[]{:S(2)}, u32[]{:S(2)}) collective-permute-start(bf16[8,128,128]{2,1,0:T(8,128)(2,1)S(1)} %get-tuple-element.72.message_ref), channel_id=1, source_target_pairs={{0,24},{4,28},{8,0},{12,4},{16,8},{20,12},{24,16},{28,20},{1,25},{... | collective-permute-start | bytes 786440 | tf_op jit(solution)/shard_map/ppermute | solution.py:453
  64.9 14.8 %collective-permute-start.13 = (bf16[1,128,1024]{2,1,0:T(8,128)(2,1)S(1)}, bf16[1,128,1024]{2,1,0:T(8,128)(2,1)S(1)}, u32[]{:S(2)}, u32[]{:S(2)}) collective-permute-start(bf16[1,128,1024]{2,1,0:T(8,128)(2,1)S(1)} %get-tuple-element.81), channel_id=1, source_target_pairs={{0,28},{4,0},{8,4},{12,8},{16,12},{20,16},{24,20},{28,24},{1,29},{... | collective-permute-start | bytes 786440 | tf_op jit(solution)/shard_map/ppermute | solution.py:453
  66.6 23.9 %collective-permute-start.14 = (bf16[1,128,1024]{2,1,0:T(8,128)(2,1)S(1)}, bf16[1,128,1024]{2,1,0:T(8,128)(2,1)S(1)}, u32[]{:S(2)}, u32[]{:S(2)}) collective-permute-start(bf16[1,128,1024]{2,1,0:T(8,128)(2,1)S(1)} %get-tuple-element.82), channel_id=1, source_target_pairs={{0,4},{4,8},{8,12},{12,16},{16,20},{20,24},{24,28},{28,0},{1,5},{5... | collective-permute-start | bytes 786440 | tf_op jit(solution)/shard_map/ppermute | solution.py:453
  73.9 27.4 %collective-permute-start.15 = (bf16[2,128,1024]{2,1,0:T(8,128)(2,1)S(1)}, bf16[2,128,1024]{2,1,0:T(8,128)(2,1)S(1)}, u32[]{:S(2)}, u32[]{:S(2)}) collective-permute-start(bf16[2,128,1024]{2,1,0:T(8,128)(2,1)S(1)} %get-tuple-element.85), channel_id=1, source_target_pairs={{0,28},{4,0},{8,4},{12,8},{16,12},{20,16},{24,20},{28,24},{1,29},{... | collective-permute-start | bytes 1572872 | tf_op jit(solution)/shard_map/ppermute | solution.py:453
  75.4 25.9 %collective-permute-start.16 = (bf16[2,128,1024]{2,1,0:T(8,128)(2,1)S(1)}, bf16[2,128,1024]{2,1,0:T(8,128)(2,1)S(1)}, u32[]{:S(2)}, u32[]{:S(2)}) collective-permute-start(bf16[2,128,1024]{2,1,0:T(8,128)(2,1)S(1)} %right.1), channel_id=1, source_target_pairs={{0,4},{4,8},{8,12},{12,16},{16,20},{20,24},{24,28},{28,0},{1,5},{5... | collective-permute-start | bytes 1572872 | tf_op jit(solution)/shard_map/ppermute | solution.py:453
  77.8 12.7 %copy-start.10 = (s32[1,2,128]{2,1,0:T(2,128)S(1)}, s32[1,2,128]{2,1,0:T(2,128)}, u32[]{:S(2)}) copy-start(s32[1,2,128]{2,1,0:T(2,128)} %param.14) | copy-start | bytes 3076
  92.0 1.3 %copy-start.5 = (bf16[2,128,1024]{2,1,0:T(8,128)(2,1)S(1)}, bf16[2,128,1024]{2,1,0:T(8,128)(2,1)}, u32[]{:S(2)}) copy-start(bf16[2,128,1024]{2,1,0:T(8,128)(2,1)} %copy-done.4) | copy-start | bytes 1572868
  92.0 1.3 %copy-start.7 = (bf16[2,128,1024]{2,1,0:T(8,128)(2,1)S(1)}, bf16[2,128,1024]{2,1,0:T(8,128)(2,1)}, u32[]{:S(2)}) copy-start(bf16[2,128,1024]{2,1,0:T(8,128)(2,1)} %copy-done.6) | copy-start | bytes 1572868

commit v4 on v3

--- a/solution.py
+++ b/solution.py
@@ -293,7 +293,7 @@
     return carried_sum(before, facts_ref, near_ref, far_ref, h).astype(BF)
 
 
-def output_kernel(scale_ref, o_ref, q_ref, facts_ref, near_ref, far_ref, cols_ref, ct_ref, u_ref, h_ref, sums_ref):
+def output_kernel(scale_ref, o_ref, q_ref, far_ref, near_ref, facts_ref, cols_ref, ct_ref, u_ref, h_ref, sums_ref):
     rows, features = q_ref.shape
     heads, width = h_ref.shape[:2]
     before = shards_before(1)
@@ -544,7 +544,7 @@
         "output",
         3,
         [full32, sds((heads, width, width)), sds((2, rows), F32)],
-        (head_scale, o_inside, q, facts_before, near, far, cols, cotangent),
+        (head_scale, o_inside, q, far, near, facts_before, cols, cotangent),
         scalars=1,
     )
     peers = lax.axis_size("head")

time: 103 us -> 103 us (level)
  waiting for transfers between devices: 42.7 us -> 40.4 us
  starting transfers between devices: 30.1 us -> 32.2 us
    ppermute x10, waiting for transfers between devices: 27.8 us -> 25.6 us  [shifted(): lax.ppermute(array, 'seq', [(i, (i + by) % peers) for i in range(peers)])]
    ppermute x10, starting transfers between devices: 20.9 us -> 23.1 us  [shifted(): lax.ppermute(array, 'seq', [(i, (i + by) % peers) for i in range(peers)])]
  transfers between devices with their start and end apart: 17 -> 17, of which waited for: 10 -> 9; matrix products, arithmetic and copies ran while one was open for 0% -> 0% of each run, Pallas kernels for 21% -> 21%
where the time goes in v4:
time: 103 us
  waiting for transfers between devices  40.4 us (39%)
  starting transfers between devices  32.2 us (31%)
  Pallas kernels  29.4 us (29%)
    pallas_call x17, Pallas kernels, local(): pl.pallas_call(kernel, in_specs=specs, out_specs=[vmem] * len(out_shape),...  29.4 us
    ppermute x10, waiting for transfers between devices, shifted(): lax.ppermute(array, 'seq', [(i, (i + by) % peers) for i in range(peers)])  25.6 us
    ppermute x10, starting transfers between devices, shifted(): lax.ppermute(array, 'seq', [(i, (i + by) % peers) for i in range(peers)])  23.1 us
    ppermute x4, waiting for transfers between devices, swapped(): lax.ppermute(array, 'seq', [(i, j if 0 <= j < peers else i) for i, j in e...  13 us
    ppermute x4, starting transfers between devices, swapped(): lax.ppermute(array, 'seq', [(i, j if 0 <= j < peers else i) for i, j in e...  7.24 us
  transfers between devices with their start and end apart: 17, of which 9 were waited for; matrix products, arithmetic and copies ran while one was open for 0% of the time, Pallas kernels for 21%

profile of v4, /device:TPU:0, one launch (start us, length us, event | category | flops | bytes accessed | tf_op | source)
XLA Modules:
  0.0 103.1 jit_solution(10748759715019772130)
XLA Ops:
  0.7 2.3 %pick.1 = (bf16[2,128,1024]{2,1,0:T(8,128)(2,1)S(1)}, bf16[2,128,1024]{2,1,0:T(8,128)(2,1)S(1)}, bf16[256,512]{1,0:T(8,128)(2,1)S(1)}) custom-call(s32[2,128]{1,0:T(2,128)} %bitcast.10, bf16[512,1024]{1,0:T(8,128)(2,1)} %k_ref.1, bf16[512,1024]{1,0:T(8,128)(2,1)} %v_ref.1), custom_call_target="tpu_custom_call" | custom-call | flops 2200000000 | bytes 1000000 | tf_op jit(solution)/shard_map/pick/pallas_call | solution.py:68
  3.0 3.0 %collective-permute-start.2 = (bf16[2,128,1024]{2,1,0:T(8,128)(2,1)S(1)}, bf16[2,128,1024]{2,1,0:T(8,128)(2,1)S(1)}, u32[]{:S(2)}, u32[]{:S(2)}) collective-permute-start(bf16[2,128,1024]{2,1,0:T(8,128)(2,1)S(1)} %get-tuple-element.54.pair_ref), channel_id=1, source_target_pairs={{0,4},{4,0},{8,12},{12,8},{16,20},{20,16},{24,28},{28,24},{1,5},{5... | collective-permute-start | bytes 1572872 | tf_op jit(solution)/shard_map/ppermute | solution.py:459
  6.8 4.9 %prep.1 = (bf16[1,128,1024]{2,1,0:T(8,128)(2,1)S(1)}, bf16[1,128,1024]{2,1,0:T(8,128)(2,1)S(1)}, bf16[512,1024]{1,0:T(8,128)(2,1)S(1)}, bf16[512,1024]{1,0:T(8,1...) custom-call(s32[8]{0:T(128)S(1)} %copy-done.11, ...), custom_call_target="tpu_custom_call" | custom-call | flops 32999999488 | bytes 1000000 | tf_op jit(solution)/shard_map/prep/pallas_call | solution.py:68
  11.7 3.6 %collective-permute-start.5 = (f32[16,128]{1,0:T(8,128)S(1)}, f32[16,128]{1,0:T(8,128)S(1)}, u32[]{:S(2)}, u32[]{:S(2)}) collective-permute-start(f32[16,128]{1,0:T(8,128)S(1)} %get-tuple-element.60.facts_ref), channel_id=1, source_target_pairs={{0,28},{4,0},{8,4},{12,8},{16,12},{20,16},{24,20},{28,24},{1,29},{... | collective-permute-start | bytes 24584 | tf_op jit(solution)/shard_map/ppermute | solution.py:453
  15.3 0.8 collective-permute-start.4
  16.1 2.9 %collective-permute-start = (bf16[1,128,1024]{2,1,0:T(8,128)(2,1)S(1)}, bf16[1,128,1024]{2,1,0:T(8,128)(2,1)S(1)}, u32[]{:S(2)}, u32[]{:S(2)}) collective-permute-start(bf16[1,128,1024]{2,1,0:T(8,128)(2,1)S(1)} %get-tuple-element.51), channel_id=1, source_target_pairs={{0,4},{4,0},{8,12},{12,8},{16,20},{20,16},{24,28},{28,24},{1,5},{5... | collective-permute-start | bytes 786440 | tf_op jit(solution)/shard_map/ppermute | solution.py:459
  19.0 10.8 %collective-permute-done.2.left_ref = bf16[2,128,1024]{2,1,0:T(8,128)(2,1)S(1)} collective-permute-done((bf16[2,128,1024]{2,1,0:T(8,128)(2,1)S(1)}, bf16[2,128,1024]{2,1,0:T(8,128)(2,1)S(1)}, u32[]{:S(2)}, u32[]{:S(2)}) %collective-permute-start.2) | collective-permute-done | bytes 524320 | tf_op jit(solution)/shard_map/ppermute | solution.py:459
  30.5 0.9 state.1._
  31.5 5.3 %collective-permute-start.7 = (bf16[8,128,128]{2,1,0:T(8,128)(2,1)S(1)}, bf16[8,128,128]{2,1,0:T(8,128)(2,1)S(1)}, u32[]{:S(2)}, u32[]{:S(2)}) collective-permute-start(bf16[8,128,128]{2,1,0:T(8,128)(2,1)S(1)} %state.1._), channel_id=1, source_target_pairs={{0,4},{4,8},{8,12},{12,16},{16,20},{20,24},{24,28},{28,0},{1,5},{5... | collective-permute-start | bytes 786440 | tf_op jit(solution)/shard_map/ppermute | solution.py:453
  36.7 1.6 %collective-permute-start.6 = (bf16[8,128,128]{2,1,0:T(8,128)(2,1)S(1)}, bf16[8,128,128]{2,1,0:T(8,128)(2,1)S(1)}, u32[]{:S(2)}, u32[]{:S(2)}) collective-permute-start(bf16[8,128,128]{2,1,0:T(8,128)(2,1)S(1)} %state.1._), channel_id=1, source_target_pairs={{0,8},{4,12},{8,16},{12,20},{16,24},{20,28},{24,0},{28,4},{1,9},{5... | collective-permute-start | bytes 786440 | tf_op jit(solution)/shard_map/ppermute | solution.py:453
  38.3 0.7 assemble.1
  39.0 2.2 %collective-permute-done.left_ref = bf16[1,128,1024]{2,1,0:T(8,128)(2,1)S(1)} collective-permute-done((bf16[1,128,1024]{2,1,0:T(8,128)(2,1)S(1)}, bf16[1,128,1024]{2,1,0:T(8,128)(2,1)S(1)}, u32[]{:S(2)}, u32[]{:S(2)}) %collective-permute-start) | collective-permute-done | bytes 262176 | tf_op jit(solution)/shard_map/ppermute | solution.py:459
  41.2 3.3 %inside.1 = (bf16[512,1024]{1,0:T(8,128)(2,1)S(1)}, bf16[8,128,512]{2,1,0:T(8,128)(2,1)S(1)}, f32[8,512,512]{2,1,0:T(8,128)S(1)}, bf16[8,512,512]{2,1,0:T(8,128)(2,1)S(1)}, f32[512,1024]{1,0:T(8,128)S(1)}) custom-call(bf16[512,256]{1,0:T(8,128)(2,1)S(1)} %get-tuple-element.50.hot_ref, bf16[1,128,1024]{2,1,0:T(8,128)(2,1)S(1)} %collective-permute-done.left_ref, ...), custom_call_target="tpu_custom_call" | custom-call | flops 32999999488 | bytes 1000000 | tf_op jit(solution)/shard_map/inside/pallas_call | solution.py:68
  44.6 1.1 %collective-permute-done.7.near_ref = bf16[8,128,128]{2,1,0:T(8,128)(2,1)S(1)} collective-permute-done((bf16[8,128,128]{2,1,0:T(8,128)(2,1)S(1)}, bf16[8,128,128]{2,1,0:T(8,128)(2,1)S(1)}, u32[]{:S(2)}, u32[]{:S(2)}) %collective-permute-start.7) | collective-permute-done | bytes 262176 | tf_op jit(solution)/shard_map/ppermute | solution.py:453
  45.7 1.6 %collective-permute-done.6.far_ref = bf16[8,128,128]{2,1,0:T(8,128)(2,1)S(1)} collective-permute-done((bf16[8,128,128]{2,1,0:T(8,128)(2,1)S(1)}, bf16[8,128,128]{2,1,0:T(8,128)(2,1)S(1)}, u32[]{:S(2)}, u32[]{:S(2)}) %collective-permute-start.6) | collective-permute-done | bytes 262176 | tf_op jit(solution)/shard_map/ppermute | solution.py:453
  47.3 1.7 %output.1 = (f32[512,1024]{1,0:T(8,128)S(1)}, bf16[8,128,128]{2,1,0:T(8,128)(2,1)S(1)}, f32[2,512]{1,0:T(2,128)S(1)}) custom-call(f32[8]{0:T(128)S(1)} %copy-done.12, f32[512,1024]{1,0:T(8,128)S(1)} %get-tuple-element.66.o_ref, bf16[512,1024]{1,0:T(8,128)(2,1)S(1)} %get-tuple-element.67.q_ref, bf16[8,128,128]{2,1,0:T(8,128)(2,1)S(1)} %collective-permute-done.6.far_ref, ...), custom_call_target="tpu_custom_call" | custom-call | flops 3300000000 | bytes 1000000 | tf_op jit(solution)/shard_map/output/pallas_call | solution.py:68
  49.1 1.6 %collective-permute-start.9 = (f32[2,512]{1,0:T(2,128)S(1)}, f32[2,512]{1,0:T(2,128)S(1)}, u32[]{:S(2)}, u32[]{:S(2)}) collective-permute-start(f32[2,512]{1,0:T(2,128)S(1)} %get-tuple-element.70.refs_0_), channel_id=1, source_target_pairs={{0,2},{1,3},{2,0},{3,1},{4,6},{5,7},{6,4},{7,5},{8,10},{9,11},{10,... | collective-permute-start | bytes 12296 | tf_op jit(solution)/shard_map/ppermute | solution.py:552
  51.0 1.2 %collective-permute-done.10.refs_3_ = f32[2,512]{1,0:T(2,128)S(1)} collective-permute-done((f32[2,512]{1,0:T(2,128)S(1)}, f32[2,512]{1,0:T(2,128)S(1)}, u32[]{:S(2)}, u32[]{:S(2)}) %collective-permute-start.10) | collective-permute-done | bytes 4128 | tf_op jit(solution)/shard_map/ppermute | solution.py:552
  52.8 1.6 %norm.1 = (bf16[512,1024]{1,0:T(8,128)(2,1)S(1)}, bf16[8,128,128]{2,1,0:T(8,128)(2,1)S(1)}, f32[512,128]{1,0:T(8,128)S(1)}) custom-call(f32[8]{0:T(128)S(1)} %copy-done.12, f32[512,1024]{1,0:T(8,128)S(1)} %get-tuple-element.68.u_ref, bf16[512,1024]{1,0:T(8,128)(2,1)S(1)} %copy-done.3, bf16[8,128,512]{2,1,0:T(8,128)(2,1)S(1)} %get-tuple-element.69.qe_ref, ...), custom_call_target="tpu_custom_call" | custom-call | flops 4400000000 | bytes 1000000 | tf_op jit(solution)/shard_map/norm/pallas_call | solution.py:68
  54.4 7.2 %collective-permute-start.12 = (bf16[8,128,128]{2,1,0:T(8,128)(2,1)S(1)}, bf16[8,128,128]{2,1,0:T(8,128)(2,1)S(1)}, u32[]{:S(2)}, u32[]{:S(2)}) collective-permute-start(bf16[8,128,128]{2,1,0:T(8,128)(2,1)S(1)} %get-tuple-element.72.message_ref), channel_id=1, source_target_pairs={{0,28},{4,0},{8,4},{12,8},{16,12},{20,16},{24,20},{28,24},{1,29},{... | collective-permute-start | bytes 786440 | tf_op jit(solution)/shard_map/ppermute | solution.py:453
  62.0 3.1 %grad_q.1 = (bf16[512,1024]{1,0:T(8,128)(2,1)S(1)}, bf16[8,512,512]{2,1,0:T(8,128)(2,1)S(1)}, bf16[1,128,1024]{2,1,0:T(8,128)(2,1)S(1)}, bf16[1,128,1024]{2,1,0:T(8,128)(2,1)S(1)}) custom-call(s32[1,512]{1,0:T(1,128)S(1)} %bitcast.5, bf16[512,1024]{1,0:T(8,128)(2,1)S(1)} %get-tuple-element.73.g_ref, bf16[512,1024]{1,0:T(8,128)(2,1)S(1)} %get-tuple-element.61.k_ref, ...), custom_call_target="tpu_custom_call" | custom-call | flops 32999999488 | bytes 1000000 | tf_op jit(solution)/shard_map/grad_q/pallas_call | solution.py:68
  65.4 1.8 %collective-permute-start.14 = (bf16[1,128,1024]{2,1,0:T(8,128)(2,1)S(1)}, bf16[1,128,1024]{2,1,0:T(8,128)(2,1)S(1)}, u32[]{:S(2)}, u32[]{:S(2)}) collective-permute-start(bf16[1,128,1024]{2,1,0:T(8,128)(2,1)S(1)} %get-tuple-element.82), channel_id=1, source_target_pairs={{0,4},{4,8},{8,12},{12,16},{16,20},{20,24},{24,28},{28,0},{1,5},{5... | collective-permute-start | bytes 786440 | tf_op jit(solution)/shard_map/ppermute | solution.py:453
  67.2 1.9 %inner.1 = (f32[512,1024]{1,0:T(8,128)S(1)}, f32[512,1024]{1,0:T(8,128)S(1)}) custom-call(bf16[8,512,512]{2,1,0:T(8,128)(2,1)S(1)} %get-tuple-element.76.z_ref, bf16[8,512,512]{2,1,0:T(8,128)(2,1)S(1)} %get-tuple-element.77.p_ref, bf16[512,1024]{1,0:T(8,128)(2,1)S(1)} %get-tuple-element.67.q_ref, bf16[512,1024]{1,0:T(8,128)(2,1)S(1)} %get-tuple-element.73.g_ref), custom_call_target="tpu_custom_call" | custom-call | flops 5500000256 | bytes 1000000 | tf_op jit(solution)/shard_map/inner/pallas_call | solution.py:68
  69.1 4.7 %collective-permute-done.11.far_ref = bf16[8,128,128]{2,1,0:T(8,128)(2,1)S(1)} collective-permute-done((bf16[8,128,128]{2,1,0:T(8,128)(2,1)S(1)}, bf16[8,128,128]{2,1,0:T(8,128)(2,1)S(1)}, u32[]{:S(2)}, u32[]{:S(2)}) %collective-permute-start.11) | collective-permute-done | bytes 262176 | tf_op jit(solution)/shard_map/ppermute | solution.py:453
  73.9 1.6 %grad_kv.1 = (bf16[512,1024]{1,0:T(8,128)(2,1)S(1)}, bf16[512,1024]{1,0:T(8,128)(2,1)S(1)}, bf16[2,128,1024]{2,1,0:T(8,128)(2,1)S(1)}) custom-call(s32[1,512]{1,0:T(1,128)S(1)} %bitcast.6, bf16[8,128,128]{2,1,0:T(8,128)(2,1)S(1)} %collective-permute-done.11.far_ref, bf16[8,128,128]{2,1,0:T(8,128)(2,1)S(1)} %collective-permute-done.12.near_ref._, ...), custom_call_target="tpu_custom_call" | custom-call | flops 3300000000 | bytes 1000000 | tf_op jit(solution)/shard_map/grad_kv/pallas_call | solution.py:68
  76.0 2.1 %collective-permute-start.16 = (bf16[2,128,1024]{2,1,0:T(8,128)(2,1)S(1)}, bf16[2,128,1024]{2,1,0:T(8,128)(2,1)S(1)}, u32[]{:S(2)}, u32[]{:S(2)}) collective-permute-start(bf16[2,128,1024]{2,1,0:T(8,128)(2,1)S(1)} %right.1), channel_id=1, source_target_pairs={{0,4},{4,8},{8,12},{12,16},{16,20},{20,24},{24,28},{28,0},{1,5},{5... | collective-permute-start | bytes 1572872 | tf_op jit(solution)/shard_map/ppermute | solution.py:453
  78.0 1.3 %normed.1 = bf16[512,1024]{1,0:T(8,128)(2,1)} custom-call(f32[512,1024]{1,0:T(8,128)S(1)} %get-tuple-element.68.u_ref, f32[512,128]{1,0:T(8,128)S(1)} %get-tuple-element.71.inverse_ref, bf16[512,1024]{1,0:T(8,128)(2,1)S(1)} %get-tuple-element.80._.refs_1_.refs_0_), custom_call_target="tpu_custom_call" | custom-call | flops 2200000000 | bytes 1000000 | tf_op jit(solution)/shard_map/normed/pallas_call | solution.py:68
  80.1 10.7 %collective-permute-done.14.left_ref = bf16[1,128,1024]{2,1,0:T(8,128)(2,1)S(1)} collective-permute-done((bf16[1,128,1024]{2,1,0:T(8,128)(2,1)S(1)}, bf16[1,128,1024]{2,1,0:T(8,128)(2,1)S(1)}, u32[]{:S(2)}, u32[]{:S(2)}) %collective-permute-start.14) | collective-permute-done | bytes 262176 | tf_op jit(solution)/shard_map/ppermute | solution.py:453
  90.8 1.4 %finish_q.1 = (bf16[512,1024]{1,0:T(8,128)(2,1)}, bf16[16,128]{1,0:T(8,128)(2,1)S(1)}) custom-call(s32[2,128]{1,0:T(2,128)S(1)} %bitcast.11, bf16[1,128,1024]{2,1,0:T(8,128)(2,1)S(1)} %collective-permute-done.13.right_ref, bf16[1,128,1024]{2,1,0:T(8,128)(2,1)S(1)} %collective-permute-done.14.left_ref, bf16[512,1024]{1,0:T(8,128)(2,1)S(1)} %own_q.1.refs_0_), custom_call_target="tpu_custom_call" | custom-call | flops 2200000000 | bytes 1000000 | tf_op jit(solution)/shard_map/finish_q/pallas_call | solution.py:68
  92.2 1.2 %own_kv.1 = (bf16[512,1024]{1,0:T(8,128)(2,1)S(1)}, bf16[512,1024]{1,0:T(8,128)(2,1)S(1)}) custom-call(s32[1,512]{1,0:T(1,128)S(1)} %bitcast.9, bf16[512,1024]{1,0:T(8,128)(2,1)S(1)} %get-tuple-element.80._.refs_1_.refs_0_, bf16[512,1024]{1,0:T(8,128)(2,1)S(1)} %get-tuple-element.88.refs_1_, bf16[16,128]{1,0:T(8,128)(2,1)S(1)} %get-tuple-element.89.refs_2_), custom_call_target="tpu_custom_call" | custom-call | flops 2200000000 | bytes 1000000 | tf_op jit(solution)/shard_map/own_kv/pallas_call | solution.py:68
  93.9 7.3 %collective-permute-done.15.right_ref = bf16[2,128,1024]{2,1,0:T(8,128)(2,1)S(1)} collective-permute-done((bf16[2,128,1024]{2,1,0:T(8,128)(2,1)S(1)}, bf16[2,128,1024]{2,1,0:T(8,128)(2,1)S(1)}, u32[]{:S(2)}, u32[]{:S(2)}) %collective-permute-start.15) | collective-permute-done | bytes 524320 | tf_op jit(solution)/shard_map/ppermute | solution.py:453
  101.3 1.8 %finish_kv.1 = (bf16[512,1024]{1,0:T(8,128)(2,1)}, bf16[512,1024]{1,0:T(8,128)(2,1)}) custom-call(s32[2,128]{1,0:T(2,128)S(1)} %bitcast.12, bf16[2,128,1024]{2,1,0:T(8,128)(2,1)S(1)} %collective-permute-done.15.right_ref, bf16[2,128,1024]{2,1,0:T(8,128)(2,1)S(1)} %collective-permute-done.16.left_ref, f32[128,1024]{1,0:T(8,128)S(1)} %get-tuple-element.86.refs_0_, ...), custom_call_target="tpu_custom_call" | custom-call | flops 2200000000 | bytes 1000000 | tf_op jit(solution)/shard_map/finish_kv/pallas_call | solution.py:68
  (45 shorter events, 4.8 us)
Async XLA Ops:
  0.6 6.1 %copy-start = (bf16[512,1024]{1,0:T(8,128)(2,1)S(1)}, bf16[512,1024]{1,0:T(8,128)(2,1)}, u32[]{:S(2)}) copy-start(bf16[512,1024]{1,0:T(8,128)(2,1)} %k_ref.1) | copy-start | bytes 3145732
  0.6 6.1 %copy-start.1 = (bf16[512,1024]{1,0:T(8,128)(2,1)S(1)}, bf16[512,1024]{1,0:T(8,128)(2,1)}, u32[]{:S(2)}) copy-start(bf16[512,1024]{1,0:T(8,128)(2,1)} %v_ref.1) | copy-start | bytes 3145732
  0.7 6.1 %copy-start.2 = (bf16[512,1024]{1,0:T(8,128)(2,1)S(1)}, bf16[512,1024]{1,0:T(8,128)(2,1)}, u32[]{:S(2)}) copy-start(bf16[512,1024]{1,0:T(8,128)(2,1)} %q_ref.1) | copy-start | bytes 3145732
  0.7 6.1 %copy-start.8 = (f32[512,8]{0,1:T(8,128)S(1)}, f32[512,8]{0,1:T(8,128)}, u32[]{:S(2)}) copy-start(f32[512,8]{0,1:T(8,128)} %param.12) | copy-start | bytes 49156
  0.7 6.1 %copy-start.9 = (s32[512]{0:T(512)S(1)}, s32[512]{0:T(512)}, u32[]{:S(2)}) copy-start(s32[512]{0:T(512)} %param.15) | copy-start | bytes 6148
  0.7 6.1 %copy-start.11 = (s32[8]{0:T(128)S(1)}, s32[8]{0:T(128)}, u32[]{:S(2)}) copy-start(s32[8]{0:T(128)} %docs_ref.1) | copy-start | bytes 100
  3.0 8.7 %copy-start.4 = (bf16[2,128,1024]{2,1,0:T(8,128)(2,1)}, bf16[2,128,1024]{2,1,0:T(8,128)(2,1)S(1)}, u32[]{:S(2)}) copy-start(bf16[2,128,1024]{2,1,0:T(8,128)(2,1)S(1)} %get-tuple-element.54.pair_ref) | copy-start | bytes 1572868
  3.0 8.7 %copy-start.6 = (bf16[2,128,1024]{2,1,0:T(8,128)(2,1)}, bf16[2,128,1024]{2,1,0:T(8,128)(2,1)S(1)}, u32[]{:S(2)}) copy-start(bf16[2,128,1024]{2,1,0:T(8,128)(2,1)S(1)} %get-tuple-element.55.other_ref) | copy-start | bytes 1572868
  3.0 26.8 %collective-permute-start.2 = (bf16[2,128,1024]{2,1,0:T(8,128)(2,1)S(1)}, bf16[2,128,1024]{2,1,0:T(8,128)(2,1)S(1)}, u32[]{:S(2)}, u32[]{:S(2)}) collective-permute-start(bf16[2,128,1024]{2,1,0:T(8,128)(2,1)S(1)} %get-tuple-element.54.pair_ref), channel_id=1, source_target_pairs={{0,4},{4,0},{8,12},{12,8},{16,20},{20,16},{24,28},{28,24},{1,5},{5... | collective-permute-start | bytes 1572872 | tf_op jit(solution)/shard_map/ppermute | solution.py:459
  6.1 24.4 %collective-permute-start.3 = (bf16[2,128,1024]{2,1,0:T(8,128)(2,1)S(1)}, bf16[2,128,1024]{2,1,0:T(8,128)(2,1)S(1)}, u32[]{:S(2)}, u32[]{:S(2)}) collective-permute-start(bf16[2,128,1024]{2,1,0:T(8,128)(2,1)S(1)} %get-tuple-element.55.other_ref), channel_id=1, source_target_pairs={{0,0},{4,8},{8,4},{12,16},{16,12},{20,24},{24,20},{28,28},{1,1},{5... | collective-permute-start | bytes 1572872 | tf_op jit(solution)/shard_map/ppermute | solution.py:459
  11.7 25.0 %collective-permute-start.5 = (f32[16,128]{1,0:T(8,128)S(1)}, f32[16,128]{1,0:T(8,128)S(1)}, u32[]{:S(2)}, u32[]{:S(2)}) collective-permute-start(f32[16,128]{1,0:T(8,128)S(1)} %get-tuple-element.60.facts_ref), channel_id=1, source_target_pairs={{0,28},{4,0},{8,4},{12,8},{16,12},{20,16},{24,20},{28,24},{1,29},{... | collective-permute-start | bytes 24584 | tf_op jit(solution)/shard_map/ppermute | solution.py:453
  15.3 23.0 %collective-permute-start.4 = (f32[16,128]{1,0:T(8,128)S(1)}, f32[16,128]{1,0:T(8,128)S(1)}, u32[]{:S(2)}, u32[]{:S(2)}) collective-permute-start(f32[16,128]{1,0:T(8,128)S(1)} %get-tuple-element.60.facts_ref), channel_id=1, source_target_pairs={{0,4},{4,8},{8,12},{12,16},{16,20},{20,24},{24,28},{28,0},{1,5},{5... | collective-permute-start | bytes 24584 | tf_op jit(solution)/shard_map/ppermute | solution.py:453
  16.1 25.1 %collective-permute-start = (bf16[1,128,1024]{2,1,0:T(8,128)(2,1)S(1)}, bf16[1,128,1024]{2,1,0:T(8,128)(2,1)S(1)}, u32[]{:S(2)}, u32[]{:S(2)}) collective-permute-start(bf16[1,128,1024]{2,1,0:T(8,128)(2,1)S(1)} %get-tuple-element.51), channel_id=1, source_target_pairs={{0,4},{4,0},{8,12},{12,8},{16,20},{20,16},{24,28},{28,24},{1,5},{5... | collective-permute-start | bytes 786440 | tf_op jit(solution)/shard_map/ppermute | solution.py:459
  29.8 11.4 %collective-permute-start.1 = (bf16[1,128,1024]{2,1,0:T(8,128)(2,1)S(1)}, bf16[1,128,1024]{2,1,0:T(8,128)(2,1)S(1)}, u32[]{:S(2)}, u32[]{:S(2)}) collective-permute-start(bf16[1,128,1024]{2,1,0:T(8,128)(2,1)S(1)} %get-tuple-element.52), channel_id=1, source_target_pairs={{0,0},{4,8},{8,4},{12,16},{16,12},{20,24},{24,20},{28,28},{1,1},{5... | collective-permute-start | bytes 786440 | tf_op jit(solution)/shard_map/ppermute | solution.py:459
  31.5 14.3 %collective-permute-start.7 = (bf16[8,128,128]{2,1,0:T(8,128)(2,1)S(1)}, bf16[8,128,128]{2,1,0:T(8,128)(2,1)S(1)}, u32[]{:S(2)}, u32[]{:S(2)}) collective-permute-start(bf16[8,128,128]{2,1,0:T(8,128)(2,1)S(1)} %state.1._), channel_id=1, source_target_pairs={{0,4},{4,8},{8,12},{12,16},{16,20},{20,24},{24,28},{28,0},{1,5},{5... | collective-permute-start | bytes 786440 | tf_op jit(solution)/shard_map/ppermute | solution.py:453
  36.7 10.6 %collective-permute-start.6 = (bf16[8,128,128]{2,1,0:T(8,128)(2,1)S(1)}, bf16[8,128,128]{2,1,0:T(8,128)(2,1)S(1)}, u32[]{:S(2)}, u32[]{:S(2)}) collective-permute-start(bf16[8,128,128]{2,1,0:T(8,128)(2,1)S(1)} %state.1._), channel_id=1, source_target_pairs={{0,8},{4,12},{8,16},{12,20},{16,24},{20,28},{24,0},{28,4},{1,9},{5... | collective-permute-start | bytes 786440 | tf_op jit(solution)/shard_map/ppermute | solution.py:453
  41.2 6.1 %copy-start.3 = (bf16[512,1024]{1,0:T(8,128)(2,1)S(1)}, bf16[512,1024]{1,0:T(8,128)(2,1)}, u32[]{:S(2)}) copy-start(bf16[512,1024]{1,0:T(8,128)(2,1)} %ct_ref.3) | copy-start | bytes 3145732
  41.2 6.1 %copy-start.12 = (f32[8]{0:T(128)S(1)}, f32[8]{0:T(128)}, u32[]{:S(2)}) copy-start(f32[8]{0:T(128)} %scale_ref.3) | copy-start | bytes 100
  49.0 3.1 %collective-permute-start.10 = (f32[2,512]{1,0:T(2,128)S(1)}, f32[2,512]{1,0:T(2,128)S(1)}, u32[]{:S(2)}, u32[]{:S(2)}) collective-permute-start(f32[2,512]{1,0:T(2,128)S(1)} %get-tuple-element.70.refs_0_), channel_id=1, source_target_pairs={{0,3},{1,2},{2,1},{3,0},{4,7},{5,6},{6,5},{7,4},{8,11},{9,10},{10,... | collective-permute-start | bytes 12296 | tf_op jit(solution)/shard_map/ppermute | solution.py:552
  49.1 3.7 %collective-permute-start.9 = (f32[2,512]{1,0:T(2,128)S(1)}, f32[2,512]{1,0:T(2,128)S(1)}, u32[]{:S(2)}, u32[]{:S(2)}) collective-permute-start(f32[2,512]{1,0:T(2,128)S(1)} %get-tuple-element.70.refs_0_), channel_id=1, source_target_pairs={{0,2},{1,3},{2,0},{3,1},{4,6},{5,7},{6,4},{7,5},{8,10},{9,11},{10,... | collective-permute-start | bytes 12296 | tf_op jit(solution)/shard_map/ppermute | solution.py:552
  50.7 2.1 %collective-permute-start.8 = (f32[2,512]{1,0:T(2,128)S(1)}, f32[2,512]{1,0:T(2,128)S(1)}, u32[]{:S(2)}, u32[]{:S(2)}) collective-permute-start(f32[2,512]{1,0:T(2,128)S(1)} %get-tuple-element.70.refs_0_), channel_id=1, source_target_pairs={{0,1},{1,0},{2,3},{3,2},{4,5},{5,4},{6,7},{7,6},{8,9},{9,8},{10,11... | collective-permute-start | bytes 12296 | tf_op jit(solution)/shard_map/ppermute | solution.py:552
  54.4 14.7 %collective-permute-start.12 = (bf16[8,128,128]{2,1,0:T(8,128)(2,1)S(1)}, bf16[8,128,128]{2,1,0:T(8,128)(2,1)S(1)}, u32[]{:S(2)}, u32[]{:S(2)}) collective-permute-start(bf16[8,128,128]{2,1,0:T(8,128)(2,1)S(1)} %get-tuple-element.72.message_ref), channel_id=1, source_target_pairs={{0,28},{4,0},{8,4},{12,8},{16,12},{20,16},{24,20},{28,24},{1,29},{... | collective-permute-start | bytes 786440 | tf_op jit(solution)/shard_map/ppermute | solution.py:453
  61.6 12.3 %collective-permute-start.11 = (bf16[8,128,128]{2,1,0:T(8,128)(2,1)S(1)}, bf16[8,128,128]{2,1,0:T(8,128)(2,1)S(1)}, u32[]{:S(2)}, u32[]{:S(2)}) collective-permute-start(bf16[8,128,128]{2,1,0:T(8,128)(2,1)S(1)} %get-tuple-element.72.message_ref), channel_id=1, source_target_pairs={{0,24},{4,28},{8,0},{12,4},{16,8},{20,12},{24,16},{28,20},{1,25},{... | collective-permute-start | bytes 786440 | tf_op jit(solution)/shard_map/ppermute | solution.py:453
  65.1 15.0 %collective-permute-start.13 = (bf16[1,128,1024]{2,1,0:T(8,128)(2,1)S(1)}, bf16[1,128,1024]{2,1,0:T(8,128)(2,1)S(1)}, u32[]{:S(2)}, u32[]{:S(2)}) collective-permute-start(bf16[1,128,1024]{2,1,0:T(8,128)(2,1)S(1)} %get-tuple-element.81), channel_id=1, source_target_pairs={{0,28},{4,0},{8,4},{12,8},{16,12},{20,16},{24,20},{28,24},{1,29},{... | collective-permute-start | bytes 786440 | tf_op jit(solution)/shard_map/ppermute | solution.py:453
  65.4 25.4 %collective-permute-start.14 = (bf16[1,128,1024]{2,1,0:T(8,128)(2,1)S(1)}, bf16[1,128,1024]{2,1,0:T(8,128)(2,1)S(1)}, u32[]{:S(2)}, u32[]{:S(2)}) collective-permute-start(bf16[1,128,1024]{2,1,0:T(8,128)(2,1)S(1)} %get-tuple-element.82), channel_id=1, source_target_pairs={{0,4},{4,8},{8,12},{12,16},{16,20},{20,24},{24,28},{28,0},{1,5},{5... | collective-permute-start | bytes 786440 | tf_op jit(solution)/shard_map/ppermute | solution.py:453
  75.4 25.8 %collective-permute-start.15 = (bf16[2,128,1024]{2,1,0:T(8,128)(2,1)S(1)}, bf16[2,128,1024]{2,1,0:T(8,128)(2,1)S(1)}, u32[]{:S(2)}, u32[]{:S(2)}) collective-permute-start(bf16[2,128,1024]{2,1,0:T(8,128)(2,1)S(1)} %get-tuple-element.85), channel_id=1, source_target_pairs={{0,28},{4,0},{8,4},{12,8},{16,12},{20,16},{24,20},{28,24},{1,29},{... | collective-permute-start | bytes 1572872 | tf_op jit(solution)/shard_map/ppermute | solution.py:453
  76.0 25.3 %collective-permute-start.16 = (bf16[2,128,1024]{2,1,0:T(8,128)(2,1)S(1)}, bf16[2,128,1024]{2,1,0:T(8,128)(2,1)S(1)}, u32[]{:S(2)}, u32[]{:S(2)}) collective-permute-start(bf16[2,128,1024]{2,1,0:T(8,128)(2,1)S(1)} %right.1), channel_id=1, source_target_pairs={{0,4},{4,8},{8,12},{12,16},{16,20},{20,24},{24,28},{28,0},{1,5},{5... | collective-permute-start | bytes 1572872 | tf_op jit(solution)/shard_map/ppermute | solution.py:453
  79.4 11.4 %copy-start.10 = (s32[1,2,128]{2,1,0:T(2,128)S(1)}, s32[1,2,128]{2,1,0:T(2,128)}, u32[]{:S(2)}) copy-start(s32[1,2,128]{2,1,0:T(2,128)} %param.14) | copy-start | bytes 3076
  92.2 1.3 %copy-start.5 = (bf16[2,128,1024]{2,1,0:T(8,128)(2,1)S(1)}, bf16[2,128,1024]{2,1,0:T(8,128)(2,1)}, u32[]{:S(2)}) copy-start(bf16[2,128,1024]{2,1,0:T(8,128)(2,1)} %copy-done.4) | copy-start | bytes 1572868
  92.2 1.3 %copy-start.7 = (bf16[2,128,1024]{2,1,0:T(8,128)(2,1)S(1)}, bf16[2,128,1024]{2,1,0:T(8,128)(2,1)}, u32[]{:S(2)}) copy-start(bf16[2,128,1024]{2,1,0:T(8,128)(2,1)} %copy-done.6) | copy-start | bytes 1572868
